TPU v7x, 512 devices: a whole 4x8x8 slice. The times are simulated.
512 devices in a mesh: mx: 16 (over y, core), my: 32 (over x, z).
Axes of the slice: x: 4, y: 8, z: 8, core: 2. Of those that a mesh axis runs over, the one named last changes fastest.
Arguments:
- patches: bfloat16 [256, 6144], P('my', 'mx'), may hold values from -6 to 6
- cotangent: bfloat16 [256, 6144], P('my', 'mx'), may hold values from -0.75 to 0.75
- w_qkv: bfloat16 [6144, 3, 4096], P('mx', None, 'my'), may hold values from -0.078125 to 0.078125
- w_out: bfloat16 [4096, 6144], P('my', 'mx'), may hold values from -0.09375 to 0.09375
- w_up: bfloat16 [6144, 24576], P('mx', 'my'), may hold values from -0.078125 to 0.078125
- w_down: bfloat16 [24576, 6144], P('my', 'mx'), may hold values from -0.0390625 to 0.0390625
- dir_qkv: bfloat16 [6144, 3, 4096], P('mx', None, 'my'), may hold values from -0.078125 to 0.078125
- dir_out: bfloat16 [4096, 6144], P('my', 'mx'), may hold values from -0.09375 to 0.09375
- dir_up: bfloat16 [6144, 24576], P('mx', 'my'), may hold values from -0.078125 to 0.078125
- dir_down: bfloat16 [24576, 6144], P('my', 'mx'), may hold values from -0.0390625 to 0.0390625
Outputs:
- hvp_qkv: bfloat16 [6144, 3, 4096], P('mx', None, 'my')
- hvp_out: bfloat16 [4096, 6144], P('my', 'mx')
- hvp_up: bfloat16 [6144, 24576], P('mx', 'my')
- hvp_down: bfloat16 [24576, 6144], P('my', 'mx')
All inputs are finite; a program needn't handle non-finite values.
Results may differ from a plain program's by a relative error of at most 0.0049.
Values may be sent and summed in bfloat16 or wider, within the bound.
No kernel may reach another device: no remote copies, remote signals or barrier semaphores. Data moves between devices by JAX's collectives and lax.ppermute only.
A program may use at most 64 MiB of HBM per device.

v0:
```python
import math

import jax
import jax.numpy as jnp
from jax import lax
from jax.sharding import PartitionSpec as P

HD = 128


def normalize(block):
    centered = block - jnp.mean(block, axis=-1, keepdims=True)
    return centered / jnp.sqrt(jnp.mean(centered * centered, axis=-1, keepdims=True) + 1e-06)


def attend(pre):
    count = pre.shape[0]
    heads = pre.shape[2] // HD
    parts = pre.reshape(count, 3, heads, HD)
    query = normalize(parts[:, 0])
    keys = normalize(parts[:, 1])
    values = parts[:, 2]
    scores = jnp.einsum("phd,khd->hpk", query, keys, precision=lax.Precision.HIGHEST) / math.sqrt(
        HD
    )
    raised = jnp.exp(scores)
    probs = raised / jnp.sum(raised, axis=2, keepdims=True)
    mixed = jnp.einsum("hpk,khd->phd", probs, values, precision=lax.Precision.HIGHEST)
    return mixed.reshape(count, heads * HD)


def attention_pair(pre, cot_in):
    result, pull = jax.vjp(attend, pre)
    return (result, pull(cot_in)[0])


def hidden_pair(pre, cot_in):
    result, pull = jax.vjp(jax.nn.gelu, pre)
    return (result, pull(cot_in)[0])


def project(left, right):
    return jnp.dot(left, right, preferred_element_type=jnp.float32)


def project_back(left, right):
    return jnp.einsum("pd,ed->pe", left, right, preferred_element_type=jnp.float32)


def body(patches, cotangent, w_qkv, w_out, w_up, w_down, dir_qkv, dir_out, dir_up, dir_down):
    rows_all, cot_all = (
        lax.all_gather(patches, "my", axis=0, tiled=True),
        lax.all_gather(cotangent, "my", axis=0, tiled=True),
    )
    width = w_qkv.shape[0]
    span = w_qkv.shape[2]
    count = rows_all.shape[0]
    flat_weight = w_qkv.reshape(width, 3 * span)
    flat_direction = dir_qkv.reshape(width, 3 * span)
    pre_qkv, tan_qkv, pre_hidden, tan_hidden = lax.psum(
        (
            project(rows_all, flat_weight),
            project(rows_all, flat_direction),
            project(rows_all, w_up),
            project(rows_all, dir_up),
        ),
        "mx",
    )
    cot_mixed, tan_mixed, cot_act, tan_act = lax.psum(
        (
            project_back(cot_all, w_out),
            project_back(cot_all, dir_out),
            project_back(cot_all, w_down),
            project_back(cot_all, dir_down),
        ),
        "mx",
    )
    hid_tan = jax.jvp(hidden_pair, (pre_hidden, cot_act), (tan_hidden, tan_act))[1]
    act_low = hid_tan[0].astype(jnp.bfloat16)
    hid_low = hid_tan[1].astype(jnp.bfloat16)
    attn_tan = jax.jvp(
        attention_pair,
        (pre_qkv.reshape(count, 3, span), cot_mixed),
        (tan_qkv.reshape(count, 3, span), tan_mixed),
    )[1]
    mixed_low = attn_tan[0].astype(jnp.bfloat16)
    pre_low = attn_tan[1].reshape(count, 3 * span).astype(jnp.bfloat16)
    hvp_qkv = jnp.einsum("pd,pe->de", rows_all, pre_low, preferred_element_type=jnp.float32)
    hvp_out = jnp.einsum("pe,pd->ed", mixed_low, cot_all, preferred_element_type=jnp.float32)
    hvp_up = jnp.einsum("pd,pe->de", rows_all, hid_low, preferred_element_type=jnp.float32)
    hvp_down = jnp.einsum("pe,pd->ed", act_low, cot_all, preferred_element_type=jnp.float32)
    return (
        hvp_qkv.reshape(width, 3, span).astype(jnp.bfloat16),
        hvp_out.astype(jnp.bfloat16),
        hvp_up.astype(jnp.bfloat16),
        hvp_down.astype(jnp.bfloat16),
    )


def solution(mesh):
    return jax.shard_map(
        body,
        mesh=mesh,
        in_specs=(
            P("my", "mx"),
            P("my", "mx"),
            P("mx", None, "my"),
            P("my", "mx"),
            P("mx", "my"),
            P("my", "mx"),
            P("mx", None, "my"),
            P("my", "mx"),
            P("mx", "my"),
            P("my", "mx"),
        ),
        out_specs=(P("mx", None, "my"), P("my", "mx"), P("mx", "my"), P("my", "mx")),
        check_vma=False,
    )
```

profile of v0, /device:TPU:1, one launch (start us, length us, event | category | flops | bytes accessed | tf_op | source)
XLA Modules:
  0.0 268.9 jit_solution(17628010586359470245)
XLA Ops:
  7.2 0.0 copy-start
  7.2 0.0 all-reduce.6.cloned.1.call-start
  7.2 42.5 %all_gather.7 = bf16[256,384]{1,0:T(8,128)(2,1)S(1)} all-gather(bf16[8,384]{1,0:T(8,128)(2,1)} %param.10), channel_id=1, replica_groups=mesh['mx'=16,'my'=32] {'my'}, dimensions={0}, use_global_device_ids=true | all-gather | bytes 202752 | tf_op jit(solution)/shard_map/all_gather | solution.py:52
  49.7 34.4 %all_gather.6 = bf16[256,384]{1,0:T(8,128)(2,1)S(1)} all-gather(bf16[8,384]{1,0:T(8,128)(2,1)} %param.11), channel_id=1, replica_groups=mesh['mx'=16,'my'=32] {'my'}, dimensions={0}, use_global_device_ids=true | all-gather | bytes 202752 | tf_op jit(solution)/shard_map/all_gather | solution.py:53
  84.1 1.8 convolution_bitcast_fusion
  85.9 0.9 convolution_bitcast_fusion.1
  86.8 0.2 copy.18
  87.0 0.2 copy.21
  87.2 1.0 fusion.68
  88.3 1.0 fusion.69
  89.3 0.0 copy-done
  89.3 1.3 fusion.72
  90.6 1.3 fusion.70
  91.9 0.0 copy-done.4
  91.9 1.3 fusion.73
  93.2 1.3 fusion.71
  94.5 0.0 all-reduce.6.cloned.1.call-update
  94.5 147.3 %all-reduce.6.cloned.1.call-done = (f32[256,3,1,128]{0,3,2,1:T(8,128)}, f32[256,3,1,128]{0,3,2,1:T(8,128)}, f32[128,256]{0,1:T(8,128)}, f32[128,256]{0,1:T(8,128...) async-done(((f32[256,3,1,128]{0,3,2,1:T(8,128)}, f32[256,3,1,128]{0,3,2,1:T(8,128)}, f32[128,256]{0,1:T(8,128)}, ...) | async-done | bytes 4194320 | tf_op jit(solution)/shard_map/psum | solution.py:60
  241.8 1.2 slice_reduce_fusion
  243.1 1.4 fusion.37
  244.5 0.0 copy-done.1
  244.5 0.0 copy-done.2
  244.5 0.0 copy-start.9
  244.5 0.1 fusion.16
  244.6 0.6 fusion.44
  245.2 0.6 fusion.41
  245.9 0.4 fusion.67
  246.3 0.0 copy-start.33
  246.3 0.0 copy-done.9
  246.3 1.1 fusion.38
  247.4 0.9 fusion.35
  248.3 0.4 fusion.18
  248.8 0.0 copy-start.6
  248.8 0.0 copy-done.17
  248.8 0.0 copy-done.19
  248.8 0.5 fusion.66
  249.3 0.0 copy-start.31
  249.3 0.4 copy-done.6
  249.7 0.4 convolution_add_fusion
  250.1 0.5 add_reduce_fusion
  250.6 0.0 copy-done.33
  250.6 0.0 copy-done.31
  250.6 0.0 copy-done.35
  250.6 0.0 copy-start.40
  250.6 0.1 add_multiply_fusion
  250.8 0.3 fusion.25
  251.1 0.4 fusion.31
  251.5 0.3 copy-done.40
  251.8 0.3 copy-done.39
  252.0 1.6 convolution_convert_fusion
  253.7 1.4 fusion
  255.1 1.1 copy.24
  256.1 1.4 fusion.4
  257.6 0.3 fusion.6
  257.9 0.8 convolution_convert_fusion.3
  258.8 0.3 fusion.23
  259.1 0.4 convolution_add_fusion.4
  259.5 0.3 convolution_add_fusion.3
  259.9 0.5 add_reduce_fusion.2
  260.4 0.1 copy-done.28
  260.6 0.1 fusion.63
  260.7 0.1 fusion.64
  260.9 0.3 convolution_convert_fusion.2
  261.1 0.9 copy.23
  (82 shorter events, 0.3 us)
Async XLA Ops:
  7.2 82.2 %copy-start = (bf16[768,384]{1,0:T(8,128)(2,1)S(1)}, bf16[768,384]{1,0:T(8,128)(2,1)}, u32[]{:S(2)}) copy-start(bf16[768,384]{1,0:T(8,128)(2,1)} %param.15) | copy-start | bytes 1769476
  7.2 78.7 %copy-start.10 = (bf16[128,384]{1,0:T(8,128)(2,1)S(1)}, bf16[128,384]{1,0:T(8,128)(2,1)}, u32[]{:S(2)}) copy-start(bf16[128,384]{1,0:T(8,128)(2,1)} %param.17) | copy-start | bytes 294916
  7.2 79.6 %copy-start.7 = (bf16[384,3,128]{2,0,1:T(8,128)(2,1)S(1)}, bf16[384,3,128]{2,0,1:T(8,128)(2,1)}, u32[]{:S(2)}) copy-start(bf16[384,3,128]{2,0,1:T(8,128)(2,1)} %param.12) | copy-start | bytes 884740
  7.2 234.6 %all-reduce.6.cloned.1.call-start = ((), (), s32[]{:S(2)}) async-start(), calls=%async_computation | async-start | bytes 8388608 | tf_op jit(solution)/shard_map/psum | solution.py:60
  49.7 37.3 %copy-start.8 = (bf16[384,3,128]{2,0,1:T(8,128)(2,1)S(1)}, bf16[384,3,128]{2,0,1:T(8,128)(2,1)}, u32[]{:S(2)}) copy-start(bf16[384,3,128]{2,0,1:T(8,128)(2,1)} %param.16) | copy-start | bytes 884740
  89.3 1.3 copy-start.3
  90.6 1.3 copy-start.4
  91.9 1.3 copy-start.5
  241.8 2.7 copy-start.1
  241.8 2.7 copy-start.2
  244.5 1.8 copy-start.9
  244.6 0.6 copy-start.27
  244.6 0.6 copy-start.29
  244.6 2.8 %copy-start.23 = (f32[256]{0:T(256)}, f32[256]{0:T(256)S(1)}, u32[]{:S(2)}) copy-start(f32[256]{0:T(256)S(1)} %get-tuple-element.15) | copy-start | bytes 3076
  244.6 2.8 %copy-start.25 = (f32[256]{0:T(256)}, f32[256]{0:T(256)S(1)}, u32[]{:S(2)}) copy-start(f32[256]{0:T(256)S(1)} %get-tuple-element.20) | copy-start | bytes 3076
  245.2 3.6 %copy-start.17 = (f32[256]{0:T(256)}, f32[256]{0:T(256)S(1)}, u32[]{:S(2)}) copy-start(f32[256]{0:T(256)S(1)} %get-tuple-element.47) | copy-start | bytes 3076
  245.2 3.6 %copy-start.19 = (f32[256]{0:T(256)}, f32[256]{0:T(256)S(1)}, u32[]{:S(2)}) copy-start(f32[256]{0:T(256)S(1)} %get-tuple-element.50) | copy-start | bytes 3076
  245.2 5.6 %copy-start.21 = (f32[256]{0:T(256)}, f32[256]{0:T(256)S(1)}, u32[]{:S(2)}) copy-start(f32[256]{0:T(256)S(1)} %get-tuple-element.51) | copy-start | bytes 3076
  245.9 2.5 copy-start.11
  245.9 2.5 copy-start.13
  245.9 5.2 %copy-start.15 = (f32[256]{0:T(256)}, f32[256]{0:T(256)S(1)}, u32[]{:S(2)}) copy-start(f32[256]{0:T(256)S(1)} %get-tuple-element.49) | copy-start | bytes 3076
  246.3 4.3 %copy-start.33 = (f32[256]{0:T(256)}, f32[256]{0:T(256)S(1)}, u32[]{:S(2)}) copy-start(f32[256]{0:T(256)S(1)} %get-tuple-element.57) | copy-start | bytes 3076
  248.8 0.9 copy-start.6
  249.3 1.3 copy-start.31
  249.3 1.3 copy-start.35
  250.6 1.1 copy-start.40
  250.8 1.3 copy-start.39
  252.0 1.6 copy-start.41
  252.0 1.6 copy-start.42
  256.1 1.4 copy-start.32
  256.1 1.4 copy-start.34
  256.1 1.4 copy-start.36
  256.1 1.4 copy-start.43
  257.5 1.2 copy-start.22
  257.5 1.5 copy-start.12
  257.6 1.5 copy-start.14
  257.6 1.5 copy-start.16
  257.9 1.6 copy-start.18
  257.9 1.6 copy-start.20
  259.1 0.8 copy-start.37
  259.1 0.8 copy-start.38
  259.9 0.7 copy-start.28
  259.9 0.7 copy-start.30
  259.9 0.8 copy-start.24
  259.9 0.8 copy-start.26
Sparse Core Ops, SparseCore 0:
  94.6 147.1 all-reduce.5
where the time goes:
time: 270 us; the launch traced here: 269 us
  waiting for transfers between devices  147 us (54%)
  blocking collectives  76.9 us (28%)
  matrix products  23.4 us (9%)
  between operations  14.7 us (5%)
  local copies, waits for them, and re-layouts  3.6 us (1%)
  other arithmetic  2.93 us (1%)
    psum x1, waiting for transfers between devices, body(): lax.psum((project(rows_all, flat_weight), project(rows_all, flat_directio...  147 us
    all_gather x1, blocking collectives, body(): lax.all_gather(patches, 'my', axis=0, tiled=True)  42.5 us
    all_gather x1, blocking collectives, body(): lax.all_gather(cotangent, 'my', axis=0, tiled=True)  34.4 us
    dot_general x7, matrix products, attend(): jnp.einsum('hpk,khd->phd', probs, values, precision=lax.Precision.HIGHEST)  5.95 us
  transfers between devices with their start and end apart: 1, of which 1 were waited for; matrix products, arithmetic and copies ran while one was open for 0% of the time, Pallas kernels for 0%

commit v1 on v0

--- a/solution.py
+++ b/solution.py
@@ -47,42 +47,118 @@
     return jnp.einsum("pd,ed->pe", left, right, preferred_element_type=jnp.float32)
 
 
+def spread(exponents):
+    return jnp.repeat(exponents, HD, axis=-1)
+
+
+def pack(block, exponents):
+    rows = block.shape[0]
+    scaled = block * jnp.exp2(14.0 - spread(exponents))
+    tail = jnp.broadcast_to(jnp.pad(exponents, (0, HD - 8)), (rows, HD))
+    return jnp.concatenate([scaled, tail], axis=1).astype(jnp.float16)
+
+
+def unpack(message):
+    wide = message.astype(jnp.float32)
+    exponents = wide[..., 8 * HD : 8 * HD + 8]
+    return wide[..., : 8 * HD] * jnp.exp2(spread(exponents) - 14.0), exponents
+
+
 def body(patches, cotangent, w_qkv, w_out, w_up, w_down, dir_qkv, dir_out, dir_up, dir_down):
-    rows_all, cot_all = (
-        lax.all_gather(patches, "my", axis=0, tiled=True),
-        lax.all_gather(cotangent, "my", axis=0, tiled=True),
-    )
+    wide = lax.axis_size("mx")
+    long = lax.axis_size("my")
+    chips = wide // 2
+    core = lax.rem(lax.axis_index("mx"), 2)
+    ring = [[chip * 2 + c for chip in range(chips)] for c in range(2)]
+    swap = [(i, i ^ 1) for i in range(wide)]
     width = w_qkv.shape[0]
     span = w_qkv.shape[2]
-    count = rows_all.shape[0]
-    flat_weight = w_qkv.reshape(width, 3 * span)
-    flat_direction = dir_qkv.reshape(width, 3 * span)
-    pre_qkv, tan_qkv, pre_hidden, tan_hidden = lax.psum(
-        (
-            project(rows_all, flat_weight),
-            project(rows_all, flat_direction),
+    own_rows = patches.shape[0]
+    count = own_rows * long
+    half = count // 2
+    share = half // chips
+
+    both = jnp.stack([patches, cotangent])
+    gathered = lax.all_to_all(
+        jnp.broadcast_to(both, (long,) + both.shape), "my", 0, 0, tiled=True
+    )
+    rows_all = gathered[:, 0].reshape(count, width)
+    cot_all = gathered[:, 1].reshape(count, width)
+    own = lambda a: lax.dynamic_slice_in_dim(a, core * half, half, 0)
+    other = lambda a: lax.dynamic_slice_in_dim(a, (1 - core) * half, half, 0)
+    rows_all = jnp.concatenate([own(rows_all), other(rows_all)])
+    cot_all = jnp.concatenate([own(cot_all), other(cot_all)])
+
+    attn_part = jnp.concatenate(
+        [
+            project(rows_all, w_qkv.reshape(width, 3 * span)),
+            project(rows_all, dir_qkv.reshape(width, 3 * span)),
+            project_back(cot_all, w_out),
+            project_back(cot_all, dir_out),
+        ],
+        axis=1,
+    )
+    hid_part = jnp.concatenate(
+        [
             project(rows_all, w_up),
             project(rows_all, dir_up),
-        ),
-        "mx",
-    )
-    cot_mixed, tan_mixed, cot_act, tan_act = lax.psum(
-        (
-            project_back(cot_all, w_out),
-            project_back(cot_all, dir_out),
             project_back(cot_all, w_down),
             project_back(cot_all, dir_down),
-        ),
+        ],
+        axis=1,
+    )
+    attn_sum = attn_part[:half] + lax.ppermute(attn_part[half:], "mx", swap)
+    hid_sum = hid_part[:half] + lax.ppermute(hid_part[half:], "mx", swap)
+
+    top = jnp.max(jnp.abs(attn_sum).reshape(half, 8, HD), axis=(0, 2))
+    exponents = jnp.clip(jnp.ceil(jnp.log2(top)), -100.0, 100.0)
+    message = pack(attn_sum, exponents).reshape(chips, share, 9 * HD)
+    attn_parts, came = unpack(
+        lax.all_to_all(message, "mx", 0, 0, tiled=True, axis_index_groups=ring)
+    )
+    hid_parts = lax.all_to_all(
+        hid_sum.astype(jnp.bfloat16).reshape(chips, share, -1),
         "mx",
+        0,
+        0,
+        tiled=True,
+        axis_index_groups=ring,
     )
+    attn_rows = pack(jnp.sum(attn_parts, axis=0), jnp.max(came, axis=(0, 1)) + 3.0)
+    attn_half = lax.all_to_all(
+        jnp.broadcast_to(attn_rows, (chips,) + attn_rows.shape),
+        "mx",
+        0,
+        0,
+        tiled=True,
+        axis_index_groups=ring,
+    ).reshape(half, 9 * HD)
+    attn_all = unpack(
+        jnp.concatenate([attn_half, lax.ppermute(attn_half, "mx", swap)])
+    )[0]
+
+    hidden = jnp.sum(hid_parts.astype(jnp.float32), axis=0)
+    pre_hidden, tan_hidden, cot_act, tan_act = jnp.split(hidden, 4, axis=1)
     hid_tan = jax.jvp(hidden_pair, (pre_hidden, cot_act), (tan_hidden, tan_act))[1]
-    act_low = hid_tan[0].astype(jnp.bfloat16)
-    hid_low = hid_tan[1].astype(jnp.bfloat16)
-    attn_tan = jax.jvp(
-        attention_pair,
-        (pre_qkv.reshape(count, 3, span), cot_mixed),
-        (tan_qkv.reshape(count, 3, span), tan_mixed),
-    )[1]
+    lows = jnp.concatenate(
+        [hid_tan[0].astype(jnp.bfloat16), hid_tan[1].astype(jnp.bfloat16)], axis=1
+    )
+    low_half = lax.all_to_all(
+        jnp.broadcast_to(lows, (chips,) + lows.shape),
+        "mx",
+        0,
+        0,
+        tiled=True,
+        axis_index_groups=ring,
+    ).reshape(half, -1)
+    low_all = jnp.concatenate([low_half, lax.ppermute(low_half, "mx", swap)])
+    act_low, hid_low = jnp.split(low_all, 2, axis=1)
+
+    pre_qkv = attn_all[:, : 3 * HD].reshape(count, 3, span)
+    tan_qkv = attn_all[:, 3 * HD : 6 * HD].reshape(count, 3, span)
+    cot_mixed = attn_all[:, 6 * HD : 7 * HD]
+    tan_mixed = attn_all[:, 7 * HD : 8 * HD]
+    attn_tan = jax.jvp(attention_pair, (pre_qkv, cot_mixed), (tan_qkv, tan_mixed))[1]
     mixed_low = attn_tan[0].astype(jnp.bfloat16)
     pre_low = attn_tan[1].reshape(count, 3 * span).astype(jnp.bfloat16)
     hvp_qkv = jnp.einsum("pd,pe->de", rows_all, pre_low, preferred_element_type=jnp.float32)

time: 270 us -> 136 us (0.50)
  waiting for transfers between devices: 147 us -> 44.1 us
  blocking collectives: 76.9 us -> 13 us
  starting transfers between devices: 0.04 us -> 43.1 us
  between operations: 14.7 us -> 1.28 us
  other arithmetic: 2.93 us -> 9.31 us
  matrix products: 23.4 us -> 18.1 us
  local copies, waits for them, and re-layouts: 3.6 us -> 6.34 us
    psum x1 -> x0, waiting for transfers between devices: 147 us -> none  [body(): lax.psum((project(rows_all, flat_weight), project(rows_all, flat_directio...]
    all_gather x2 -> x0, blocking collectives: 76.9 us -> none  [the longest x1 42.5 us: body(): lax.all_gather(patches, 'my', axis=0, tiled=True)]
    all_to_all x0 -> x4, waiting for transfers between devices: none -> 43.8 us  [the longest x1 15.5 us: body(): lax.all_to_all(hid_sum.astype(jnp.bfloat16).reshape(chips, share, -1), 'm...]
    all_to_all x0 -> x4, starting transfers between devices: none -> 27.5 us  [the longest x1 13.7 us: body(): lax.all_to_all(jnp.broadcast_to(both, (long,) + both.shape), 'my', 0, 0,...]
    ppermute x0 -> x4, starting transfers between devices: none -> 15.6 us  [the longest x1 5.87 us: body(): attn_sum = attn_part[:half] + lax.ppermute(attn_part[half:], 'mx', swap)]
    all_to_all x0 -> x1, blocking collectives: none -> 13 us  [body(): lax.all_to_all(jnp.broadcast_to(attn_rows, (chips,) + attn_rows.shape), '...]
    convert_element_type x1 -> x4, other arithmetic: 0.02 us -> 4.14 us  [the longest x1 2.94 us: body(): hid_sum.astype(jnp.bfloat16).reshape(chips, share, -1)]
    dot_general x4, matrix products: 4.6 us -> 1.41 us  [project(): return jnp.dot(left, right, preferred_element_type=jnp.float32)]
  transfers between devices with their start and end apart: 1 -> 8, of which waited for: 1 -> 5; matrix products, arithmetic and copies ran while one was open for 0% -> 19% of each run, Pallas kernels for 0% -> 0%
where the time goes in v1:
time: 136 us; the launch traced here: 135 us
  waiting for transfers between devices  44.1 us (32%)
  starting transfers between devices  43.1 us (32%)
  matrix products  18.1 us (13%)
  blocking collectives  13 us (10%)
  other arithmetic  9.31 us (7%)
  local copies, waits for them, and re-layouts  6.34 us (5%)
    all_to_all x1, waiting for transfers between devices, body(): lax.all_to_all(hid_sum.astype(jnp.bfloat16).reshape(chips, share, -1), 'm...  15.5 us
    all_to_all x1, starting transfers between devices, body(): lax.all_to_all(jnp.broadcast_to(both, (long,) + both.shape), 'my', 0, 0,...  13.7 us
    all_to_all x1, blocking collectives, body(): lax.all_to_all(jnp.broadcast_to(attn_rows, (chips,) + attn_rows.shape), '...  13 us
    all_to_all x1, waiting for transfers between devices, body(): lax.all_to_all(jnp.broadcast_to(lows, (chips,) + lows.shape), 'mx', 0, 0,...  12.1 us
    all_to_all x1, waiting for transfers between devices, body(): lax.all_to_all(jnp.broadcast_to(both, (long,) + both.shape), 'my', 0, 0,...  10.2 us
    all_to_all x1, starting transfers between devices, body(): lax.all_to_all(message, 'mx', 0, 0, tiled=True, axis_index_groups=ring)  6.83 us
    all_to_all x1, waiting for transfers between devices, body(): lax.all_to_all(message, 'mx', 0, 0, tiled=True, axis_index_groups=ring)  5.98 us
    ppermute x1, starting transfers between devices, body(): attn_sum = attn_part[:half] + lax.ppermute(attn_part[half:], 'mx', swap)  5.87 us
  transfers between devices with their start and end apart: 8, of which 5 were waited for; matrix products, arithmetic and copies ran while one was open for 19% of the time, Pallas kernels for 0%

profile of v1, /device:TPU:1, one launch (start us, length us, event | category | flops | bytes accessed | tf_op | source)
XLA Modules:
  0.0 135.3 jit_solution(5983335626190694352)
XLA Ops:
  0.7 0.8 pad_maximum_fusion.9
  1.4 0.8 broadcast_in_dim.80
  2.2 13.7 %all-to-all-start = ((bf16[32,2,8,384]{3,2,1,0:T(8,128)(2,1)}), bf16[32,2,8,384]{3,2,1,0:T(8,128)(2,1)S(1)}, u32[]{:S(2)}, u32[]{:S(2)}) async-start(bf16[32,2,8,384]{3,2,1,0:T(8,128)(2,1)} %broadcast_in_dim.80), calls=%async_computation | async-start | bytes 786432 | tf_op jit(solution)/shard_map/all_to_all | solution.py:82
  16.0 1.2 copy.48
  17.1 0.2 copy.49
  17.4 10.2 %all-to-all-done = bf16[32,2,8,384]{3,2,1,0:T(8,128)(2,1)S(1)} async-done(((bf16[32,2,8,384]{3,2,1,0:T(8,128)(2,1)}), bf16[32,2,8,384]{3,2,1,0:T(8,128)(2,1)S(1)}, u32[]{:S(2)}, u32[]{:S(2)}) %all-to-all-start) | async-done | bytes 393248 | tf_op jit(solution)/shard_map/all_to_all | solution.py:82
  27.7 0.1 copy.62
  27.9 0.1 copy.63
  28.0 0.3 fusion.69
  28.3 0.3 fusion.68
  28.6 0.2 fusion.65
  28.9 0.2 fusion.64
  29.3 5.9 %collective-permute-start = (f32[128,1024]{1,0:T(8,128)S(1)}, f32[128,1024]{1,0:T(8,128)S(1)}, u32[]{:S(2)}, u32[]{:S(2)}) collective-permute-start(f32[128,1024]{1,0:T(8,128)S(1)} %slice.83), channel_id=1, source_target_pairs={{0,32},{32,0},{64,96},{96,64},{128,160},{160,128},{192,224},{224,1... | collective-permute-start | bytes 1572872 | tf_op jit(solution)/shard_map/ppermute | solution.py:110
  35.2 0.4 fusion.66
  35.6 0.4 fusion.67
  36.0 0.4 fusion.62
  36.4 0.3 collective-permute-done
  36.7 0.1 bitcast_reduce_fusion
  37.0 0.8 pad_maximum_fusion.4
  37.8 6.8 %all-to-all-start.1 = ((f16[8,16,1152]{2,1,0:T(8,128)(2,1)}), f16[8,16,1152]{2,1,0:T(8,128)(2,1)}, u32[]{:S(2)}, u32[]{:S(2)}) async-start(f16[8,16,1152]{2,1,0:T(8,128)(2,1)} %pad_maximum_fusion.4), calls=%async_computation.1 | async-start | bytes 589824 | tf_op jit(solution)/shard_map/all_to_all | solution.py:117
  44.7 1.4 %fusion.63 = f32[256,768]{1,0:T(8,128)S(1)} fusion(bf16[768,384]{1,0:T(8,128)(2,1)} %param.15, bf16[128,384]{1,0:T(8,128)(2,1)S(1)} %get-tuple-element.37, bf16[128,384]{1,0:T(8,128)(2,1)S(1)} %get-tuple-element.36), kind=kOutput, calls=%fused_computation.180 | convolution fusion | flops 151388160 | bytes 1572864 | tf_op jit(solution)/shard_map/pd,ed->pe/dot_general | solution.py:47
  46.1 0.4 pad_maximum_fusion
  46.5 1.4 %slice.98 = f32[128,3072]{1,0:T(8,128)} slice(f32[256,3072]{1,0:T(8,128)S(1)} %pad_maximum_fusion), slice={[128:256], [0:3072]} | slice | bytes 3145728 | tf_op jit(solution)/shard_map/slice | solution.py:111
  47.9 0.7 copy-done.1
  48.6 2.6 %collective-permute-start.2 = (f32[128,3072]{1,0:T(8,128)}, f32[128,3072]{1,0:T(8,128)}, u32[]{:S(2)}, u32[]{:S(2)}) collective-permute-start(f32[128,3072]{1,0:T(8,128)} %slice.98), channel_id=1, source_target_pairs={{0,32},{32,0},{64,96},{96,64},{128,160},{160,128},{192,224},{224,1... | collective-permute-start | bytes 4718600 | tf_op jit(solution)/shard_map/ppermute | solution.py:111
  51.2 6.0 %all-to-all-done.1 = f16[8,16,1152]{2,1,0:T(8,128)(2,1)} async-done(((f16[8,16,1152]{2,1,0:T(8,128)(2,1)}), f16[8,16,1152]{2,1,0:T(8,128)(2,1)}, u32[]{:S(2)}, u32[]{:S(2)}) %all-to-all-start.1) | async-done | bytes 294944 | tf_op jit(solution)/shard_map/all_to_all | solution.py:117
  57.2 1.0 convert_element_type.54
  58.2 0.2 broadcast_in_dim.83
  58.8 13.0 %all_to_all.25 = f16[8,16,1152]{2,1,0:T(8,128)(2,1)S(1)} all-to-all(f16[8,16,1152]{2,1,0:T(8,128)(2,1)S(1)} %broadcast_in_dim.86), channel_id=1, replica_groups={{0,64,128,192,256,320,384,448},{32,96,160,224,288,352,416,480},{1,65,12..., dimensions={0} | all-to-all | bytes 589824 | tf_op jit(solution)/shard_map/all_to_all | solution.py:128
  71.8 0.3 copy.54
  72.1 4.8 %collective-permute-start.1 = (f16[128,1152]{0,1:T(8,128)(2,1)S(1)}, f16[128,1152]{0,1:T(8,128)(2,1)S(1)}, u32[]{:S(2)}, u32[]{:S(2)}) collective-permute-start(f16[128,1152]{0,1:T(8,128)(2,1)S(1)} %copy.54), channel_id=1, source_target_pairs={{0,32},{32,0},{64,96},{96,64},{128,160},{160,128},{192,224},{224,1... | collective-permute-start | bytes 884744 | tf_op jit(solution)/shard_map/ppermute | solution.py:137
  76.9 2.9 %fusion = bf16[128,3072]{1,0:T(8,128)(2,1)} fusion(f32[128,3072]{1,0:T(8,128)} %collective-permute-done.2, f32[256,3072]{1,0:T(8,128)} %copy-done.1), kind=kLoop, calls=%fused_computation.2 | loop fusion | flops 786432 | bytes 3932160 | tf_op jit(solution)/shard_map/convert_element_type | solution.py:120
  79.8 3.5 %all-to-all-start.3 = ((bf16[8,16,3072]{2,1,0:T(8,128)(2,1)}), bf16[8,16,3072]{2,1,0:T(8,128)(2,1)S(1)}, u32[]{:S(2)}, u32[]{:S(2)}) async-start(bf16[8,16,3072]{2,1,0:T(8,128)(2,1)} %bitcast.54), calls=%async_computation.3 | async-start | bytes 1572864 | tf_op jit(solution)/shard_map/all_to_all | solution.py:119
  83.4 0.1 maximum_convert_fusion
  83.8 0.4 fusion.37
  84.3 0.5 fusion.75
  84.8 0.4 fusion.20
  85.2 0.5 fusion.74
  85.7 0.4 convolution_add_fusion
  86.1 0.5 add_reduce_fusion
  86.6 0.1 add_multiply_fusion
  86.8 0.3 fusion.27
  87.1 0.4 fusion.33
  87.5 0.3 fusion.25
  87.8 0.3 convolution_add_fusion.3
  88.1 0.4 convolution_add_fusion.4
  88.5 0.5 add_reduce_fusion.2
  89.1 0.7 fusion.71
  89.9 0.6 add_bitcast_fusion.1
  90.5 0.9 fusion.39
  91.5 15.5 %all-to-all-done.3 = bf16[8,16,3072]{2,1,0:T(8,128)(2,1)S(1)} async-done(((bf16[8,16,3072]{2,1,0:T(8,128)(2,1)}), bf16[8,16,3072]{2,1,0:T(8,128)(2,1)S(1)}, u32[]{:S(2)}, u32[]{:S(2)}) %all-to-all-start.3) | async-done | bytes 786464 | tf_op jit(solution)/shard_map/all_to_all | solution.py:119
  107.0 0.1 convert_reduce_fusion
  107.2 0.8 broadcast_in_dim.99
  108.0 3.5 %all-to-all-start.4 = ((bf16[8,16,1536]{2,1,0:T(8,128)(2,1)}), bf16[8,16,1536]{2,1,0:T(8,128)(2,1)S(1)}, u32[]{:S(2)}, u32[]{:S(2)}) async-start(bf16[8,16,1536]{2,1,0:T(8,128)(2,1)} %broadcast_in_dim.99), calls=%async_computation.4 | async-start | bytes 786432 | tf_op jit(solution)/shard_map/all_to_all | solution.py:146
  111.5 0.7 add_bitcast_fusion
  112.1 1.1 fusion.38
  113.2 1.2 fusion.6
  114.4 12.1 %all-to-all-done.4 = bf16[8,16,1536]{2,1,0:T(8,128)(2,1)S(1)} async-done(((bf16[8,16,1536]{2,1,0:T(8,128)(2,1)}), bf16[8,16,1536]{2,1,0:T(8,128)(2,1)S(1)}, u32[]{:S(2)}, u32[]{:S(2)}) %all-to-all-start.4) | async-done | bytes 393248 | tf_op jit(solution)/shard_map/all_to_all | solution.py:146
  126.5 2.4 %collective-permute-start.3 = (bf16[128,1536]{1,0:T(8,128)(2,1)S(1)}, bf16[128,1536]{1,0:T(8,128)(2,1)S(1)}, u32[]{:S(2)}, u32[]{:S(2)}) collective-permute-start(bf16[128,1536]{1,0:T(8,128)(2,1)S(1)} %bitcast.230), channel_id=1, source_target_pairs={{0,32},{32,0},{64,96},{96,64},{128,160},{160,128},{192,224},{224,1... | collective-permute-start | bytes 1179656 | tf_op jit(solution)/shard_map/ppermute | solution.py:154
  128.9 1.3 fusion.4
  130.2 1.9 %convolution_convert_fusion.2 = bf16[384,3,128]{2,0,1:T(8,128)(2,1)} fusion(f32[256,1,1,128]{0,3,2,1:T(8,128)} %add_bitcast_fusion, f32[256,1,1,128]{0,3,2,1:T(8,128)S(1)} %copy-done.8, f32[256,1,1,128]{0,3,2,1:T(8,128)S(1)} %fusion.4, bf16[128,384]{0,1:T(8,128)(2,1)S(1)} %copy.63, bf16[128,384]{0,1:T(8,128)(2,1)S(1)} %copy.62), kind=kOutput, calls=%fused_computation.6 | convolution fusion | flops 76333056 | bytes 884736 | tf_op jit(solution)/shard_map/pd,pe->de/dot_general | solution.py:164
  132.2 0.8 convolution_convert_fusion.3
  133.0 1.2 convolution_convert_fusion
  134.2 1.1 convolution_convert_fusion.1
  (66 shorter events, 1.4 us)
Async XLA Ops:
  0.6 34.5 %copy-start = (bf16[384,768]{1,0:T(8,128)(2,1)S(1)}, bf16[384,768]{1,0:T(8,128)(2,1)}, u32[]{:S(2)}) copy-start(bf16[384,768]{1,0:T(8,128)(2,1)} %param.18) | copy-start | bytes 1769476
  0.6 16.5 %copy-start.7 = (bf16[384,3,128]{2,0,1:T(8,128)(2,1)S(1)}, bf16[384,3,128]{2,0,1:T(8,128)(2,1)}, u32[]{:S(2)}) copy-start(bf16[384,3,128]{2,0,1:T(8,128)(2,1)} %param.16) | copy-start | bytes 884740
  2.2 25.4 %all-to-all-start = ((bf16[32,2,8,384]{3,2,1,0:T(8,128)(2,1)}), bf16[32,2,8,384]{3,2,1,0:T(8,128)(2,1)S(1)}, u32[]{:S(2)}, u32[]{:S(2)}) async-start(bf16[32,2,8,384]{3,2,1,0:T(8,128)(2,1)} %broadcast_in_dim.80), calls=%async_computation | async-start | bytes 786432 | tf_op jit(solution)/shard_map/all_to_all | solution.py:82
  27.6 1.0 copy-start.9
  27.7 1.2 copy-start.10
  29.2 6.4 %copy-start.4 = (bf16[384,768]{1,0:T(8,128)(2,1)S(1)}, bf16[384,768]{1,0:T(8,128)(2,1)}, u32[]{:S(2)}) copy-start(bf16[384,768]{1,0:T(8,128)(2,1)} %param.14) | copy-start | bytes 1769476
  29.3 6.7 %copy-start.5 = (bf16[768,384]{1,0:T(8,128)(2,1)S(1)}, bf16[768,384]{1,0:T(8,128)(2,1)}, u32[]{:S(2)}) copy-start(bf16[768,384]{1,0:T(8,128)(2,1)} %param.19) | copy-start | bytes 1769476
  29.3 7.4 %collective-permute-start = (f32[128,1024]{1,0:T(8,128)S(1)}, f32[128,1024]{1,0:T(8,128)S(1)}, u32[]{:S(2)}, u32[]{:S(2)}) collective-permute-start(f32[128,1024]{1,0:T(8,128)S(1)} %slice.83), channel_id=1, source_target_pairs={{0,32},{32,0},{64,96},{96,64},{128,160},{160,128},{192,224},{224,1... | collective-permute-start | bytes 1572872 | tf_op jit(solution)/shard_map/ppermute | solution.py:110
  37.8 19.3 %all-to-all-start.1 = ((f16[8,16,1152]{2,1,0:T(8,128)(2,1)}), f16[8,16,1152]{2,1,0:T(8,128)(2,1)}, u32[]{:S(2)}, u32[]{:S(2)}) async-start(f16[8,16,1152]{2,1,0:T(8,128)(2,1)} %pad_maximum_fusion.4), calls=%async_computation.1 | async-start | bytes 589824 | tf_op jit(solution)/shard_map/all_to_all | solution.py:117
  46.5 2.1 %copy-start.1 = (f32[256,3072]{1,0:T(8,128)}, f32[256,3072]{1,0:T(8,128)S(1)}, u32[]{:S(2)}) copy-start(f32[256,3072]{1,0:T(8,128)S(1)} %pad_maximum_fusion) | copy-start | bytes 9437188
  48.6 28.2 %collective-permute-start.2 = (f32[128,3072]{1,0:T(8,128)}, f32[128,3072]{1,0:T(8,128)}, u32[]{:S(2)}, u32[]{:S(2)}) collective-permute-start(f32[128,3072]{1,0:T(8,128)} %slice.98), channel_id=1, source_target_pairs={{0,32},{32,0},{64,96},{96,64},{128,160},{160,128},{192,224},{224,1... | collective-permute-start | bytes 4718600 | tf_op jit(solution)/shard_map/ppermute | solution.py:111
  72.1 11.3 %collective-permute-start.1 = (f16[128,1152]{0,1:T(8,128)(2,1)S(1)}, f16[128,1152]{0,1:T(8,128)(2,1)S(1)}, u32[]{:S(2)}, u32[]{:S(2)}) collective-permute-start(f16[128,1152]{0,1:T(8,128)(2,1)S(1)} %copy.54), channel_id=1, source_target_pairs={{0,32},{32,0},{64,96},{96,64},{128,160},{160,128},{192,224},{224,1... | collective-permute-start | bytes 884744 | tf_op jit(solution)/shard_map/ppermute | solution.py:137
  79.8 27.1 %all-to-all-start.3 = ((bf16[8,16,3072]{2,1,0:T(8,128)(2,1)}), bf16[8,16,3072]{2,1,0:T(8,128)(2,1)S(1)}, u32[]{:S(2)}, u32[]{:S(2)}) async-start(bf16[8,16,3072]{2,1,0:T(8,128)(2,1)} %bitcast.54), calls=%async_computation.3 | async-start | bytes 1572864 | tf_op jit(solution)/shard_map/all_to_all | solution.py:119
  85.7 1.1 copy-start.2
  107.1 4.4 %copy-start.6 = (f32[256,128]{0,1:T(8,128)S(1)}, f32[256,128]{0,1:T(8,128)}, u32[]{:S(2)}) copy-start(f32[256,128]{0,1:T(8,128)} %get-tuple-element.21) | copy-start | bytes 393220
  107.1 6.1 %copy-start.3 = (f32[256,256]{0,1:T(8,128)S(1)}, f32[256,256]{0,1:T(8,128)}, u32[]{:S(2)}) copy-start(f32[256,256]{0,1:T(8,128)} %copy-done.2) | copy-start | bytes 786436
  108.0 18.5 %all-to-all-start.4 = ((bf16[8,16,1536]{2,1,0:T(8,128)(2,1)}), bf16[8,16,1536]{2,1,0:T(8,128)(2,1)S(1)}, u32[]{:S(2)}, u32[]{:S(2)}) async-start(bf16[8,16,1536]{2,1,0:T(8,128)(2,1)} %broadcast_in_dim.99), calls=%async_computation.4 | async-start | bytes 786432 | tf_op jit(solution)/shard_map/all_to_all | solution.py:146
  112.1 18.1 %copy-start.8 = (f32[256,1,1,128]{0,3,2,1:T(8,128)S(1)}, f32[256,1,1,128]{0,3,2,1:T(8,128)}, u32[]{:S(2)}) copy-start(f32[256,1,1,128]{0,3,2,1:T(8,128)} %add_bitcast_fusion.1) | copy-start | bytes 393220
  126.5 6.5 %collective-permute-start.3 = (bf16[128,1536]{1,0:T(8,128)(2,1)S(1)}, bf16[128,1536]{1,0:T(8,128)(2,1)S(1)}, u32[]{:S(2)}, u32[]{:S(2)}) collective-permute-start(bf16[128,1536]{1,0:T(8,128)(2,1)S(1)} %bitcast.230), channel_id=1, source_target_pairs={{0,32},{32,0},{64,96},{96,64},{128,160},{160,128},{192,224},{224,1... | collective-permute-start | bytes 1179656 | tf_op jit(solution)/shard_map/ppermute | solution.py:154

commit v2 on v0

v2 whole, which is shorter than its diff:
```python
import math

import jax
import jax.numpy as jnp
from jax import lax
from jax.experimental import pallas as pl
from jax.experimental.pallas import tpu as pltpu
from jax.sharding import PartitionSpec as P

HD = 128
F32 = jnp.float32
BF16 = jnp.bfloat16
VMEM = pl.BlockSpec(memory_space=pltpu.VMEM)
SMEM = pl.BlockSpec(memory_space=pltpu.SMEM)

NN = ((1,), (0,))
NT = ((1,), (1,))
TN = ((0,), (0,))


def dot(left, right, dims):
    return lax.dot_general(left, right, (dims, ((), ())), preferred_element_type=F32)


def halves(x):
    high = x.astype(BF16)
    return high, (x - high.astype(F32)).astype(BF16)


def dot3(left, right, dims):
    return (
        dot(left[0], right[0], dims) + dot(left[0], right[1], dims) + dot(left[1], right[0], dims)
    )


def mean(x):
    return jnp.mean(x, axis=-1, keepdims=True)


def total(x):
    return jnp.sum(x, axis=-1, keepdims=True)


def centre(x):
    return x - mean(x)


def normalize(x, x_tan):
    centred = centre(x)
    inverse = lax.rsqrt(mean(centred * centred) + 1e-06)
    y = centred * inverse
    shift = mean(y * x_tan)
    return y, (centre(x_tan) - y * shift) * inverse, inverse, shift


def normalize_back(y, y_tan, inverse, shift, cot, cot_tan):
    along = mean(y * cot)
    back = (centre(cot) - y * along) * inverse
    along_tan = mean(y_tan * cot) + mean(y * cot_tan)
    return (centre(cot_tan) - y_tan * along - y * along_tan - back * shift) * inverse


def attention(q, k, v, tq, tk, tv, cot, cot_tan):
    scale = 1.0 / math.sqrt(HD)
    qn, dqn, q_inverse, q_shift = normalize(q, tq)
    kn, dkn, k_inverse, k_shift = normalize(k, tk)
    qs, dqs, ks, dks = halves(qn * scale), halves(dqn * scale), halves(kn), halves(dkn)
    vs, dvs, cs, dcs = halves(v), halves(tv), halves(cot), halves(cot_tan)
    raised = jnp.exp(dot3(qs, ks, NT))
    probs = raised / total(raised)
    score_tan = dot3(dqs, ks, NT) + dot3(qs, dks, NT)
    probs_tan = probs * (score_tan - total(probs * score_tan))
    ps, dps = halves(probs), halves(probs_tan)
    mixed_tan = dot3(dps, vs, NN) + dot3(ps, dvs, NN)
    v_tan = dot3(dps, cs, TN) + dot3(ps, dcs, TN)
    cot_probs = dot3(cs, vs, NT)
    cot_probs_tan = dot3(dcs, vs, NT) + dot3(cs, dvs, NT)
    away = cot_probs - total(probs * cot_probs)
    away_tan = cot_probs_tan - total(probs_tan * cot_probs + probs * cot_probs_tan)
    ss, dss = halves(probs * away), halves(probs_tan * away + probs * away_tan)
    q_cot = scale * dot3(ss, ks, NN)
    q_cot_tan = scale * (dot3(dss, ks, NN) + dot3(ss, dks, NN))
    k_cot = dot3(ss, qs, TN)
    k_cot_tan = dot3(dss, qs, TN) + dot3(ss, dqs, TN)
    q_tan = normalize_back(qn, dqn, q_inverse, q_shift, q_cot, q_cot_tan)
    k_tan = normalize_back(kn, dkn, k_inverse, k_shift, k_cot, k_cot_tan)
    return mixed_tan, q_tan, k_tan, v_tan


def sums_kernel(rows, cots, rows_b, cots_b, w_rows, w_cots, w_rows_b, w_cots_b, out):
    front = dot(rows[...], w_rows[...], NN) + dot(rows_b[...], w_rows_b[...], NN)
    back = dot(cots[...], w_cots[...], NT) + dot(cots_b[...], w_cots_b[...], NT)
    hidden = (w_rows.shape[1] - 3 * HD) // 2
    high, low = halves(front[:, :HD])
    out[:, :HD] = high
    out[:, HD : 2 * HD] = low
    out[:, 2 * HD : 4 * HD] = front[:, HD : 3 * HD].astype(BF16)
    out[:, 4 * HD : 5 * HD] = back[:, :HD].astype(BF16)
    out[:, 5 * HD : 5 * HD + 2 * hidden] = front[:, 3 * HD :].astype(BF16)
    out[:, 5 * HD + 2 * hidden :] = back[:, HD:].astype(BF16)


def results_kernel(core, mine, theirs, rows, cots, qkv_out, out_out, up_out, down_out):
    first = core[0] == 0
    zero = jnp.where(first, mine[...], theirs[...])
    one = jnp.where(first, theirs[...], mine[...])

    def wide(x, at):
        return x[:, at * HD : (at + 1) * HD].astype(F32) + x[:, (at + 4) * HD : (at + 5) * HD].astype(F32)

    q, v, tq, cot = (wide(zero, at) for at in range(4))
    k, tk, tv, cot_tan = (wide(one, at) for at in range(4))
    mixed, q_tan, k_tan, v_tan = attention(q, k, v, tq, tk, tv, cot, cot_tan)
    rows_all, cots_all = rows[...], cots[...]
    hidden = (zero.shape[1] - 8 * HD) // 2
    for at, part in enumerate((zero, one)):
        place = slice(at * hidden, (at + 1) * hidden)
        act = part[:, 8 * HD : 8 * HD + hidden]
        hid = part[:, 8 * HD + hidden :]
        up_out[:, place] = dot(rows_all, hid, TN).astype(BF16)
        down_out[place, :] = dot(act, cots_all, TN).astype(BF16)
    for at, part in enumerate((q_tan, k_tan, v_tan)):
        qkv_out[at] = dot(rows_all, part.astype(BF16), TN).astype(BF16)
    out_out[...] = dot(mixed.astype(BF16), cots_all, TN).astype(BF16)


def hidden_pair(pre, cot_in):
    result, pull = jax.vjp(jax.nn.gelu, pre)
    return (result, pull(cot_in)[0])


def body(patches, cotangent, w_qkv, w_out, w_up, w_down, dir_qkv, dir_out, dir_up, dir_down):
    wide = lax.axis_size("mx")
    long = lax.axis_size("my")
    chips = wide // 2
    core = lax.rem(lax.axis_index("mx"), 2)
    ring = [[chip * 2 + c for chip in range(chips)] for c in range(2)]
    swap = [(i, i ^ 1) for i in range(wide)]
    width = w_qkv.shape[0]
    hidden = w_up.shape[1] // 2
    count = patches.shape[0] * long
    share = count // chips

    both = jnp.stack([patches, cotangent])
    gathered = lax.all_to_all(jnp.broadcast_to(both, (long,) + both.shape), "my", 0, 0, tiled=True)
    swapped = lax.ppermute(gathered, "mx", swap)

    def pick(at):
        zero = jnp.concatenate([w_qkv[:, 0], w_qkv[:, 2], dir_qkv[:, 0]], axis=1)
        one = jnp.concatenate([w_qkv[:, 1], dir_qkv[:, 1], dir_qkv[:, 2]], axis=1)
        cut = lambda a, dim: lax.dynamic_slice_in_dim(a, at * hidden, hidden, dim)
        front = [jnp.where(at == 0, zero, one), cut(w_up, 1), cut(dir_up, 1)]
        back = [jnp.where(at == 0, w_out, dir_out), cut(w_down, 0), cut(dir_down, 0)]
        return jnp.concatenate(front, axis=1), jnp.concatenate(back, axis=0)

    kept = pick(core)
    lent = pick(1 - core)
    taken = tuple(lax.ppermute(a, "mx", swap) for a in lent)

    flat = lambda a, at: a[:, at].reshape(count, width)
    rows, cots = flat(gathered, 0), flat(gathered, 1)
    columns = 5 * HD + 4 * hidden
    message = pl.pallas_call(
        sums_kernel,
        out_shape=jax.ShapeDtypeStruct((count, columns), BF16),
        in_specs=[VMEM] * 8,
        out_specs=VMEM,
        compiler_params=pltpu.CompilerParams(vmem_limit_bytes=48 * 2**20),
        name="sums",
    )(rows, cots, flat(swapped, 0), flat(swapped, 1), *kept, *taken)
    parts = lax.all_to_all(
        message.reshape(chips, share, columns), "mx", 0, 0, tiled=True, axis_index_groups=ring
    )
    sums = jnp.sum(parts.astype(F32), axis=0)
    attn = jnp.concatenate([sums[:, :HD] + sums[:, HD : 2 * HD], sums[:, 2 * HD : 5 * HD]], axis=1)
    pre_hidden, tan_hidden, cot_act, tan_act = jnp.split(sums[:, 5 * HD :], 4, axis=1)
    hid_tan = jax.jvp(hidden_pair, (pre_hidden, cot_act), (tan_hidden, tan_act))[1]
    attn_high = lax.reduce_precision(attn, 8, 7)
    reply = jnp.concatenate([attn_high, attn - attn_high, hid_tan[0], hid_tan[1]], axis=1).astype(BF16)
    mine = lax.all_to_all(
        jnp.broadcast_to(reply, (chips,) + reply.shape),
        "mx",
        0,
        0,
        tiled=True,
        axis_index_groups=ring,
    ).reshape(count, -1)
    theirs = lax.ppermute(mine, "mx", swap)
    hvp_qkv, hvp_out, hvp_up, hvp_down = pl.pallas_call(
        results_kernel,
        out_shape=(
            jax.ShapeDtypeStruct((3, width, HD), BF16),
            jax.ShapeDtypeStruct(w_out.shape, BF16),
            jax.ShapeDtypeStruct(w_up.shape, BF16),
            jax.ShapeDtypeStruct(w_down.shape, BF16),
        ),
        in_specs=[SMEM] + [VMEM] * 4,
        out_specs=(VMEM,) * 4,
        compiler_params=pltpu.CompilerParams(vmem_limit_bytes=48 * 2**20),
        name="results",
    )(core.reshape(1).astype(jnp.int32), mine, theirs, rows, cots)
    return jnp.transpose(hvp_qkv, (1, 0, 2)), hvp_out, hvp_up, hvp_down


def solution(mesh):
    return jax.shard_map(
        body,
        mesh=mesh,
        in_specs=(
            P("my", "mx"),
            P("my", "mx"),
            P("mx", None, "my"),
            P("my", "mx"),
            P("mx", "my"),
            P("my", "mx"),
            P("mx", None, "my"),
            P("my", "mx"),
            P("mx", "my"),
            P("my", "mx"),
        ),
        out_specs=(P("mx", None, "my"), P("my", "mx"), P("mx", "my"), P("my", "mx")),
        check_vma=False,
    )
```

time: 270 us -> 111 us (0.41)
  waiting for transfers between devices: 147 us -> 7.35 us
  starting transfers between devices: 0.04 us -> 28.7 us
  matrix products: 23.4 us -> 0 us
  blocking collectives: 76.9 us -> 63 us
  between operations: 14.7 us -> 0.92 us
  Pallas kernels: 0 us -> 5.7 us
    psum x1 -> x0, waiting for transfers between devices: 147 us -> none  [body(): lax.psum((project(rows_all, flat_weight), project(rows_all, flat_directio...]
    all_gather x2 -> x0, blocking collectives: 76.9 us -> none  [the longest x1 42.5 us: body(): lax.all_gather(patches, 'my', axis=0, tiled=True)]
    all_to_all x0 -> x2, blocking collectives: none -> 63 us  [the longest x1 36.2 us: body(): lax.all_to_all(message.reshape(chips, share, columns), 'mx', 0, 0, tiled=...]
    dot_general x28 -> x0, matrix products: 23.4 us -> none  [the longest x7 5.95 us: attend(): jnp.einsum('hpk,khd->phd', probs, values, precision=lax.Precision.HIGHEST)]
    ppermute x0 -> x4, starting transfers between devices: none -> 15 us  [the longest x1 5.73 us: body(): swapped = lax.ppermute(gathered, 'mx', swap)]
    all_to_all x0 -> x1, starting transfers between devices: none -> 13.7 us  [body(): lax.all_to_all(jnp.broadcast_to(both, (long,) + both.shape), 'my', 0, 0,...]
    pallas_call x0 -> x2, Pallas kernels: none -> 5.7 us  [the longest x1 4.32 us: body(): pl.pallas_call(results_kernel, out_shape=(jax.ShapeDtypeStruct((3, width,...]
    all_to_all x0 -> x1, waiting for transfers between devices: none -> 4.15 us  [body(): lax.all_to_all(jnp.broadcast_to(both, (long,) + both.shape), 'my', 0, 0,...]
  transfers between devices with their start and end apart: 1 -> 5, of which waited for: 1 -> 3; matrix products, arithmetic and copies ran while one was open for 0% -> 2% of each run, Pallas kernels for 0% -> 0%
where the time goes in v2:
time: 111 us; the launch traced here: 110 us
  blocking collectives  63 us (57%)
  starting transfers between devices  28.7 us (26%)
  waiting for transfers between devices  7.35 us (7%)
  Pallas kernels  5.7 us (5%)
  other arithmetic  3.29 us (3%)
  local copies, waits for them, and re-layouts  1.28 us (1%)
    all_to_all x1, blocking collectives, body(): lax.all_to_all(message.reshape(chips, share, columns), 'mx', 0, 0, tiled=...  36.2 us
    all_to_all x1, blocking collectives, body(): lax.all_to_all(jnp.broadcast_to(reply, (chips,) + reply.shape), 'mx', 0,...  26.8 us
    all_to_all x1, starting transfers between devices, body(): lax.all_to_all(jnp.broadcast_to(both, (long,) + both.shape), 'my', 0, 0,...  13.7 us
    ppermute x1, starting transfers between devices, body(): swapped = lax.ppermute(gathered, 'mx', swap)  5.73 us
    ppermute x2, starting transfers between devices, body(): taken = tuple((lax.ppermute(a, 'mx', swap) for a in lent))  4.89 us
    ppermute x1, starting transfers between devices, body(): theirs = lax.ppermute(mine, 'mx', swap)  4.4 us
    pallas_call x1, Pallas kernels, body(): pl.pallas_call(results_kernel, out_shape=(jax.ShapeDtypeStruct((3, width,...  4.32 us
    all_to_all x1, waiting for transfers between devices, body(): lax.all_to_all(jnp.broadcast_to(both, (long,) + both.shape), 'my', 0, 0,...  4.15 us
  transfers between devices with their start and end apart: 5, of which 3 were waited for; matrix products, arithmetic and copies ran while one was open for 2% of the time, Pallas kernels for 0%

profile of v2, /device:TPU:1, one launch (start us, length us, event | category | flops | bytes accessed | tf_op | source)
XLA Modules:
  0.0 110.3 jit_solution(370448377442796105)
XLA Ops:
  0.6 0.0 copy-start.4
  0.6 0.0 copy-start.5
  0.7 0.8 pad_maximum_fusion.8
  1.4 0.0 copy-start
  1.4 0.0 copy-start.1
  1.4 0.8 broadcast_in_dim.6
  2.2 13.7 %all-to-all-start = ((bf16[32,2,8,384]{3,2,1,0:T(8,128)(2,1)}), bf16[32,2,8,384]{3,2,1,0:T(8,128)(2,1)S(1)}, u32[]{:S(2)}, u32[]{:S(2)}) async-start(bf16[32,2,8,384]{3,2,1,0:T(8,128)(2,1)} %broadcast_in_dim.6), calls=%async_computation | async-start | bytes 786432 | tf_op jit(solution)/shard_map/all_to_all | solution.py:145
  16.0 0.0 copy-done.4
  16.0 0.0 copy-done.5
  16.0 0.0 copy-done
  16.0 0.0 copy-done.1
  16.0 0.1 constant_dynamic-slice_fusion.2
  16.2 0.2 broadcast_select_fusion
  16.3 0.0 copy-start.2
  16.4 0.0 copy-start.3
  16.4 1.0 pad_maximum_fusion.1
  17.4 0.0 copy-start.6
  17.4 0.0 copy-start.7
  17.4 3.0 %collective-permute-start.1 = (bf16[384,1152]{1,0:T(8,128)(2,1)}, bf16[384,1152]{1,0:T(8,128)(2,1)S(1)}, u32[]{:S(2)}, u32[]{:S(2)}) collective-permute-start(bf16[384,1152]{1,0:T(8,128)(2,1)} %pad_maximum_fusion.1), channel_id=1, source_target_pairs={{0,32},{32,0},{64,96},{96,64},{128,160},{160,128},{192,224},{224,1... | collective-permute-start | bytes 2654216 | tf_op jit(solution)/shard_map/ppermute | solution.py:158
  20.4 0.0 copy-done.2
  20.4 0.0 copy-done.3
  20.4 0.1 constant_dynamic-slice_fusion
  20.5 0.0 copy-done.6
  20.5 0.0 copy-done.7
  20.6 0.9 pad_maximum_fusion.3
  21.5 1.9 %collective-permute-start.2 = (bf16[896,384]{1,0:T(8,128)(2,1)}, bf16[896,384]{1,0:T(8,128)(2,1)S(1)}, u32[]{:S(2)}, u32[]{:S(2)}) collective-permute-start(bf16[896,384]{1,0:T(8,128)(2,1)} %pad_maximum_fusion.3), channel_id=1, source_target_pairs={{0,32},{32,0},{64,96},{96,64},{128,160},{160,128},{192,224},{224,1... | collective-permute-start | bytes 2064392 | tf_op jit(solution)/shard_map/ppermute | solution.py:158
  23.4 4.2 %all-to-all-done = bf16[32,2,8,384]{3,2,1,0:T(8,128)(2,1)S(1)} async-done(((bf16[32,2,8,384]{3,2,1,0:T(8,128)(2,1)}), bf16[32,2,8,384]{3,2,1,0:T(8,128)(2,1)S(1)}, u32[]{:S(2)}, u32[]{:S(2)}) %all-to-all-start) | async-done | bytes 393248 | tf_op jit(solution)/shard_map/all_to_all | solution.py:145
  27.6 5.7 %collective-permute-start = (bf16[32,2,8,384]{3,2,1,0:T(8,128)(2,1)S(1)}, bf16[32,2,8,384]{3,2,1,0:T(8,128)(2,1)S(1)}, u32[]{:S(2)}, u32[]{:S(2)}) collective-permute-start(bf16[32,2,8,384]{3,2,1,0:T(8,128)(2,1)S(1)} %all-to-all-done), channel_id=1, source_target_pairs={{0,32},{32,0},{64,96},{96,64},{128,160},{160,128},{192,224},{224,1... | collective-permute-start | bytes 1179656 | tf_op jit(solution)/shard_map/ppermute | solution.py:146
  33.3 0.1 pad_maximum_fusion.w_rows
  33.4 0.1 pad_maximum_fusion.2.w_cots
  33.5 1.1 %collective-permute-done = bf16[32,2,8,384]{3,2,1,0:T(8,128)(2,1)S(1)} collective-permute-done((bf16[32,2,8,384]{3,2,1,0:T(8,128)(2,1)S(1)}, bf16[32,2,8,384]{3,2,1,0:T(8,128)(2,1)S(1)}, u32[]{:S(2)}, u32[]{:S(2)}) %collective-permute-start) | collective-permute-done | bytes 393248 | tf_op jit(solution)/shard_map/ppermute | solution.py:146
  34.7 0.0 collective-permute-done.2.w_cots_b
  34.7 0.0 collective-permute-done.1.w_rows_b
  34.7 1.4 %sums.1 = bf16[256,2176]{1,0:T(8,128)(2,1)S(1)} custom-call(bf16[256,384]{1,0:T(8,128)(2,1)S(1)} %get-tuple-element.25.rows, bf16[256,384]{1,0:T(8,128)(2,1)S(1)} %get-tuple-element.24.cots, bf16[256,384]{1,0:T(8,128)(2,1)S(1)} %get-tuple-element.23.rows_b, bf16[256,384]{1,0:T(8,128)(2,1)S(1)} %get-tuple-element.22.cots_b, ...), custom_call_target="tpu_custom_call" | custom-call | tf_op jit(solution)/shard_map/sums/pallas_call | solution.py:163
  36.1 36.2 %all_to_all.15 = bf16[8,32,2176]{2,1,0:T(8,128)(2,1)S(1)} all-to-all(bf16[8,32,2176]{2,1,0:T(8,128)(2,1)S(1)} %bitcast.26), channel_id=1, replica_groups={{0,64,128,192,256,320,384,448},{32,96,160,224,288,352,416,480},{1,65,12..., dimensions={0} | all-to-all | bytes 2228224 | tf_op jit(solution)/shard_map/all_to_all | solution.py:171
  72.3 0.1 convert_reduce_fusion
  72.5 0.1 fusion.6
  72.6 0.1 broadcast_in_dim.7
  72.7 26.8 %all_to_all.16 = bf16[8,32,1792]{2,1,0:T(8,128)(2,1)S(1)} all-to-all(bf16[8,32,1792]{2,1,0:T(8,128)(2,1)S(1)} %broadcast_in_dim.7), channel_id=1, replica_groups={{0,64,128,192,256,320,384,448},{32,96,160,224,288,352,416,480},{1,65,12..., dimensions={0} | all-to-all | bytes 1835008 | tf_op jit(solution)/shard_map/all_to_all | solution.py:180
  99.5 4.4 %collective-permute-start.3 = (bf16[256,1792]{1,0:T(8,128)(2,1)S(1)}, bf16[256,1792]{1,0:T(8,128)(2,1)S(1)}, u32[]{:S(2)}, u32[]{:S(2)}) collective-permute-start(bf16[256,1792]{1,0:T(8,128)(2,1)S(1)} %bitcast.27), channel_id=1, source_target_pairs={{0,32},{32,0},{64,96},{96,64},{128,160},{160,128},{192,224},{224,1... | collective-permute-start | bytes 2752520 | tf_op jit(solution)/shard_map/ppermute | solution.py:188
  103.9 2.1 %collective-permute-done.3.theirs = bf16[256,1792]{1,0:T(8,128)(2,1)S(1)} collective-permute-done((bf16[256,1792]{1,0:T(8,128)(2,1)S(1)}, bf16[256,1792]{1,0:T(8,128)(2,1)S(1)}, u32[]{:S(2)}, u32[]{:S(2)}) %collective-permute-start.3) | collective-permute-done | bytes 917536 | tf_op jit(solution)/shard_map/ppermute | solution.py:188
  106.0 4.3 %results.1 = (bf16[3,384,128]{2,1,0:T(8,128)(2,1)}, bf16[128,384]{1,0:T(8,128)(2,1)}, bf16[384,768]{1,0:T(8,128)(2,1)}, bf16[768,384]{1,0:T(8,128)(2,1)}) custom-call(s32[1]{0:T(128)} %bitcast.core, bf16[256,1792]{1,0:T(8,128)(2,1)S(1)} %bitcast.28, bf16[256,1792]{1,0:T(8,128)(2,1)S(1)} %collective-permute-done.3.theirs, ...), custom_call_target="tpu_custom_call" | custom-call | tf_op jit(solution)/shard_map/results/pallas_call | solution.py:189
  (7 shorter events, 0.2 us)
Async XLA Ops:
  0.6 15.3 %copy-start.4 = (bf16[384,3,128]{2,0,1:T(8,128)(2,1)S(1)}, bf16[384,3,128]{2,0,1:T(8,128)(2,1)}, u32[]{:S(2)}) copy-start(bf16[384,3,128]{2,0,1:T(8,128)(2,1)} %param.16) | copy-start | bytes 884740
  0.6 15.3 %copy-start.5 = (bf16[384,3,128]{2,0,1:T(8,128)(2,1)S(1)}, bf16[384,3,128]{2,0,1:T(8,128)(2,1)}, u32[]{:S(2)}) copy-start(bf16[384,3,128]{2,0,1:T(8,128)(2,1)} %param.12) | copy-start | bytes 884740
  1.4 14.6 %copy-start = (bf16[384,768]{1,0:T(8,128)(2,1)S(1)}, bf16[384,768]{1,0:T(8,128)(2,1)}, u32[]{:S(2)}) copy-start(bf16[384,768]{1,0:T(8,128)(2,1)} %param.18) | copy-start | bytes 1769476
  1.4 14.6 %copy-start.1 = (bf16[384,768]{1,0:T(8,128)(2,1)S(1)}, bf16[384,768]{1,0:T(8,128)(2,1)}, u32[]{:S(2)}) copy-start(bf16[384,768]{1,0:T(8,128)(2,1)} %param.14) | copy-start | bytes 1769476
  2.2 25.4 %all-to-all-start = ((bf16[32,2,8,384]{3,2,1,0:T(8,128)(2,1)}), bf16[32,2,8,384]{3,2,1,0:T(8,128)(2,1)S(1)}, u32[]{:S(2)}, u32[]{:S(2)}) async-start(bf16[32,2,8,384]{3,2,1,0:T(8,128)(2,1)} %broadcast_in_dim.6), calls=%async_computation | async-start | bytes 786432 | tf_op jit(solution)/shard_map/all_to_all | solution.py:145
  16.3 4.0 %copy-start.2 = (bf16[768,384]{1,0:T(8,128)(2,1)S(1)}, bf16[768,384]{1,0:T(8,128)(2,1)}, u32[]{:S(2)}) copy-start(bf16[768,384]{1,0:T(8,128)(2,1)} %param.19) | copy-start | bytes 1769476
  16.4 4.0 %copy-start.3 = (bf16[768,384]{1,0:T(8,128)(2,1)S(1)}, bf16[768,384]{1,0:T(8,128)(2,1)}, u32[]{:S(2)}) copy-start(bf16[768,384]{1,0:T(8,128)(2,1)} %param.15) | copy-start | bytes 1769476
  17.4 3.2 %copy-start.6 = (bf16[128,384]{1,0:T(8,128)(2,1)S(1)}, bf16[128,384]{1,0:T(8,128)(2,1)}, u32[]{:S(2)}) copy-start(bf16[128,384]{1,0:T(8,128)(2,1)} %param.13) | copy-start | bytes 294916
  17.4 3.2 %copy-start.7 = (bf16[128,384]{1,0:T(8,128)(2,1)S(1)}, bf16[128,384]{1,0:T(8,128)(2,1)}, u32[]{:S(2)}) copy-start(bf16[128,384]{1,0:T(8,128)(2,1)} %param.17) | copy-start | bytes 294916
  17.4 17.3 %collective-permute-start.1 = (bf16[384,1152]{1,0:T(8,128)(2,1)}, bf16[384,1152]{1,0:T(8,128)(2,1)S(1)}, u32[]{:S(2)}, u32[]{:S(2)}) collective-permute-start(bf16[384,1152]{1,0:T(8,128)(2,1)} %pad_maximum_fusion.1), channel_id=1, source_target_pairs={{0,32},{32,0},{64,96},{96,64},{128,160},{160,128},{192,224},{224,1... | collective-permute-start | bytes 2654216 | tf_op jit(solution)/shard_map/ppermute | solution.py:158
  21.5 13.2 %collective-permute-start.2 = (bf16[896,384]{1,0:T(8,128)(2,1)}, bf16[896,384]{1,0:T(8,128)(2,1)S(1)}, u32[]{:S(2)}, u32[]{:S(2)}) collective-permute-start(bf16[896,384]{1,0:T(8,128)(2,1)} %pad_maximum_fusion.3), channel_id=1, source_target_pairs={{0,32},{32,0},{64,96},{96,64},{128,160},{160,128},{192,224},{224,1... | collective-permute-start | bytes 2064392 | tf_op jit(solution)/shard_map/ppermute | solution.py:158
  27.6 7.1 %collective-permute-start = (bf16[32,2,8,384]{3,2,1,0:T(8,128)(2,1)S(1)}, bf16[32,2,8,384]{3,2,1,0:T(8,128)(2,1)S(1)}, u32[]{:S(2)}, u32[]{:S(2)}) collective-permute-start(bf16[32,2,8,384]{3,2,1,0:T(8,128)(2,1)S(1)} %all-to-all-done), channel_id=1, source_target_pairs={{0,32},{32,0},{64,96},{96,64},{128,160},{160,128},{192,224},{224,1... | collective-permute-start | bytes 1179656 | tf_op jit(solution)/shard_map/ppermute | solution.py:146
  99.5 6.5 %collective-permute-start.3 = (bf16[256,1792]{1,0:T(8,128)(2,1)S(1)}, bf16[256,1792]{1,0:T(8,128)(2,1)S(1)}, u32[]{:S(2)}, u32[]{:S(2)}) collective-permute-start(bf16[256,1792]{1,0:T(8,128)(2,1)S(1)} %bitcast.27), channel_id=1, source_target_pairs={{0,32},{32,0},{64,96},{96,64},{128,160},{160,128},{192,224},{224,1... | collective-permute-start | bytes 2752520 | tf_op jit(solution)/shard_map/ppermute | solution.py:188

commit v3 on v2

--- a/solution.py
+++ b/solution.py
@@ -31,6 +31,23 @@
     return (
         dot(left[0], right[0], dims) + dot(left[0], right[1], dims) + dot(left[1], right[0], dims)
     )
+
+
+def low_code(x, high):
+    rest = (x - high) / jnp.where(high == 0.0, 1.0, high)
+    return jnp.clip(jnp.floor(rest * 512.0 + 2.0), 0.0, 3.0)
+
+
+def with_code(high, code):
+    return high + high * ((code - 1.5) / 512.0)
+
+
+def split_codes(packed):
+    codes = []
+    for place in (64.0, 16.0, 4.0):
+        codes.insert(0, jnp.floor(packed / place))
+        packed = packed - place * codes[0]
+    return [packed] + codes
 
 
 def mean(x):
@@ -87,41 +104,65 @@
     return mixed_tan, q_tan, k_tan, v_tan
 
 
+def copies_kernel(patches, cotangent, out):
+    both = jnp.concatenate([patches[...].astype(F32), cotangent[...].astype(F32)], axis=0)
+    for at in range(out.shape[0]):
+        out[at] = both.astype(BF16)
+
+
 def sums_kernel(rows, cots, rows_b, cots_b, w_rows, w_cots, w_rows_b, w_cots_b, out):
     front = dot(rows[...], w_rows[...], NN) + dot(rows_b[...], w_rows_b[...], NN)
     back = dot(cots[...], w_cots[...], NT) + dot(cots_b[...], w_cots_b[...], NT)
     hidden = (w_rows.shape[1] - 3 * HD) // 2
-    high, low = halves(front[:, :HD])
-    out[:, :HD] = high
-    out[:, HD : 2 * HD] = low
-    out[:, 2 * HD : 4 * HD] = front[:, HD : 3 * HD].astype(BF16)
-    out[:, 4 * HD : 5 * HD] = back[:, :HD].astype(BF16)
+    blocks = [front[:, at * HD : (at + 1) * HD] for at in range(3)] + [back[:, :HD]]
+    packed = 0.0
+    for at, block in enumerate(blocks):
+        high = block.astype(BF16)
+        out[:, at * HD : (at + 1) * HD] = high
+        packed = packed + low_code(block, high.astype(F32)) * 4.0**at
+    out[:, 4 * HD : 5 * HD] = packed.astype(BF16)
     out[:, 5 * HD : 5 * HD + 2 * hidden] = front[:, 3 * HD :].astype(BF16)
     out[:, 5 * HD + 2 * hidden :] = back[:, HD:].astype(BF16)
 
 
-def results_kernel(core, mine, theirs, rows, cots, qkv_out, out_out, up_out, down_out):
+def results_kernel(
+    core, mine, theirs, rows, cots, qkv_out, out_out, up_out, down_out, qkv, out, up, down, sems
+):
     first = core[0] == 0
     zero = jnp.where(first, mine[...], theirs[...])
     one = jnp.where(first, theirs[...], mine[...])
-
-    def wide(x, at):
-        return x[:, at * HD : (at + 1) * HD].astype(F32) + x[:, (at + 4) * HD : (at + 5) * HD].astype(F32)
-
-    q, v, tq, cot = (wide(zero, at) for at in range(4))
-    k, tk, tv, cot_tan = (wide(one, at) for at in range(4))
-    mixed, q_tan, k_tan, v_tan = attention(q, k, v, tq, tk, tv, cot, cot_tan)
     rows_all, cots_all = rows[...], cots[...]
-    hidden = (zero.shape[1] - 8 * HD) // 2
+    hidden = (zero.shape[1] - 5 * HD) // 2
     for at, part in enumerate((zero, one)):
         place = slice(at * hidden, (at + 1) * hidden)
-        act = part[:, 8 * HD : 8 * HD + hidden]
-        hid = part[:, 8 * HD + hidden :]
-        up_out[:, place] = dot(rows_all, hid, TN).astype(BF16)
-        down_out[place, :] = dot(act, cots_all, TN).astype(BF16)
+        act = part[:, 5 * HD : 5 * HD + hidden]
+        hid = part[:, 5 * HD + hidden :]
+        up[:, place] = dot(rows_all, hid, TN).astype(BF16)
+        down[place, :] = dot(act, cots_all, TN).astype(BF16)
+    up_copy = pltpu.make_async_copy(up, up_out, sems.at[0])
+    down_copy = pltpu.make_async_copy(down, down_out, sems.at[1])
+    up_copy.start()
+    down_copy.start()
+
+    def blocks(part):
+        codes = split_codes(part[:, 4 * HD : 5 * HD].astype(F32))
+        highs = [part[:, at * HD : (at + 1) * HD].astype(F32) for at in range(4)]
+        return [with_code(high, code) for high, code in zip(highs, codes)]
+
+    q, v, tq, cot = blocks(zero)
+    k, tk, tv, cot_tan = blocks(one)
+    mixed, q_tan, k_tan, v_tan = attention(q, k, v, tq, tk, tv, cot, cot_tan)
     for at, part in enumerate((q_tan, k_tan, v_tan)):
-        qkv_out[at] = dot(rows_all, part.astype(BF16), TN).astype(BF16)
-    out_out[...] = dot(mixed.astype(BF16), cots_all, TN).astype(BF16)
+        qkv[at] = dot(rows_all, part.astype(BF16), TN).astype(BF16)
+    out[...] = dot(mixed.astype(BF16), cots_all, TN).astype(BF16)
+    qkv_copy = pltpu.make_async_copy(qkv, qkv_out, sems.at[2])
+    out_copy = pltpu.make_async_copy(out, out_out, sems.at[3])
+    qkv_copy.start()
+    out_copy.start()
+    up_copy.wait()
+    down_copy.wait()
+    qkv_copy.wait()
+    out_copy.wait()
 
 
 def hidden_pair(pre, cot_in):
@@ -141,8 +182,15 @@
     count = patches.shape[0] * long
     share = count // chips
 
-    both = jnp.stack([patches, cotangent])
-    gathered = lax.all_to_all(jnp.broadcast_to(both, (long,) + both.shape), "my", 0, 0, tiled=True)
+    own_rows = patches.shape[0]
+    copies = pl.pallas_call(
+        copies_kernel,
+        out_shape=jax.ShapeDtypeStruct((long, 2 * own_rows, width), BF16),
+        in_specs=[VMEM] * 2,
+        out_specs=VMEM,
+        name="copies",
+    )(patches, cotangent)
+    gathered = lax.all_to_all(copies, "my", 0, 0, tiled=True)
     swapped = lax.ppermute(gathered, "mx", swap)
 
     def pick(at):
@@ -157,7 +205,7 @@
     lent = pick(1 - core)
     taken = tuple(lax.ppermute(a, "mx", swap) for a in lent)
 
-    flat = lambda a, at: a[:, at].reshape(count, width)
+    flat = lambda a, at: a[:, at * own_rows : (at + 1) * own_rows].reshape(count, width)
     rows, cots = flat(gathered, 0), flat(gathered, 1)
     columns = 5 * HD + 4 * hidden
     message = pl.pallas_call(
@@ -171,12 +219,16 @@
     parts = lax.all_to_all(
         message.reshape(chips, share, columns), "mx", 0, 0, tiled=True, axis_index_groups=ring
     )
-    sums = jnp.sum(parts.astype(F32), axis=0)
-    attn = jnp.concatenate([sums[:, :HD] + sums[:, HD : 2 * HD], sums[:, 2 * HD : 5 * HD]], axis=1)
-    pre_hidden, tan_hidden, cot_act, tan_act = jnp.split(sums[:, 5 * HD :], 4, axis=1)
+    wide_parts = parts.astype(F32)
+    block = lambda a, at: a[..., at * HD : (at + 1) * HD]
+    codes = split_codes(block(wide_parts, 4))
+    sums = [jnp.sum(with_code(block(wide_parts, at), codes[at]), axis=0) for at in range(4)]
+    highs = [lax.reduce_precision(a, 8, 7) for a in sums]
+    packed = sum(low_code(a, high) * 4.0**at for at, (a, high) in enumerate(zip(sums, highs)))
+    hidden_sums = jnp.sum(wide_parts[..., 5 * HD :], axis=0)
+    pre_hidden, tan_hidden, cot_act, tan_act = jnp.split(hidden_sums, 4, axis=1)
     hid_tan = jax.jvp(hidden_pair, (pre_hidden, cot_act), (tan_hidden, tan_act))[1]
-    attn_high = lax.reduce_precision(attn, 8, 7)
-    reply = jnp.concatenate([attn_high, attn - attn_high, hid_tan[0], hid_tan[1]], axis=1).astype(BF16)
+    reply = jnp.concatenate(highs + [packed, hid_tan[0], hid_tan[1]], axis=1).astype(BF16)
     mine = lax.all_to_all(
         jnp.broadcast_to(reply, (chips,) + reply.shape),
         "mx",
@@ -186,16 +238,14 @@
         axis_index_groups=ring,
     ).reshape(count, -1)
     theirs = lax.ppermute(mine, "mx", swap)
+    shapes = ((3, width, HD), w_out.shape, w_up.shape, w_down.shape)
     hvp_qkv, hvp_out, hvp_up, hvp_down = pl.pallas_call(
         results_kernel,
-        out_shape=(
-            jax.ShapeDtypeStruct((3, width, HD), BF16),
-            jax.ShapeDtypeStruct(w_out.shape, BF16),
-            jax.ShapeDtypeStruct(w_up.shape, BF16),
-            jax.ShapeDtypeStruct(w_down.shape, BF16),
-        ),
+        out_shape=tuple(jax.ShapeDtypeStruct(shape, BF16) for shape in shapes),
         in_specs=[SMEM] + [VMEM] * 4,
-        out_specs=(VMEM,) * 4,
+        out_specs=(pl.BlockSpec(memory_space=pl.ANY),) * 4,
+        scratch_shapes=[pltpu.VMEM(shape, BF16) for shape in shapes]
+        + [pltpu.SemaphoreType.DMA((4,))],
         compiler_params=pltpu.CompilerParams(vmem_limit_bytes=48 * 2**20),
         name="results",
     )(core.reshape(1).astype(jnp.int32), mine, theirs, rows, cots)

time: 111 us -> 107 us (0.964)
  blocking collectives: 63 us -> 58.4 us
  Pallas kernels: 5.7 us -> 7.42 us
  waiting for transfers between devices: 7.35 us -> 6.09 us
    all_to_all x1, blocking collectives: 26.8 us -> 22.1 us  [body(): lax.all_to_all(jnp.broadcast_to(reply, (chips,) + reply.shape), 'mx', 0,...]
    pallas_call x1 -> x2, Pallas kernels: 4.32 us -> 6.04 us  [the longest x1 4.45 us: body(): pl.pallas_call(results_kernel, out_shape=tuple((jax.ShapeDtypeStruct(shap...]
    squeeze x1, local copies, waits for them, and re-layouts: 0.04 us -> 1.17 us  [pick(): zero = jnp.concatenate([w_qkv[:, 0], w_qkv[:, 2], dir_qkv[:, 0]], axis=1)]
  transfers between devices with their start and end apart: 5 -> 5, of which waited for: 3 -> 3; matrix products, arithmetic and copies ran while one was open for 2% -> 4% of each run, Pallas kernels for 0% -> 0%
where the time goes in v3:
time: 107 us; the launch traced here: 106 us
  blocking collectives  58.4 us (55%)
  starting transfers between devices  29 us (27%)
  Pallas kernels  7.42 us (7%)
  waiting for transfers between devices  6.09 us (6%)
  other arithmetic  2.85 us (3%)
  local copies, waits for them, and re-layouts  1.61 us (2%)
    all_to_all x1, blocking collectives, body(): lax.all_to_all(message.reshape(chips, share, columns), 'mx', 0, 0, tiled=...  36.3 us
    all_to_all x1, blocking collectives, body(): lax.all_to_all(jnp.broadcast_to(reply, (chips,) + reply.shape), 'mx', 0,...  22.1 us
    all_to_all x1, starting transfers between devices, body(): gathered = lax.all_to_all(copies, 'my', 0, 0, tiled=True)  13.7 us
    ppermute x1, starting transfers between devices, body(): swapped = lax.ppermute(gathered, 'mx', swap)  5.73 us
    ppermute x1, starting transfers between devices, body(): theirs = lax.ppermute(mine, 'mx', swap)  4.83 us
    ppermute x2, starting transfers between devices, body(): taken = tuple((lax.ppermute(a, 'mx', swap) for a in lent))  4.76 us
    pallas_call x1, Pallas kernels, body(): pl.pallas_call(results_kernel, out_shape=tuple((jax.ShapeDtypeStruct(shap...  4.45 us
    all_to_all x1, waiting for transfers between devices, body(): gathered = lax.all_to_all(copies, 'my', 0, 0, tiled=True)  3.18 us
  transfers between devices with their start and end apart: 5, of which 3 were waited for; matrix products, arithmetic and copies ran while one was open for 4% of the time, Pallas kernels for 0%

profile of v3, /device:TPU:1, one launch (start us, length us, event | category | flops | bytes accessed | tf_op | source)
XLA Modules:
  0.0 106.3 jit_solution(8301210080383261008)
XLA Ops:
  0.6 0.0 copy-start
  0.6 0.0 copy-start.1
  0.7 1.6 %copies.1 = bf16[32,16,384]{2,1,0:T(8,128)(2,1)} custom-call(bf16[8,384]{1,0:T(8,128)(2,1)} %patches.1, bf16[8,384]{1,0:T(8,128)(2,1)} %cotangent.1), custom_call_target="tpu_custom_call" | custom-call | tf_op jit(solution)/shard_map/copies/pallas_call | solution.py:186
  2.2 13.7 %all-to-all-start = ((bf16[32,16,384]{2,1,0:T(8,128)(2,1)}), bf16[32,16,384]{2,1,0:T(8,128)(2,1)S(1)}, u32[]{:S(2)}, u32[]{:S(2)}) async-start(bf16[32,16,384]{2,1,0:T(8,128)(2,1)} %copies.1), calls=%async_computation | async-start | bytes 786432 | tf_op jit(solution)/shard_map/all_to_all | solution.py:193
  16.0 1.2 %slice_bitcast_fusion.7 = (bf16[384,128]{1,0:T(8,128)(2,1)S(1)}, bf16[384,128]{1,0:T(8,128)(2,1)S(1)}, bf16[384,128]{1,0:T(8,128)(2,1)S(1)}, bf16[384,128]{1,0:T...) fusion(bf16[384,3,128]{2,0,1:T(8,128)(2,1)} %param.16, bf16[384,3,128]{2,0,1:T(8,128)(2,1)} %param.12), kind=kLoop, calls=%fused_computation.29 | loop fusion | bytes 1179648 | tf_op jit(solution)/shard_map/squeeze | solution.py:197
  17.2 0.0 copy-done
  17.2 0.0 copy-done.1
  17.2 0.1 constant_dynamic-slice_fusion.2
  17.3 0.0 copy-start.2
  17.3 0.0 copy-start.3
  17.3 0.2 broadcast_select_fusion
  17.5 0.0 copy-start.4
  17.5 0.0 copy-start.5
  17.5 1.0 pad_maximum_fusion.1
  18.5 2.9 %collective-permute-start.1 = (bf16[384,1152]{1,0:T(8,128)(2,1)}, bf16[384,1152]{1,0:T(8,128)(2,1)S(1)}, u32[]{:S(2)}, u32[]{:S(2)}) collective-permute-start(bf16[384,1152]{1,0:T(8,128)(2,1)} %pad_maximum_fusion.1), channel_id=1, source_target_pairs={{0,32},{32,0},{64,96},{96,64},{128,160},{160,128},{192,224},{224,1... | collective-permute-start | bytes 2654216 | tf_op jit(solution)/shard_map/ppermute | solution.py:206
  21.4 0.0 copy-done.2
  21.4 0.0 copy-done.3
  21.4 0.1 constant_dynamic-slice_fusion
  21.5 0.0 copy-done.4
  21.5 0.0 copy-done.5
  21.6 0.9 pad_maximum_fusion.3
  22.5 1.9 %collective-permute-start.2 = (bf16[896,384]{1,0:T(8,128)(2,1)}, bf16[896,384]{1,0:T(8,128)(2,1)S(1)}, u32[]{:S(2)}, u32[]{:S(2)}) collective-permute-start(bf16[896,384]{1,0:T(8,128)(2,1)} %pad_maximum_fusion.3), channel_id=1, source_target_pairs={{0,32},{32,0},{64,96},{96,64},{128,160},{160,128},{192,224},{224,1... | collective-permute-start | bytes 2064392 | tf_op jit(solution)/shard_map/ppermute | solution.py:206
  24.4 3.2 %all-to-all-done = bf16[32,16,384]{2,1,0:T(8,128)(2,1)S(1)} async-done(((bf16[32,16,384]{2,1,0:T(8,128)(2,1)}), bf16[32,16,384]{2,1,0:T(8,128)(2,1)S(1)}, u32[]{:S(2)}, u32[]{:S(2)}) %all-to-all-start) | async-done | bytes 393248 | tf_op jit(solution)/shard_map/all_to_all | solution.py:193
  27.6 5.7 %collective-permute-start = (bf16[32,16,384]{2,1,0:T(8,128)(2,1)S(1)}, bf16[32,16,384]{2,1,0:T(8,128)(2,1)S(1)}, u32[]{:S(2)}, u32[]{:S(2)}) collective-permute-start(bf16[32,16,384]{2,1,0:T(8,128)(2,1)S(1)} %all-to-all-done), channel_id=1, source_target_pairs={{0,32},{32,0},{64,96},{96,64},{128,160},{160,128},{192,224},{224,1... | collective-permute-start | bytes 1179656 | tf_op jit(solution)/shard_map/ppermute | solution.py:194
  33.3 0.1 pad_maximum_fusion.w_rows
  33.4 0.1 pad_maximum_fusion.2.w_cots
  33.6 1.1 %collective-permute-done = bf16[32,16,384]{2,1,0:T(8,128)(2,1)S(1)} collective-permute-done((bf16[32,16,384]{2,1,0:T(8,128)(2,1)S(1)}, bf16[32,16,384]{2,1,0:T(8,128)(2,1)S(1)}, u32[]{:S(2)}, u32[]{:S(2)}) %collective-permute-start) | collective-permute-done | bytes 393248 | tf_op jit(solution)/shard_map/ppermute | solution.py:194
  34.7 0.0 collective-permute-done.2.w_cots_b
  34.7 0.0 collective-permute-done.1.w_rows_b
  34.7 1.4 %sums.1 = bf16[256,2176]{1,0:T(8,128)(2,1)S(1)} custom-call(bf16[256,384]{1,0:T(8,128)(2,1)S(1)} %get-tuple-element.29.rows, bf16[256,384]{1,0:T(8,128)(2,1)S(1)} %get-tuple-element.28.cots, bf16[256,384]{1,0:T(8,128)(2,1)S(1)} %get-tuple-element.27.rows_b, bf16[256,384]{1,0:T(8,128)(2,1)S(1)} %get-tuple-element.26.cots_b, ...), custom_call_target="tpu_custom_call" | custom-call | tf_op jit(solution)/shard_map/sums/pallas_call | solution.py:211
  36.1 36.3 %all_to_all.15 = bf16[8,32,2176]{2,1,0:T(8,128)(2,1)S(1)} all-to-all(bf16[8,32,2176]{2,1,0:T(8,128)(2,1)S(1)} %bitcast.24), channel_id=1, replica_groups={{0,64,128,192,256,320,384,448},{32,96,160,224,288,352,416,480},{1,65,12..., dimensions={0} | all-to-all | bytes 2228224 | tf_op jit(solution)/shard_map/all_to_all | solution.py:219
  72.4 0.2 convert_element_type.4
  72.5 0.1 fusion.3
  72.7 0.1 slice_reduce_fusion
  72.9 0.1 fusion.9
  72.9 0.1 fusion.10
  73.0 0.1 broadcast_in_dim.11
  73.1 22.1 %all_to_all.16 = bf16[8,32,1408]{2,1,0:T(8,128)(2,1)S(1)} all-to-all(bf16[8,32,1408]{2,1,0:T(8,128)(2,1)S(1)} %broadcast_in_dim.11), channel_id=1, replica_groups={{0,64,128,192,256,320,384,448},{32,96,160,224,288,352,416,480},{1,65,12..., dimensions={0} | all-to-all | bytes 1441792 | tf_op jit(solution)/shard_map/all_to_all | solution.py:232
  95.2 4.8 %collective-permute-start.3 = (bf16[256,1408]{1,0:T(8,128)(2,1)S(1)}, bf16[256,1408]{1,0:T(8,128)(2,1)S(1)}, u32[]{:S(2)}, u32[]{:S(2)}) collective-permute-start(bf16[256,1408]{1,0:T(8,128)(2,1)S(1)} %bitcast.25), channel_id=1, source_target_pairs={{0,32},{32,0},{64,96},{96,64},{128,160},{160,128},{192,224},{224,1... | collective-permute-start | bytes 2162696 | tf_op jit(solution)/shard_map/ppermute | solution.py:240
  100.0 1.8 %collective-permute-done.3.theirs = bf16[256,1408]{1,0:T(8,128)(2,1)S(1)} collective-permute-done((bf16[256,1408]{1,0:T(8,128)(2,1)S(1)}, bf16[256,1408]{1,0:T(8,128)(2,1)S(1)}, u32[]{:S(2)}, u32[]{:S(2)}) %collective-permute-start.3) | collective-permute-done | bytes 720928 | tf_op jit(solution)/shard_map/ppermute | solution.py:240
  101.8 4.5 %results.1 = (bf16[3,384,128]{2,1,0:T(8,128)(2,1)}, bf16[128,384]{1,0:T(8,128)(2,1)}, bf16[384,768]{1,0:T(8,128)(2,1)}, bf16[768,384]{1,0:T(8,128)(2,1)}) custom-call(s32[1]{0:T(128)} %bitcast.core, bf16[256,1408]{1,0:T(8,128)(2,1)S(1)} %bitcast.26, bf16[256,1408]{1,0:T(8,128)(2,1)S(1)} %collective-permute-done.3.theirs, ...), custom_call_target="tpu_custom_call" | custom-call | tf_op jit(solution)/shard_map/results/pallas_call | solution.py:242
  (8 shorter events, 0.2 us)
Async XLA Ops:
  0.6 16.5 %copy-start = (bf16[384,768]{1,0:T(8,128)(2,1)S(1)}, bf16[384,768]{1,0:T(8,128)(2,1)}, u32[]{:S(2)}) copy-start(bf16[384,768]{1,0:T(8,128)(2,1)} %param.18) | copy-start | bytes 1769476
  0.6 16.5 %copy-start.1 = (bf16[384,768]{1,0:T(8,128)(2,1)S(1)}, bf16[384,768]{1,0:T(8,128)(2,1)}, u32[]{:S(2)}) copy-start(bf16[384,768]{1,0:T(8,128)(2,1)} %param.14) | copy-start | bytes 1769476
  2.2 25.4 %all-to-all-start = ((bf16[32,16,384]{2,1,0:T(8,128)(2,1)}), bf16[32,16,384]{2,1,0:T(8,128)(2,1)S(1)}, u32[]{:S(2)}, u32[]{:S(2)}) async-start(bf16[32,16,384]{2,1,0:T(8,128)(2,1)} %copies.1), calls=%async_computation | async-start | bytes 786432 | tf_op jit(solution)/shard_map/all_to_all | solution.py:193
  17.3 4.1 %copy-start.2 = (bf16[768,384]{1,0:T(8,128)(2,1)S(1)}, bf16[768,384]{1,0:T(8,128)(2,1)}, u32[]{:S(2)}) copy-start(bf16[768,384]{1,0:T(8,128)(2,1)} %param.19) | copy-start | bytes 1769476
  17.3 4.1 %copy-start.3 = (bf16[768,384]{1,0:T(8,128)(2,1)S(1)}, bf16[768,384]{1,0:T(8,128)(2,1)}, u32[]{:S(2)}) copy-start(bf16[768,384]{1,0:T(8,128)(2,1)} %param.15) | copy-start | bytes 1769476
  17.5 4.0 %copy-start.4 = (bf16[128,384]{1,0:T(8,128)(2,1)S(1)}, bf16[128,384]{1,0:T(8,128)(2,1)}, u32[]{:S(2)}) copy-start(bf16[128,384]{1,0:T(8,128)(2,1)} %param.13) | copy-start | bytes 294916
  17.5 4.0 %copy-start.5 = (bf16[128,384]{1,0:T(8,128)(2,1)S(1)}, bf16[128,384]{1,0:T(8,128)(2,1)}, u32[]{:S(2)}) copy-start(bf16[128,384]{1,0:T(8,128)(2,1)} %param.17) | copy-start | bytes 294916
  18.5 16.2 %collective-permute-start.1 = (bf16[384,1152]{1,0:T(8,128)(2,1)}, bf16[384,1152]{1,0:T(8,128)(2,1)S(1)}, u32[]{:S(2)}, u32[]{:S(2)}) collective-permute-start(bf16[384,1152]{1,0:T(8,128)(2,1)} %pad_maximum_fusion.1), channel_id=1, source_target_pairs={{0,32},{32,0},{64,96},{96,64},{128,160},{160,128},{192,224},{224,1... | collective-permute-start | bytes 2654216 | tf_op jit(solution)/shard_map/ppermute | solution.py:206
  22.5 12.2 %collective-permute-start.2 = (bf16[896,384]{1,0:T(8,128)(2,1)}, bf16[896,384]{1,0:T(8,128)(2,1)S(1)}, u32[]{:S(2)}, u32[]{:S(2)}) collective-permute-start(bf16[896,384]{1,0:T(8,128)(2,1)} %pad_maximum_fusion.3), channel_id=1, source_target_pairs={{0,32},{32,0},{64,96},{96,64},{128,160},{160,128},{192,224},{224,1... | collective-permute-start | bytes 2064392 | tf_op jit(solution)/shard_map/ppermute | solution.py:206
  27.6 7.1 %collective-permute-start = (bf16[32,16,384]{2,1,0:T(8,128)(2,1)S(1)}, bf16[32,16,384]{2,1,0:T(8,128)(2,1)S(1)}, u32[]{:S(2)}, u32[]{:S(2)}) collective-permute-start(bf16[32,16,384]{2,1,0:T(8,128)(2,1)S(1)} %all-to-all-done), channel_id=1, source_target_pairs={{0,32},{32,0},{64,96},{96,64},{128,160},{160,128},{192,224},{224,1... | collective-permute-start | bytes 1179656 | tf_op jit(solution)/shard_map/ppermute | solution.py:194
  95.2 6.6 %collective-permute-start.3 = (bf16[256,1408]{1,0:T(8,128)(2,1)S(1)}, bf16[256,1408]{1,0:T(8,128)(2,1)S(1)}, u32[]{:S(2)}, u32[]{:S(2)}) collective-permute-start(bf16[256,1408]{1,0:T(8,128)(2,1)S(1)} %bitcast.25), channel_id=1, source_target_pairs={{0,32},{32,0},{64,96},{96,64},{128,160},{160,128},{192,224},{224,1... | collective-permute-start | bytes 2162696 | tf_op jit(solution)/shard_map/ppermute | solution.py:240

commit v4 on v3

--- a/solution.py
+++ b/solution.py
@@ -27,9 +27,11 @@
     return high, (x - high.astype(F32)).astype(BF16)
 
 
-def dot3(left, right, dims):
-    return (
-        dot(left[0], right[0], dims) + dot(left[0], right[1], dims) + dot(left[1], right[0], dims)
+def product(pairs, dims):
+    left = [part for (high, low), _ in pairs for part in (high, high, low)]
+    right = [part for _, (high, low) in pairs for part in (high, low, high)]
+    return dot(
+        jnp.concatenate(left, axis=dims[0][0]), jnp.concatenate(right, axis=dims[1][0]), dims
     )
 
 
@@ -83,36 +85,35 @@
     kn, dkn, k_inverse, k_shift = normalize(k, tk)
     qs, dqs, ks, dks = halves(qn * scale), halves(dqn * scale), halves(kn), halves(dkn)
     vs, dvs, cs, dcs = halves(v), halves(tv), halves(cot), halves(cot_tan)
-    raised = jnp.exp(dot3(qs, ks, NT))
+    raised = jnp.exp(product([(qs, ks)], NT))
     probs = raised / total(raised)
-    score_tan = dot3(dqs, ks, NT) + dot3(qs, dks, NT)
+    score_tan = product([(dqs, ks), (qs, dks)], NT)
     probs_tan = probs * (score_tan - total(probs * score_tan))
     ps, dps = halves(probs), halves(probs_tan)
-    mixed_tan = dot3(dps, vs, NN) + dot3(ps, dvs, NN)
-    v_tan = dot3(dps, cs, TN) + dot3(ps, dcs, TN)
-    cot_probs = dot3(cs, vs, NT)
-    cot_probs_tan = dot3(dcs, vs, NT) + dot3(cs, dvs, NT)
+    mixed_tan = product([(dps, vs), (ps, dvs)], NN)
+    v_tan = product([(dps, cs), (ps, dcs)], TN)
+    cot_probs = product([(cs, vs)], NT)
+    cot_probs_tan = product([(dcs, vs), (cs, dvs)], NT)
     away = cot_probs - total(probs * cot_probs)
     away_tan = cot_probs_tan - total(probs_tan * cot_probs + probs * cot_probs_tan)
     ss, dss = halves(probs * away), halves(probs_tan * away + probs * away_tan)
-    q_cot = scale * dot3(ss, ks, NN)
-    q_cot_tan = scale * (dot3(dss, ks, NN) + dot3(ss, dks, NN))
-    k_cot = dot3(ss, qs, TN)
-    k_cot_tan = dot3(dss, qs, TN) + dot3(ss, dqs, TN)
+    q_cot = scale * product([(ss, ks)], NN)
+    q_cot_tan = scale * product([(dss, ks), (ss, dks)], NN)
+    k_cot = product([(ss, qs)], TN)
+    k_cot_tan = product([(dss, qs), (ss, dqs)], TN)
     q_tan = normalize_back(qn, dqn, q_inverse, q_shift, q_cot, q_cot_tan)
     k_tan = normalize_back(kn, dkn, k_inverse, k_shift, k_cot, k_cot_tan)
     return mixed_tan, q_tan, k_tan, v_tan
 
 
-def copies_kernel(patches, cotangent, out):
-    both = jnp.concatenate([patches[...].astype(F32), cotangent[...].astype(F32)], axis=0)
-    for at in range(out.shape[0]):
-        out[at] = both.astype(BF16)
-
-
-def sums_kernel(rows, cots, rows_b, cots_b, w_rows, w_cots, w_rows_b, w_cots_b, out):
-    front = dot(rows[...], w_rows[...], NN) + dot(rows_b[...], w_rows_b[...], NN)
-    back = dot(cots[...], w_cots[...], NT) + dot(cots_b[...], w_cots_b[...], NT)
+def own_sums_kernel(rows, cots, w_rows, w_cots, front, back):
+    front[...] = dot(rows[...], w_rows[...], NN)
+    back[...] = dot(cots[...], w_cots[...], NT)
+
+
+def sums_kernel(front_a, back_a, rows, cots, w_rows, w_cots, out):
+    front = front_a[...] + dot(rows[...], w_rows[...], NN)
+    back = back_a[...] + dot(cots[...], w_cots[...], NT)
     hidden = (w_rows.shape[1] - 3 * HD) // 2
     blocks = [front[:, at * HD : (at + 1) * HD] for at in range(3)] + [back[:, :HD]]
     packed = 0.0
@@ -125,24 +126,36 @@
     out[:, 5 * HD + 2 * hidden :] = back[:, HD:].astype(BF16)
 
 
+def hidden_products(part, rows, cots):
+    hidden = (part.shape[1] - 5 * HD) // 2
+    act = part[:, 5 * HD : 5 * HD + hidden]
+    hid = part[:, 5 * HD + hidden :]
+    return dot(rows, hid, TN).astype(BF16), dot(act, cots, TN).astype(BF16)
+
+
+def own_products_kernel(mine, rows, cots, up, down):
+    up[...], down[...] = hidden_products(mine[...], rows[...], cots[...])
+
+
 def results_kernel(
-    core, mine, theirs, rows, cots, qkv_out, out_out, up_out, down_out, qkv, out, up, down, sems
+    core, mine, theirs, rows, cots, own_up, own_down,
+    qkv_out, out_out, up_out, down_out,
+    qkv, out, up, down, sems,
 ):
     first = core[0] == 0
-    zero = jnp.where(first, mine[...], theirs[...])
-    one = jnp.where(first, theirs[...], mine[...])
     rows_all, cots_all = rows[...], cots[...]
-    hidden = (zero.shape[1] - 5 * HD) // 2
-    for at, part in enumerate((zero, one)):
-        place = slice(at * hidden, (at + 1) * hidden)
-        act = part[:, 5 * HD : 5 * HD + hidden]
-        hid = part[:, 5 * HD + hidden :]
-        up[:, place] = dot(rows_all, hid, TN).astype(BF16)
-        down[place, :] = dot(act, cots_all, TN).astype(BF16)
+    other_up, other_down = hidden_products(theirs[...], rows_all, cots_all)
+    hidden = other_down.shape[0]
+    up[:, :hidden] = jnp.where(first, own_up[...], other_up)
+    up[:, hidden:] = jnp.where(first, other_up, own_up[...])
+    down[:hidden, :] = jnp.where(first, own_down[...], other_down)
+    down[hidden:, :] = jnp.where(first, other_down, own_down[...])
     up_copy = pltpu.make_async_copy(up, up_out, sems.at[0])
     down_copy = pltpu.make_async_copy(down, down_out, sems.at[1])
     up_copy.start()
     down_copy.start()
+    zero = jnp.where(first, mine[:, : 5 * HD], theirs[:, : 5 * HD])
+    one = jnp.where(first, theirs[:, : 5 * HD], mine[:, : 5 * HD])
 
     def blocks(part):
         codes = split_codes(part[:, 4 * HD : 5 * HD].astype(F32))
@@ -183,13 +196,12 @@
     share = count // chips
 
     own_rows = patches.shape[0]
-    copies = pl.pallas_call(
-        copies_kernel,
-        out_shape=jax.ShapeDtypeStruct((long, 2 * own_rows, width), BF16),
-        in_specs=[VMEM] * 2,
-        out_specs=VMEM,
-        name="copies",
-    )(patches, cotangent)
+    copy_shape = (long, 2, own_rows, width)
+    copies = jnp.where(
+        lax.broadcasted_iota(jnp.int32, copy_shape, 1) == 0,
+        jnp.broadcast_to(patches, copy_shape),
+        jnp.broadcast_to(cotangent, copy_shape),
+    )
     gathered = lax.all_to_all(copies, "my", 0, 0, tiled=True)
     swapped = lax.ppermute(gathered, "mx", swap)
 
@@ -205,17 +217,34 @@
     lent = pick(1 - core)
     taken = tuple(lax.ppermute(a, "mx", swap) for a in lent)
 
-    flat = lambda a, at: a[:, at * own_rows : (at + 1) * own_rows].reshape(count, width)
+    flat = lambda a, at: a[:, at].reshape(count, width)
     rows, cots = flat(gathered, 0), flat(gathered, 1)
     columns = 5 * HD + 4 * hidden
+    widths = (3 * HD + 2 * hidden, HD + 2 * hidden)
+    room = pltpu.CompilerParams(vmem_limit_bytes=48 * 2**20)
+    sums_cost = pl.CostEstimate(
+        flops=2 * count * width * sum(widths),
+        bytes_accessed=2 * width * sum(widths) + 4 * count * sum(widths),
+        transcendentals=0,
+    )
+    own_sums = pl.pallas_call(
+        own_sums_kernel,
+        out_shape=tuple(jax.ShapeDtypeStruct((count, n), F32) for n in widths),
+        in_specs=[VMEM] * 4,
+        out_specs=(VMEM,) * 2,
+        compiler_params=room,
+        cost_estimate=sums_cost,
+        name="own_sums",
+    )(rows, cots, *kept)
     message = pl.pallas_call(
         sums_kernel,
         out_shape=jax.ShapeDtypeStruct((count, columns), BF16),
-        in_specs=[VMEM] * 8,
+        in_specs=[VMEM] * 6,
         out_specs=VMEM,
-        compiler_params=pltpu.CompilerParams(vmem_limit_bytes=48 * 2**20),
+        compiler_params=room,
+        cost_estimate=sums_cost,
         name="sums",
-    )(rows, cots, flat(swapped, 0), flat(swapped, 1), *kept, *taken)
+    )(*own_sums, flat(swapped, 0), flat(swapped, 1), *taken)
     parts = lax.all_to_all(
         message.reshape(chips, share, columns), "mx", 0, 0, tiled=True, axis_index_groups=ring
     )
@@ -238,17 +267,33 @@
         axis_index_groups=ring,
     ).reshape(count, -1)
     theirs = lax.ppermute(mine, "mx", swap)
+    own_products = pl.pallas_call(
+        own_products_kernel,
+        out_shape=(
+            jax.ShapeDtypeStruct((width, hidden), BF16),
+            jax.ShapeDtypeStruct((hidden, width), BF16),
+        ),
+        in_specs=[VMEM] * 3,
+        out_specs=(VMEM,) * 2,
+        compiler_params=room,
+        cost_estimate=pl.CostEstimate(
+            flops=4 * count * width * hidden,
+            bytes_accessed=4 * width * hidden + 8 * count * width,
+            transcendentals=0,
+        ),
+        name="own_products",
+    )(mine, rows, cots)
     shapes = ((3, width, HD), w_out.shape, w_up.shape, w_down.shape)
     hvp_qkv, hvp_out, hvp_up, hvp_down = pl.pallas_call(
         results_kernel,
         out_shape=tuple(jax.ShapeDtypeStruct(shape, BF16) for shape in shapes),
-        in_specs=[SMEM] + [VMEM] * 4,
+        in_specs=[SMEM] + [VMEM] * 6,
         out_specs=(pl.BlockSpec(memory_space=pl.ANY),) * 4,
         scratch_shapes=[pltpu.VMEM(shape, BF16) for shape in shapes]
         + [pltpu.SemaphoreType.DMA((4,))],
-        compiler_params=pltpu.CompilerParams(vmem_limit_bytes=48 * 2**20),
+        compiler_params=room,
         name="results",
-    )(core.reshape(1).astype(jnp.int32), mine, theirs, rows, cots)
+    )(core.reshape(1).astype(jnp.int32), mine, theirs, rows, cots, *own_products)
     return jnp.transpose(hvp_qkv, (1, 0, 2)), hvp_out, hvp_up, hvp_down
 
 

time: 107 us -> 106 us (level)
  other arithmetic: 2.85 us -> 4.53 us
  Pallas kernels: 7.42 us -> 5.85 us
  waiting for transfers between devices: 6.09 us -> 4.77 us
    select_n x0 -> x1, other arithmetic: none -> 1.65 us  [body(): jnp.where(lax.broadcasted_iota(jnp.int32, copy_shape, 1) == 0, jnp.broadc...]
  transfers between devices with their start and end apart: 5 -> 5, of which waited for: 3 -> 3; matrix products, arithmetic and copies ran while one was open for 4% -> 4% of each run, Pallas kernels for 0% -> 1%
where the time goes in v4:
time: 106 us; the launch traced here: 105 us
  blocking collectives  58.4 us (55%)
  starting transfers between devices  29.2 us (28%)
  Pallas kernels  5.85 us (6%)
  waiting for transfers between devices  4.77 us (4%)
  other arithmetic  4.53 us (4%)
  local copies, waits for them, and re-layouts  1.61 us (2%)
    all_to_all x1, blocking collectives, body(): lax.all_to_all(message.reshape(chips, share, columns), 'mx', 0, 0, tiled=...  36.2 us
    all_to_all x1, blocking collectives, body(): lax.all_to_all(jnp.broadcast_to(reply, (chips,) + reply.shape), 'mx', 0,...  22.1 us
    all_to_all x1, starting transfers between devices, body(): gathered = lax.all_to_all(copies, 'my', 0, 0, tiled=True)  13.7 us
    ppermute x1, starting transfers between devices, body(): swapped = lax.ppermute(gathered, 'mx', swap)  5.73 us
    ppermute x2, starting transfers between devices, body(): taken = tuple((lax.ppermute(a, 'mx', swap) for a in lent))  4.89 us
    ppermute x1, starting transfers between devices, body(): theirs = lax.ppermute(mine, 'mx', swap)  4.84 us
    pallas_call x1, Pallas kernels, body(): pl.pallas_call(results_kernel, out_shape=tuple((jax.ShapeDtypeStruct(shap...  3.9 us
    all_to_all x1, waiting for transfers between devices, body(): gathered = lax.all_to_all(copies, 'my', 0, 0, tiled=True)  2.95 us
  transfers between devices with their start and end apart: 5, of which 3 were waited for; matrix products, arithmetic and copies ran while one was open for 4% of the time, Pallas kernels for 1%

profile of v4, /device:TPU:1, one launch (start us, length us, event | category | flops | bytes accessed | tf_op | source)
XLA Modules:
  0.0 105.2 jit_solution(6375621003397960686)
XLA Ops:
  0.6 0.0 copy-start
  0.6 0.0 copy-start.1
  0.7 1.7 %broadcast_select_fusion = bf16[32,2,8,384]{3,2,1,0:T(8,128)(2,1)} fusion(pred[2]{0:T(512)(128)(4,1)S(1)} %iota_compare_fusion, bf16[8,384]{1,0:T(8,128)(2,1)} %param.11, bf16[8,384]{1,0:T(8,128)(2,1)} %param.10), kind=kLoop, calls=%fused_computation.5 | loop fusion | flops 196608 | bytes 405506 | tf_op jit(solution)/shard_map/jit(_where)/select_n | solution.py:200
  2.3 13.7 %all-to-all-start = ((bf16[32,2,8,384]{3,2,1,0:T(8,128)(2,1)}), bf16[32,2,8,384]{3,2,1,0:T(8,128)(2,1)S(1)}, u32[]{:S(2)}, u32[]{:S(2)}) async-start(bf16[32,2,8,384]{3,2,1,0:T(8,128)(2,1)} %broadcast_select_fusion), calls=%async_computation | async-start | bytes 786432 | tf_op jit(solution)/shard_map/all_to_all | solution.py:205
  16.1 1.2 %slice_bitcast_fusion.7 = (bf16[384,128]{1,0:T(8,128)(2,1)S(1)}, bf16[384,128]{1,0:T(8,128)(2,1)S(1)}, bf16[384,128]{1,0:T(8,128)(2,1)S(1)}, bf16[384,128]{1,0:T...) fusion(bf16[384,3,128]{2,0,1:T(8,128)(2,1)} %param.16, bf16[384,3,128]{2,0,1:T(8,128)(2,1)} %param.12), kind=kLoop, calls=%fused_computation.30 | loop fusion | bytes 1179648 | tf_op jit(solution)/shard_map/squeeze | solution.py:209
  17.2 0.0 copy-done
  17.2 0.0 copy-done.1
  17.3 0.1 constant_dynamic-slice_fusion.2
  17.4 0.0 copy-start.2
  17.4 0.0 copy-start.3
  17.4 0.2 broadcast_select_fusion.1
  17.6 1.0 pad_maximum_fusion.1
  18.6 0.0 copy-start.4
  18.6 0.0 copy-start.5
  18.6 3.0 %collective-permute-start.1 = (bf16[384,1152]{1,0:T(8,128)(2,1)}, bf16[384,1152]{1,0:T(8,128)(2,1)S(1)}, u32[]{:S(2)}, u32[]{:S(2)}) collective-permute-start(bf16[384,1152]{1,0:T(8,128)(2,1)} %pad_maximum_fusion.1), channel_id=1, source_target_pairs={{0,32},{32,0},{64,96},{96,64},{128,160},{160,128},{192,224},{224,1... | collective-permute-start | bytes 2654216 | tf_op jit(solution)/shard_map/ppermute | solution.py:218
  21.6 0.0 copy-done.2
  21.6 0.0 copy-done.3
  21.6 0.1 constant_dynamic-slice_fusion
  21.8 0.0 copy-done.4
  21.8 0.0 copy-done.5
  21.8 0.9 pad_maximum_fusion.3
  22.7 1.9 %collective-permute-start.2 = (bf16[896,384]{1,0:T(8,128)(2,1)}, bf16[896,384]{1,0:T(8,128)(2,1)S(1)}, u32[]{:S(2)}, u32[]{:S(2)}) collective-permute-start(bf16[896,384]{1,0:T(8,128)(2,1)} %pad_maximum_fusion.3), channel_id=1, source_target_pairs={{0,32},{32,0},{64,96},{96,64},{128,160},{160,128},{192,224},{224,1... | collective-permute-start | bytes 2064392 | tf_op jit(solution)/shard_map/ppermute | solution.py:218
  24.7 0.1 pad_maximum_fusion.w_rows
  24.7 2.9 %all-to-all-done = bf16[32,2,8,384]{3,2,1,0:T(8,128)(2,1)S(1)} async-done(((bf16[32,2,8,384]{3,2,1,0:T(8,128)(2,1)}), bf16[32,2,8,384]{3,2,1,0:T(8,128)(2,1)S(1)}, u32[]{:S(2)}, u32[]{:S(2)}) %all-to-all-start) | async-done | bytes 393248 | tf_op jit(solution)/shard_map/all_to_all | solution.py:205
  27.7 5.7 %collective-permute-start = (bf16[32,2,8,384]{3,2,1,0:T(8,128)(2,1)S(1)}, bf16[32,2,8,384]{3,2,1,0:T(8,128)(2,1)S(1)}, u32[]{:S(2)}, u32[]{:S(2)}) collective-permute-start(bf16[32,2,8,384]{3,2,1,0:T(8,128)(2,1)S(1)} %all-to-all-done), channel_id=1, source_target_pairs={{0,32},{32,0},{64,96},{96,64},{128,160},{160,128},{192,224},{224,1... | collective-permute-start | bytes 1179656 | tf_op jit(solution)/shard_map/ppermute | solution.py:206
  33.4 0.1 pad_maximum_fusion.2.w_cots
  33.6 0.8 own_sums.1
  34.3 0.4 collective-permute-done
  34.8 0.0 collective-permute-done.2.w_cots
  34.8 0.0 collective-permute-done.1.w_rows
  34.8 0.8 sums.1
  35.6 36.2 %all_to_all.15 = bf16[8,32,2176]{2,1,0:T(8,128)(2,1)S(1)} all-to-all(bf16[8,32,2176]{2,1,0:T(8,128)(2,1)S(1)} %bitcast.27), channel_id=1, replica_groups={{0,64,128,192,256,320,384,448},{32,96,160,224,288,352,416,480},{1,65,12..., dimensions={0} | all-to-all | bytes 2228224 | tf_op jit(solution)/shard_map/all_to_all | solution.py:248
  71.9 0.2 convert_element_type.4
  72.0 0.1 fusion.3
  72.2 0.1 slice_reduce_fusion
  72.4 0.1 fusion.9
  72.4 0.1 fusion.10
  72.5 0.1 broadcast_in_dim.19
  72.6 22.1 %all_to_all.16 = bf16[8,32,1408]{2,1,0:T(8,128)(2,1)S(1)} all-to-all(bf16[8,32,1408]{2,1,0:T(8,128)(2,1)S(1)} %broadcast_in_dim.19), channel_id=1, replica_groups={{0,64,128,192,256,320,384,448},{32,96,160,224,288,352,416,480},{1,65,12..., dimensions={0} | all-to-all | bytes 1441792 | tf_op jit(solution)/shard_map/all_to_all | solution.py:261
  94.7 4.8 %collective-permute-start.3 = (bf16[256,1408]{1,0:T(8,128)(2,1)S(1)}, bf16[256,1408]{1,0:T(8,128)(2,1)S(1)}, u32[]{:S(2)}, u32[]{:S(2)}) collective-permute-start(bf16[256,1408]{1,0:T(8,128)(2,1)S(1)} %bitcast.24), channel_id=1, source_target_pairs={{0,32},{32,0},{64,96},{96,64},{128,160},{160,128},{192,224},{224,1... | collective-permute-start | bytes 2162696 | tf_op jit(solution)/shard_map/ppermute | solution.py:269
  99.5 0.4 own_products.1
  99.9 1.4 %collective-permute-done.3.theirs = bf16[256,1408]{1,0:T(8,128)(2,1)S(1)} collective-permute-done((bf16[256,1408]{1,0:T(8,128)(2,1)S(1)}, bf16[256,1408]{1,0:T(8,128)(2,1)S(1)}, u32[]{:S(2)}, u32[]{:S(2)}) %collective-permute-start.3) | collective-permute-done | bytes 720928 | tf_op jit(solution)/shard_map/ppermute | solution.py:269
  101.3 3.9 %results.1 = (bf16[3,384,128]{2,1,0:T(8,128)(2,1)}, bf16[128,384]{1,0:T(8,128)(2,1)}, bf16[384,768]{1,0:T(8,128)(2,1)}, bf16[768,384]{1,0:T(8,128)(2,1)}) custom-call(s32[1]{0:T(128)} %bitcast.core, bf16[256,1408]{1,0:T(8,128)(2,1)S(1)} %bitcast.26, bf16[256,1408]{1,0:T(8,128)(2,1)S(1)} %collective-permute-done.3.theirs, ...), custom_call_target="tpu_custom_call" | custom-call | tf_op jit(solution)/shard_map/results/pallas_call | solution.py:287
  (9 shorter events, 0.2 us)
Async XLA Ops:
  0.6 16.6 %copy-start = (bf16[384,768]{1,0:T(8,128)(2,1)S(1)}, bf16[384,768]{1,0:T(8,128)(2,1)}, u32[]{:S(2)}) copy-start(bf16[384,768]{1,0:T(8,128)(2,1)} %param.18) | copy-start | bytes 1769476
  0.6 16.6 %copy-start.1 = (bf16[384,768]{1,0:T(8,128)(2,1)S(1)}, bf16[384,768]{1,0:T(8,128)(2,1)}, u32[]{:S(2)}) copy-start(bf16[384,768]{1,0:T(8,128)(2,1)} %param.14) | copy-start | bytes 1769476
  2.3 25.4 %all-to-all-start = ((bf16[32,2,8,384]{3,2,1,0:T(8,128)(2,1)}), bf16[32,2,8,384]{3,2,1,0:T(8,128)(2,1)S(1)}, u32[]{:S(2)}, u32[]{:S(2)}) async-start(bf16[32,2,8,384]{3,2,1,0:T(8,128)(2,1)} %broadcast_select_fusion), calls=%async_computation | async-start | bytes 786432 | tf_op jit(solution)/shard_map/all_to_all | solution.py:205
  17.4 4.2 %copy-start.2 = (bf16[768,384]{1,0:T(8,128)(2,1)S(1)}, bf16[768,384]{1,0:T(8,128)(2,1)}, u32[]{:S(2)}) copy-start(bf16[768,384]{1,0:T(8,128)(2,1)} %param.19) | copy-start | bytes 1769476
  17.4 4.2 %copy-start.3 = (bf16[768,384]{1,0:T(8,128)(2,1)S(1)}, bf16[768,384]{1,0:T(8,128)(2,1)}, u32[]{:S(2)}) copy-start(bf16[768,384]{1,0:T(8,128)(2,1)} %param.15) | copy-start | bytes 1769476
  18.6 3.2 %copy-start.4 = (bf16[128,384]{1,0:T(8,128)(2,1)S(1)}, bf16[128,384]{1,0:T(8,128)(2,1)}, u32[]{:S(2)}) copy-start(bf16[128,384]{1,0:T(8,128)(2,1)} %param.13) | copy-start | bytes 294916
  18.6 3.2 %copy-start.5 = (bf16[128,384]{1,0:T(8,128)(2,1)S(1)}, bf16[128,384]{1,0:T(8,128)(2,1)}, u32[]{:S(2)}) copy-start(bf16[128,384]{1,0:T(8,128)(2,1)} %param.17) | copy-start | bytes 294916
  18.6 16.2 %collective-permute-start.1 = (bf16[384,1152]{1,0:T(8,128)(2,1)}, bf16[384,1152]{1,0:T(8,128)(2,1)S(1)}, u32[]{:S(2)}, u32[]{:S(2)}) collective-permute-start(bf16[384,1152]{1,0:T(8,128)(2,1)} %pad_maximum_fusion.1), channel_id=1, source_target_pairs={{0,32},{32,0},{64,96},{96,64},{128,160},{160,128},{192,224},{224,1... | collective-permute-start | bytes 2654216 | tf_op jit(solution)/shard_map/ppermute | solution.py:218
  22.7 12.1 %collective-permute-start.2 = (bf16[896,384]{1,0:T(8,128)(2,1)}, bf16[896,384]{1,0:T(8,128)(2,1)S(1)}, u32[]{:S(2)}, u32[]{:S(2)}) collective-permute-start(bf16[896,384]{1,0:T(8,128)(2,1)} %pad_maximum_fusion.3), channel_id=1, source_target_pairs={{0,32},{32,0},{64,96},{96,64},{128,160},{160,128},{192,224},{224,1... | collective-permute-start | bytes 2064392 | tf_op jit(solution)/shard_map/ppermute | solution.py:218
  27.7 7.1 %collective-permute-start = (bf16[32,2,8,384]{3,2,1,0:T(8,128)(2,1)S(1)}, bf16[32,2,8,384]{3,2,1,0:T(8,128)(2,1)S(1)}, u32[]{:S(2)}, u32[]{:S(2)}) collective-permute-start(bf16[32,2,8,384]{3,2,1,0:T(8,128)(2,1)S(1)} %all-to-all-done), channel_id=1, source_target_pairs={{0,32},{32,0},{64,96},{96,64},{128,160},{160,128},{192,224},{224,1... | collective-permute-start | bytes 1179656 | tf_op jit(solution)/shard_map/ppermute | solution.py:206
  94.7 6.6 %collective-permute-start.3 = (bf16[256,1408]{1,0:T(8,128)(2,1)S(1)}, bf16[256,1408]{1,0:T(8,128)(2,1)S(1)}, u32[]{:S(2)}, u32[]{:S(2)}) collective-permute-start(bf16[256,1408]{1,0:T(8,128)(2,1)S(1)} %bitcast.24), channel_id=1, source_target_pairs={{0,32},{32,0},{64,96},{96,64},{128,160},{160,128},{192,224},{224,1... | collective-permute-start | bytes 2162696 | tf_op jit(solution)/shard_map/ppermute | solution.py:269

commit v5 on v4

v5 whole, which is shorter than its diff:
```python
import math

import jax
import jax.numpy as jnp
from jax import lax
from jax.experimental import pallas as pl
from jax.experimental.pallas import tpu as pltpu
from jax.sharding import PartitionSpec as P

HD = 128
F32 = jnp.float32
BF16 = jnp.bfloat16
VMEM = pl.BlockSpec(memory_space=pltpu.VMEM)
SMEM = pl.BlockSpec(memory_space=pltpu.SMEM)

NN = ((1,), (0,))
NT = ((1,), (1,))
TN = ((0,), (0,))


def dot(left, right, dims):
    return lax.dot_general(left, right, (dims, ((), ())), preferred_element_type=F32)


def halves(x):
    high = x.astype(BF16)
    return high, (x - high.astype(F32)).astype(BF16)


def product(pairs, dims):
    left = [part for (high, low), _ in pairs for part in (high, high, low)]
    right = [part for _, (high, low) in pairs for part in (high, low, high)]
    return dot(
        jnp.concatenate(left, axis=dims[0][0]), jnp.concatenate(right, axis=dims[1][0]), dims
    )


def low_code(x, high):
    rest = (x - high) / jnp.where(high == 0.0, 1.0, high)
    return jnp.clip(jnp.floor(rest * 512.0 + 2.0), 0.0, 3.0)


def with_code(high, code):
    return high + high * ((code - 1.5) / 512.0)


def split_codes(packed):
    codes = []
    for place in (64.0, 16.0, 4.0):
        codes.insert(0, jnp.floor(packed / place))
        packed = packed - place * codes[0]
    return [packed] + codes


def mean(x):
    return jnp.mean(x, axis=-1, keepdims=True)


def total(x):
    return jnp.sum(x, axis=-1, keepdims=True)


def centre(x):
    return x - mean(x)


def normalize(x, x_tan):
    centred = centre(x)
    inverse = lax.rsqrt(mean(centred * centred) + 1e-06)
    y = centred * inverse
    shift = mean(y * x_tan)
    return y, (centre(x_tan) - y * shift) * inverse, inverse, shift


def normalize_back(y, y_tan, inverse, shift, cot, cot_tan):
    along = mean(y * cot)
    back = (centre(cot) - y * along) * inverse
    along_tan = mean(y_tan * cot) + mean(y * cot_tan)
    return (centre(cot_tan) - y_tan * along - y * along_tan - back * shift) * inverse


def attention(q, k, v, tq, tk, tv, cot, cot_tan):
    scale = 1.0 / math.sqrt(HD)
    qn, dqn, q_inverse, q_shift = normalize(q, tq)
    kn, dkn, k_inverse, k_shift = normalize(k, tk)
    qs, dqs, ks, dks = halves(qn * scale), halves(dqn * scale), halves(kn), halves(dkn)
    vs, dvs, cs, dcs = halves(v), halves(tv), halves(cot), halves(cot_tan)
    raised = jnp.exp(product([(qs, ks)], NT))
    probs = raised / total(raised)
    score_tan = product([(dqs, ks), (qs, dks)], NT)
    probs_tan = probs * (score_tan - total(probs * score_tan))
    ps, dps = halves(probs), halves(probs_tan)
    mixed_tan = product([(dps, vs), (ps, dvs)], NN)
    v_tan = product([(dps, cs), (ps, dcs)], TN)
    cot_probs = product([(cs, vs)], NT)
    cot_probs_tan = product([(dcs, vs), (cs, dvs)], NT)
    away = cot_probs - total(probs * cot_probs)
    away_tan = cot_probs_tan - total(probs_tan * cot_probs + probs * cot_probs_tan)
    ss, dss = halves(probs * away), halves(probs_tan * away + probs * away_tan)
    q_cot = scale * product([(ss, ks)], NN)
    q_cot_tan = scale * product([(dss, ks), (ss, dks)], NN)
    k_cot = product([(ss, qs)], TN)
    k_cot_tan = product([(dss, qs), (ss, dqs)], TN)
    q_tan = normalize_back(qn, dqn, q_inverse, q_shift, q_cot, q_cot_tan)
    k_tan = normalize_back(kn, dkn, k_inverse, k_shift, k_cot, k_cot_tan)
    return mixed_tan, q_tan, k_tan, v_tan


def own_sums_kernel(rows, cots, w_rows, w_cots, front, back):
    front[...] = dot(rows[...], w_rows[...], NN)
    back[...] = dot(cots[...], w_cots[...], NT)


def attention_sums_kernel(front_a, back_a, rows, cots, w_rows, w_cots, out):
    front = front_a[:, : 6 * HD] + dot(rows[...], w_rows[:, : 6 * HD], NN)
    back = back_a[:, : 2 * HD] + dot(cots[...], w_cots[: 2 * HD, :], NT)
    packed = [0.0, 0.0]
    for at in range(8):
        block = front[:, at * HD : (at + 1) * HD] if at < 6 else back[:, (at - 6) * HD : (at - 5) * HD]
        high = block.astype(BF16)
        out[:, at * HD : (at + 1) * HD] = high
        packed[at // 4] += low_code(block, high.astype(F32)) * 4.0 ** (at % 4)
    out[:, 8 * HD : 9 * HD] = packed[0].astype(BF16)
    out[:, 9 * HD :] = packed[1].astype(BF16)


def hidden_sums_kernel(front_a, back_a, rows, cots, w_rows, w_cots, out):
    columns = w_rows.shape[1]
    out[:, :columns] = (front_a[...] + dot(rows[...], w_rows[...], NN)).astype(BF16)
    out[:, columns:] = (back_a[...] + dot(cots[...], w_cots[...], NT)).astype(BF16)


def attention_kernel(whole, out):
    blocks = []
    for group in range(2):
        codes = split_codes(whole[:, (8 + group) * HD : (9 + group) * HD].astype(F32))
        for at in range(4):
            place = 4 * group + at
            blocks.append(with_code(whole[:, place * HD : (place + 1) * HD].astype(F32), codes[at]))
    mixed, q_tan, k_tan, v_tan = attention(*blocks)
    for at, part in enumerate((q_tan, k_tan, v_tan, mixed)):
        out[:, at * HD : (at + 1) * HD] = part.astype(BF16)
    out[:, 4 * HD :] = jnp.zeros((out.shape[0], out.shape[1] - 4 * HD), BF16)


def products_kernel(role, lows, rows, cots, *refs):
    qkv_out, out_out, up_out, down_out, qkv, out, up, down, sems = refs[-9:]

    def write(pairs):
        copies = [pltpu.make_async_copy(*pair, sems.at[at]) for at, pair in enumerate(pairs)]
        for copy in copies:
            copy.start()
        for copy in copies:
            copy.wait()

    @pl.when(role[0] == 0)
    def _():
        for at in range(3):
            qkv[at] = dot(rows[...], lows[:, at * HD : (at + 1) * HD], TN).astype(BF16)
        out[...] = dot(lows[:, 3 * HD : 4 * HD], cots[...], TN).astype(BF16)
        write([(qkv, qkv_out), (out, out_out)])

    @pl.when(role[0] == 1)
    def _():
        hidden = down.shape[0]
        up[...] = dot(rows[...], lows[:, hidden:], TN).astype(BF16)
        down[...] = dot(lows[:, :hidden], cots[...], TN).astype(BF16)
        write([(up, up_out), (down, down_out)])


def hidden_pair(pre, cot_in):
    result, pull = jax.vjp(jax.nn.gelu, pre)
    return (result, pull(cot_in)[0])


def body(patches, cotangent, w_qkv, w_out, w_up, w_down, dir_qkv, dir_out, dir_up, dir_down):
    wide = lax.axis_size("mx")
    long = lax.axis_size("my")
    chips = wide // 2
    core = lax.rem(lax.axis_index("mx"), 2)
    ring = [[chip * 2 + c for chip in range(chips)] for c in range(2)]
    swap = [(i, i ^ 1) for i in range(wide)]
    width = w_qkv.shape[0]
    hidden = w_up.shape[1]
    count = patches.shape[0] * long
    share = count // chips

    own_rows = patches.shape[0]
    copy_shape = (long, 2, own_rows, width)
    copies = jnp.where(
        lax.broadcasted_iota(jnp.int32, copy_shape, 1) == 0,
        jnp.broadcast_to(patches, copy_shape),
        jnp.broadcast_to(cotangent, copy_shape),
    )
    gathered = lax.all_to_all(copies, "my", 0, 0, tiled=True)
    swapped = lax.ppermute(gathered, "mx", swap)

    first = core == 0
    flat = lambda a: [a[:, at] for at in range(3)]
    attn_front = jnp.concatenate(flat(w_qkv) + flat(dir_qkv), axis=1)
    attn_front = jnp.pad(attn_front, ((0, 0), (0, 2 * hidden - 6 * HD)))
    attn_back = jnp.pad(jnp.concatenate([w_out, dir_out]), ((0, 2 * hidden - 2 * HD), (0, 0)))
    hid_front = jnp.concatenate([w_up, dir_up], axis=1)
    hid_back = jnp.concatenate([w_down, dir_down])
    kept = (jnp.where(first, attn_front, hid_front), jnp.where(first, attn_back, hid_back))
    lent = (jnp.where(first, hid_front, attn_front), jnp.where(first, hid_back, attn_back))
    taken = tuple(lax.ppermute(a, "mx", swap) for a in lent)

    pick = lambda a, at: a[:, at].reshape(count, width)
    rows, cots = pick(gathered, 0), pick(gathered, 1)
    room = pltpu.CompilerParams(vmem_limit_bytes=48 * 2**20)
    own_sums = pl.pallas_call(
        own_sums_kernel,
        out_shape=(jax.ShapeDtypeStruct((count, 2 * hidden), F32),) * 2,
        in_specs=[VMEM] * 4,
        out_specs=(VMEM,) * 2,
        compiler_params=room,
        cost_estimate=pl.CostEstimate(
            flops=8 * count * width * hidden,
            bytes_accessed=8 * width * hidden + 16 * count * hidden,
            transcendentals=0,
        ),
        name="own_sums",
    )(rows, cots, *kept)

    def sums(kernel, columns, name, operands):
        message = pl.pallas_call(
            kernel,
            out_shape=jax.ShapeDtypeStruct((count, columns), BF16),
            in_specs=[VMEM] * 6,
            out_specs=VMEM,
            compiler_params=room,
            name=name,
        )(*operands)
        message = message.reshape(chips, share, columns)
        return lax.all_to_all(message, "mx", 0, 0, tiled=True, axis_index_groups=ring).astype(F32)

    def spread(reply):
        copies = jnp.broadcast_to(reply.astype(BF16), (chips,) + reply.shape)
        whole = lax.all_to_all(copies, "mx", 0, 0, tiled=True, axis_index_groups=ring)
        return whole.reshape(count, -1)

    def attention_part(*operands):
        parts = sums(attention_sums_kernel, 10 * HD, "attention_sums", operands)
        block = lambda at: parts[..., at * HD : (at + 1) * HD]
        reply, packed = [], []
        for group in range(2):
            codes = split_codes(block(8 + group))
            whole = [jnp.sum(with_code(block(4 * group + at), codes[at]), axis=0) for at in range(4)]
            highs = [lax.reduce_precision(a, 8, 7) for a in whole]
            reply += highs
            packed.append(sum(low_code(a, high) * 4.0**at for at, (a, high) in enumerate(zip(whole, highs))))
        return pl.pallas_call(
            attention_kernel,
            out_shape=jax.ShapeDtypeStruct((count, 2 * hidden), BF16),
            in_specs=[VMEM],
            out_specs=VMEM,
            compiler_params=room,
            name="attention",
        )(spread(jnp.concatenate(reply + packed, axis=1)))

    def hidden_part(*operands):
        parts = sums(hidden_sums_kernel, 4 * hidden, "hidden_sums", operands)
        whole = jnp.sum(parts, axis=0)
        pre_hidden, tan_hidden, cot_act, tan_act = jnp.split(whole, 4, axis=1)
        hid_tan = jax.jvp(hidden_pair, (pre_hidden, cot_act), (tan_hidden, tan_act))[1]
        return spread(jnp.concatenate(hid_tan, axis=1))

    lows = lax.cond(
        first,
        attention_part,
        hidden_part,
        *own_sums,
        pick(swapped, 0),
        pick(swapped, 1),
        *taken,
    )
    theirs = lax.ppermute(lows, "mx", swap)

    shapes = ((3, width, HD), w_out.shape, w_up.shape, w_down.shape)
    anywhere = pl.BlockSpec(memory_space=pl.ANY)

    def products(role, part, written, name):
        return pl.pallas_call(
            products_kernel,
            out_shape=tuple(jax.ShapeDtypeStruct(shape, BF16) for shape in shapes),
            in_specs=[SMEM] + [VMEM] * 3 + [anywhere] * len(written),
            out_specs=(anywhere,) * 4,
            scratch_shapes=[pltpu.VMEM(shape, BF16) for shape in shapes]
            + [pltpu.SemaphoreType.DMA((2,))],
            input_output_aliases={4 + at: at for at in range(len(written))},
            compiler_params=room,
            cost_estimate=pl.CostEstimate(
                flops=8 * count * width * hidden,
                bytes_accessed=8 * width * hidden,
                transcendentals=0,
            ),
            name=name,
        )(role.reshape(1).astype(jnp.int32), part, rows, cots, *written)

    written = products(core, lows, (), "own_products")
    hvp_qkv, hvp_out, hvp_up, hvp_down = products(1 - core, theirs, written, "other_products")
    return jnp.transpose(hvp_qkv, (1, 0, 2)), hvp_out, hvp_up, hvp_down


def solution(mesh):
    return jax.shard_map(
        body,
        mesh=mesh,
        in_specs=(
            P("my", "mx"),
            P("my", "mx"),
            P("mx", None, "my"),
            P("my", "mx"),
            P("mx", "my"),
            P("my", "mx"),
            P("mx", None, "my"),
            P("my", "mx"),
            P("mx", "my"),
            P("my", "mx"),
        ),
        out_specs=(P("mx", None, "my"), P("my", "mx"), P("mx", "my"), P("my", "mx")),
        check_vma=False,
    )
```

time: 106 us -> 98.1 us (0.925)
  blocking collectives: 58.4 us -> 54.4 us
  starting transfers between devices: 29.2 us -> 26.3 us
  waiting for transfers between devices: 4.77 us -> 3.7 us
    all_to_all x2, blocking collectives: 58.4 us -> 54.4 us  [the longest x1 37 us: sums(): lax.all_to_all(message, 'mx', 0, 0, tiled=True, axis_index_groups=ring)]
    ppermute x1, starting transfers between devices: 4.84 us -> 1.91 us  [body(): theirs = lax.ppermute(lows, 'mx', swap)]
    select_n x2, other arithmetic: 0.18 us -> 2.81 us  [the longest x1 1.43 us: body(): jnp.where(first, hid_front, attn_front)]
    concatenate x5 -> x1, other arithmetic: 2.19 us -> 0.01 us  [hidden_part(): return spread(jnp.concatenate(hid_tan, axis=1))]
    squeeze x1 -> x0, local copies, waits for them, and re-layouts: 1.17 us -> none  [pick(): zero = jnp.concatenate([w_qkv[:, 0], w_qkv[:, 2], dir_qkv[:, 0]], axis=1)]
  transfers between devices with their start and end apart: 5 -> 5, of which waited for: 3 -> 3; matrix products, arithmetic and copies ran while one was open for 4% -> 3% of each run, Pallas kernels for 1% -> 2%
where the time goes in v5:
time: 98.1 us; the launch traced here: 97.6 us
  blocking collectives  54.4 us (55%)
  starting transfers between devices  26.3 us (27%)
  Pallas kernels  6.13 us (6%)
  other arithmetic  4.84 us (5%)
  waiting for transfers between devices  3.7 us (4%)
  local copies, waits for them, and re-layouts  1.35 us (1%)
    all_to_all x1, blocking collectives, sums(): lax.all_to_all(message, 'mx', 0, 0, tiled=True, axis_index_groups=ring)  37 us
    all_to_all x1, blocking collectives, spread(): lax.all_to_all(copies, 'mx', 0, 0, tiled=True, axis_index_groups=ring)  17.4 us
    all_to_all x1, starting transfers between devices, body(): gathered = lax.all_to_all(copies, 'my', 0, 0, tiled=True)  13.7 us
    ppermute x1, starting transfers between devices, body(): swapped = lax.ppermute(gathered, 'mx', swap)  5.73 us
    ppermute x2, starting transfers between devices, body(): taken = tuple((lax.ppermute(a, 'mx', swap) for a in lent))  4.89 us
    pallas_call x1, Pallas kernels, sums(): pl.pallas_call(kernel, out_shape=jax.ShapeDtypeStruct((count, columns), B...  2.6 us
    all_to_all x1, waiting for transfers between devices, body(): gathered = lax.all_to_all(copies, 'my', 0, 0, tiled=True)  2.57 us
    pallas_call x2, Pallas kernels, products(): pl.pallas_call(products_kernel, out_shape=tuple((jax.ShapeDtypeStruct(sha...  2.56 us
  transfers between devices with their start and end apart: 5, of which 3 were waited for; matrix products, arithmetic and copies ran while one was open for 3% of the time, Pallas kernels for 2%

profile of v5, /device:TPU:1, one launch (start us, length us, event | category | flops | bytes accessed | tf_op | source)
XLA Modules:
  0.0 97.6 jit_solution(6518044482335379892)
XLA Ops:
  0.6 0.0 copy-start.4
  0.6 0.0 copy-start.5
  0.7 0.0 copy-start
  0.7 1.6 %broadcast_select_fusion.2 = bf16[32,2,8,384]{3,2,1,0:T(8,128)(2,1)} fusion(pred[2]{0:T(512)(128)(4,1)S(1)} %iota_compare_fusion.1, bf16[8,384]{1,0:T(8,128)(2,1)} %param.13, bf16[8,384]{1,0:T(8,128)(2,1)} %param.12), kind=kLoop, calls=%fused_computation.135 | loop fusion | flops 196608 | bytes 405506 | tf_op jit(solution)/shard_map/jit(_where)/select_n | solution.py:190
  2.3 13.7 %all-to-all-start.4 = ((bf16[32,2,8,384]{3,2,1,0:T(8,128)(2,1)}), bf16[32,2,8,384]{3,2,1,0:T(8,128)(2,1)S(1)}, u32[]{:S(2)}, u32[]{:S(2)}) async-start(bf16[32,2,8,384]{3,2,1,0:T(8,128)(2,1)} %broadcast_select_fusion.2), calls=%async_computation.4 | async-start | bytes 786432 | tf_op jit(solution)/shard_map/all_to_all | solution.py:195
  16.1 0.0 copy-done.4
  16.1 0.0 copy-start.1
  16.2 0.0 copy-done.5
  16.3 0.0 copy-done
  16.3 0.8 copy-done.1
  17.2 0.0 copy-start.2
  17.2 1.4 %pad_select_fusion = (bf16[384,1536]{1,0:T(8,128)(2,1)}, bf16[384,1536]{1,0:T(8,128)(2,1)S(1)}) fusion(bf16[384,1536]{1,0:T(8,128)(2,1)S(1)} %constant_dynamic-update-slice_fusion.10, bf16[384,768]{1,0:T(8,128)(2,1)S(1)} %bitcast_dynamic-update-slice_fusion, pred[]{:T(512)S(6)} %eq.34), kind=kLoop, calls=%fused_computation.130 | loop fusion | flops 1179648 | bytes 4128769 | tf_op jit(solution)/shard_map/jit(_where)/select_n | solution.py:206
  18.6 0.0 copy-start.3
  18.6 0.0 copy-start.6
  18.6 0.0 copy-start.7
  18.6 3.0 %collective-permute-start.1 = (bf16[384,1536]{1,0:T(8,128)(2,1)}, bf16[384,1536]{1,0:T(8,128)(2,1)}, u32[]{:S(2)}, u32[]{:S(2)}) collective-permute-start(bf16[384,1536]{1,0:T(8,128)(2,1)} %get-tuple-element.73), channel_id=1, source_target_pairs={{0,32},{32,0},{64,96},{96,64},{128,160},{160,128},{192,224},{224,1... | collective-permute-start | bytes 3538952 | tf_op jit(solution)/shard_map/ppermute | solution.py:207
  21.6 0.0 copy-done.2
  21.6 0.1 constant_dynamic-update-slice_fusion.13
  21.7 0.0 copy-done.3
  21.7 0.1 constant_dynamic-update-slice_fusion.12
  21.8 0.0 copy-done.6
  21.8 0.0 copy-done.7
  21.8 1.4 %broadcast_select_fusion = (bf16[1536,384]{1,0:T(8,128)(2,1)}, bf16[1536,384]{1,0:T(8,128)(2,1)S(1)}) fusion(bf16[1536,384]{1,0:T(8,128)(2,1)S(1)} %constant_dynamic-update-slice_fusion.12, pred[]{:T(512)S(6)} %eq.34, bf16[128,384]{1,0:T(8,128)(2,1)S(1)} %copy-done.6, bf16[128,384]{1,0:T(8,128)(2,1)S(1)} %copy-done.7), kind=kLoop, calls=%fused_computation.133 | loop fusion | flops 5308416 | bytes 3735553 | tf_op jit(solution)/shard_map/jit(_where)/select_n | solution.py:206
  23.2 1.9 %collective-permute-start.2 = (bf16[1536,384]{1,0:T(8,128)(2,1)}, bf16[1536,384]{1,0:T(8,128)(2,1)}, u32[]{:S(2)}, u32[]{:S(2)}) collective-permute-start(bf16[1536,384]{1,0:T(8,128)(2,1)} %get-tuple-element.75), channel_id=1, source_target_pairs={{0,32},{32,0},{64,96},{96,64},{128,160},{160,128},{192,224},{224,1... | collective-permute-start | bytes 3538952 | tf_op jit(solution)/shard_map/ppermute | solution.py:207
  25.1 2.6 %all-to-all-done.4 = bf16[32,2,8,384]{3,2,1,0:T(8,128)(2,1)S(1)} async-done(((bf16[32,2,8,384]{3,2,1,0:T(8,128)(2,1)}), bf16[32,2,8,384]{3,2,1,0:T(8,128)(2,1)S(1)}, u32[]{:S(2)}, u32[]{:S(2)}) %all-to-all-start.4) | async-done | bytes 393248 | tf_op jit(solution)/shard_map/all_to_all | solution.py:195
  27.7 5.7 %collective-permute-start = (bf16[32,2,8,384]{3,2,1,0:T(8,128)(2,1)S(1)}, bf16[32,2,8,384]{3,2,1,0:T(8,128)(2,1)S(1)}, u32[]{:S(2)}, u32[]{:S(2)}) collective-permute-start(bf16[32,2,8,384]{3,2,1,0:T(8,128)(2,1)S(1)} %all-to-all-done.4), channel_id=1, source_target_pairs={{0,32},{32,0},{64,96},{96,64},{128,160},{160,128},{192,224},{224,1... | collective-permute-start | bytes 1179656 | tf_op jit(solution)/shard_map/ppermute | solution.py:196
  33.5 1.0 own_sums.1
  34.5 0.3 collective-permute-done
  34.8 0.0 collective-permute-done.1
  34.8 0.0 collective-permute-done.2
  34.8 57.5 %conditional.1 = (bf16[256,1536]{1,0:T(8,128)(2,1)S(1)}) conditional(s32[]{:T(128)} %convert_element_type.15, (f32[256,1536]{1,0:T(8,128)S(1)}, f32[256,1536]{1,0:T(8,128)S(1)}, bf16[256,384]{1,0:T(8,128)(2,1)S(1)}, bf16[256,384]{1,0:T(8,128)(2,1)S(1)}, bf16[384,1536]{1,0:T(8,128)(2,1)}, /*index=5*/bf16[1536,384]{1,0:T(8,128)(2,1)}) %tuple.14, ...), branch_computations={%region_0.2_spmd, %region_2.11_spmd} | conditional | flops 2826240 | bytes 8257544 | solution.py:269
  34.8 2.6 %hidden_sums.1 = bf16[256,3072]{1,0:T(8,128)(2,1)S(1)} custom-call(f32[256,1536]{1,0:T(8,128)S(1)} %get-tuple-element.17.front_a, f32[256,1536]{1,0:T(8,128)S(1)} %get-tuple-element.28.back_a, bf16[256,384]{1,0:T(8,128)(2,1)S(1)} %get-tuple-element.29.rows, bf16[256,384]{1,0:T(8,128)(2,1)S(1)} %get-tuple-element.30.cots, ...), custom_call_target="tpu_custom_call" | custom-call | tf_op jit(solution)/shard_map/cond/branch_0_fun/hidden_sums/pallas_call | solution.py:227
  37.5 37.0 %all_to_all.21 = bf16[8,32,3072]{2,1,0:T(8,128)(2,1)S(1)} all-to-all(bf16[8,32,3072]{2,1,0:T(8,128)(2,1)S(1)} %bitcast.27), channel_id=1, replica_groups={{0,64,128,192,256,320,384,448},{32,96,160,224,288,352,416,480},{1,65,12..., dimensions={0} | all-to-all | bytes 3145728 | tf_op jit(solution)/shard_map/cond/branch_0_fun/all_to_all | solution.py:236
  74.5 0.2 convert_reduce_fusion
  74.7 0.2 add_convert_fusion.1
  74.9 0.1 broadcast_in_dim.18
  75.0 17.4 %all_to_all.22 = bf16[8,32,1536]{2,1,0:T(8,128)(2,1)S(1)} all-to-all(bf16[8,32,1536]{2,1,0:T(8,128)(2,1)S(1)} %broadcast_in_dim.18), channel_id=1, replica_groups={{0,64,128,192,256,320,384,448},{32,96,160,224,288,352,416,480},{1,65,12..., dimensions={0} | all-to-all | bytes 1572864 | tf_op jit(solution)/shard_map/cond/branch_0_fun/all_to_all | solution.py:240
  92.3 1.9 %collective-permute-start.3 = (bf16[256,1536]{1,0:T(8,128)(2,1)S(1)}, bf16[256,1536]{1,0:T(8,128)(2,1)S(1)}, u32[]{:S(2)}, u32[]{:S(2)}) collective-permute-start(bf16[256,1536]{1,0:T(8,128)(2,1)S(1)} %get-tuple-element.81.lows), channel_id=1, source_target_pairs={{0,32},{32,0},{64,96},{96,64},{128,160},{160,128},{192,224},{224,1... | collective-permute-start | bytes 2359304 | tf_op jit(solution)/shard_map/ppermute | solution.py:278
  94.2 1.4 %own_products.1 = (bf16[3,384,128]{2,1,0:T(8,128)(2,1)}, bf16[128,384]{1,0:T(8,128)(2,1)}, bf16[384,768]{1,0:T(8,128)(2,1)}, bf16[768,384]{1,0:T(8,128)(2,1)}) custom-call(s32[1]{0:T(128)} %bitcast.15.role, bf16[256,1536]{1,0:T(8,128)(2,1)S(1)} %get-tuple-element.81.lows, bf16[256,384]{1,0:T(8,128)(2,1)S(1)} %get-tuple-element.80.rows, ...), custom_call_target="tpu_custom_call" | custom-call | flops 603979776 | bytes 2359296 | tf_op jit(solution)/shard_map/own_products/pallas_call | solution.py:284
  95.7 0.8 collective-permute-done.3.lows
  96.5 1.1 %other_products.1 = (bf16[3,384,128]{2,1,0:T(8,128)(2,1)}, bf16[128,384]{1,0:T(8,128)(2,1)}, bf16[384,768]{1,0:T(8,128)(2,1)}, bf16[768,384]{1,0:T(8,128)(2,1)}) custom-call(s32[1]{0:T(128)} %bitcast.4.role, bf16[256,1536]{1,0:T(8,128)(2,1)S(1)} %collective-permute-done.3.lows, ...), custom_call_target="tpu_custom_call", output_to_operand_aliasing={{0}: (4, {}), {1}: (5, {}), {2}: (6, {}), {3}: (7, {})} | custom-call | flops 603979776 | bytes 2359296 | tf_op jit(solution)/shard_map/other_products/pallas_call | solution.py:284
  (12 shorter events, 0.3 us)
Async XLA Ops:
  0.6 15.4 %copy-start.4 = (bf16[384,3,128]{2,0,1:T(8,128)(2,1)S(1)}, bf16[384,3,128]{2,0,1:T(8,128)(2,1)}, u32[]{:S(2)}) copy-start(bf16[384,3,128]{2,0,1:T(8,128)(2,1)} %param.14) | copy-start | bytes 884740
  0.6 15.5 %copy-start.5 = (bf16[384,3,128]{2,0,1:T(8,128)(2,1)S(1)}, bf16[384,3,128]{2,0,1:T(8,128)(2,1)}, u32[]{:S(2)}) copy-start(bf16[384,3,128]{2,0,1:T(8,128)(2,1)} %param.18) | copy-start | bytes 884740
  0.7 15.6 %copy-start = (bf16[384,768]{1,0:T(8,128)(2,1)S(1)}, bf16[384,768]{1,0:T(8,128)(2,1)}, u32[]{:S(2)}) copy-start(bf16[384,768]{1,0:T(8,128)(2,1)} %param.16) | copy-start | bytes 1769476
  2.3 25.4 %all-to-all-start.4 = ((bf16[32,2,8,384]{3,2,1,0:T(8,128)(2,1)}), bf16[32,2,8,384]{3,2,1,0:T(8,128)(2,1)S(1)}, u32[]{:S(2)}, u32[]{:S(2)}) async-start(bf16[32,2,8,384]{3,2,1,0:T(8,128)(2,1)} %broadcast_select_fusion.2), calls=%async_computation.4 | async-start | bytes 786432 | tf_op jit(solution)/shard_map/all_to_all | solution.py:195
  16.1 1.1 %copy-start.1 = (bf16[384,768]{1,0:T(8,128)(2,1)S(1)}, bf16[384,768]{1,0:T(8,128)(2,1)}, u32[]{:S(2)}) copy-start(bf16[384,768]{1,0:T(8,128)(2,1)} %param.20) | copy-start | bytes 1769476
  17.2 4.4 %copy-start.2 = (bf16[768,384]{1,0:T(8,128)(2,1)S(1)}, bf16[768,384]{1,0:T(8,128)(2,1)}, u32[]{:S(2)}) copy-start(bf16[768,384]{1,0:T(8,128)(2,1)} %param.17) | copy-start | bytes 1769476
  18.6 3.1 %copy-start.3 = (bf16[768,384]{1,0:T(8,128)(2,1)S(1)}, bf16[768,384]{1,0:T(8,128)(2,1)}, u32[]{:S(2)}) copy-start(bf16[768,384]{1,0:T(8,128)(2,1)} %param.21) | copy-start | bytes 1769476
  18.6 3.2 %copy-start.6 = (bf16[128,384]{1,0:T(8,128)(2,1)S(1)}, bf16[128,384]{1,0:T(8,128)(2,1)}, u32[]{:S(2)}) copy-start(bf16[128,384]{1,0:T(8,128)(2,1)} %param.19) | copy-start | bytes 294916
  18.6 3.2 %copy-start.7 = (bf16[128,384]{1,0:T(8,128)(2,1)S(1)}, bf16[128,384]{1,0:T(8,128)(2,1)}, u32[]{:S(2)}) copy-start(bf16[128,384]{1,0:T(8,128)(2,1)} %param.15) | copy-start | bytes 294916
  18.6 16.2 %collective-permute-start.1 = (bf16[384,1536]{1,0:T(8,128)(2,1)}, bf16[384,1536]{1,0:T(8,128)(2,1)}, u32[]{:S(2)}, u32[]{:S(2)}) collective-permute-start(bf16[384,1536]{1,0:T(8,128)(2,1)} %get-tuple-element.73), channel_id=1, source_target_pairs={{0,32},{32,0},{64,96},{96,64},{128,160},{160,128},{192,224},{224,1... | collective-permute-start | bytes 3538952 | tf_op jit(solution)/shard_map/ppermute | solution.py:207
  23.2 11.6 %collective-permute-start.2 = (bf16[1536,384]{1,0:T(8,128)(2,1)}, bf16[1536,384]{1,0:T(8,128)(2,1)}, u32[]{:S(2)}, u32[]{:S(2)}) collective-permute-start(bf16[1536,384]{1,0:T(8,128)(2,1)} %get-tuple-element.75), channel_id=1, source_target_pairs={{0,32},{32,0},{64,96},{96,64},{128,160},{160,128},{192,224},{224,1... | collective-permute-start | bytes 3538952 | tf_op jit(solution)/shard_map/ppermute | solution.py:207
  27.7 7.1 %collective-permute-start = (bf16[32,2,8,384]{3,2,1,0:T(8,128)(2,1)S(1)}, bf16[32,2,8,384]{3,2,1,0:T(8,128)(2,1)S(1)}, u32[]{:S(2)}, u32[]{:S(2)}) collective-permute-start(bf16[32,2,8,384]{3,2,1,0:T(8,128)(2,1)S(1)} %all-to-all-done.4), channel_id=1, source_target_pairs={{0,32},{32,0},{64,96},{96,64},{128,160},{160,128},{192,224},{224,1... | collective-permute-start | bytes 1179656 | tf_op jit(solution)/shard_map/ppermute | solution.py:196
  92.3 4.2 %collective-permute-start.3 = (bf16[256,1536]{1,0:T(8,128)(2,1)S(1)}, bf16[256,1536]{1,0:T(8,128)(2,1)S(1)}, u32[]{:S(2)}, u32[]{:S(2)}) collective-permute-start(bf16[256,1536]{1,0:T(8,128)(2,1)S(1)} %get-tuple-element.81.lows), channel_id=1, source_target_pairs={{0,32},{32,0},{64,96},{96,64},{128,160},{160,128},{192,224},{224,1... | collective-permute-start | bytes 2359304 | tf_op jit(solution)/shard_map/ppermute | solution.py:278

commit v6 on v5

--- a/solution.py
+++ b/solution.py
@@ -35,20 +35,20 @@
     )
 
 
-def low_code(x, high):
+def low_code(x, high, levels):
     rest = (x - high) / jnp.where(high == 0.0, 1.0, high)
-    return jnp.clip(jnp.floor(rest * 512.0 + 2.0), 0.0, 3.0)
-
-
-def with_code(high, code):
-    return high + high * ((code - 1.5) / 512.0)
-
-
-def split_codes(packed):
+    return jnp.clip(jnp.floor((rest * 256.0 + 1.0) * (levels / 2)), 0.0, levels - 1.0)
+
+
+def with_code(high, code, levels):
+    return high + high * (((code + 0.5) * (2 / levels) - 1.0) / 256.0)
+
+
+def split_codes(packed, levels, number):
     codes = []
-    for place in (64.0, 16.0, 4.0):
-        codes.insert(0, jnp.floor(packed / place))
-        packed = packed - place * codes[0]
+    for place in range(number - 1, 0, -1):
+        codes.insert(0, jnp.floor(packed / float(levels) ** place))
+        packed = packed - float(levels) ** place * codes[0]
     return [packed] + codes
 
 
@@ -111,33 +111,41 @@
     back[...] = dot(cots[...], w_cots[...], NT)
 
 
-def attention_sums_kernel(front_a, back_a, rows, cots, w_rows, w_cots, out):
-    front = front_a[:, : 6 * HD] + dot(rows[...], w_rows[:, : 6 * HD], NN)
-    back = back_a[:, : 2 * HD] + dot(cots[...], w_cots[: 2 * HD, :], NT)
-    packed = [0.0, 0.0]
-    for at in range(8):
-        block = front[:, at * HD : (at + 1) * HD] if at < 6 else back[:, (at - 6) * HD : (at - 5) * HD]
-        high = block.astype(BF16)
-        out[:, at * HD : (at + 1) * HD] = high
-        packed[at // 4] += low_code(block, high.astype(F32)) * 4.0 ** (at % 4)
-    out[:, 8 * HD : 9 * HD] = packed[0].astype(BF16)
-    out[:, 9 * HD :] = packed[1].astype(BF16)
-
-
-def hidden_sums_kernel(front_a, back_a, rows, cots, w_rows, w_cots, out):
-    columns = w_rows.shape[1]
-    out[:, :columns] = (front_a[...] + dot(rows[...], w_rows[...], NN)).astype(BF16)
-    out[:, columns:] = (back_a[...] + dot(cots[...], w_cots[...], NT)).astype(BF16)
+def sums_kernel(role, front_a, back_a, rows, cots, w_rows, w_cots, out):
+    @pl.when(role[0] == 0)
+    def _():
+        front = front_a[:, : 6 * HD] + dot(rows[...], w_rows[:, : 6 * HD], NN)
+        back = back_a[:, : 2 * HD] + dot(cots[...], w_cots[: 2 * HD, :], NT)
+        packed = 0.0
+        for at in range(8):
+            half, place = at // 4, at % 4
+            if place < 3:
+                block = front[:, (3 * half + place) * HD : (3 * half + place + 1) * HD]
+            else:
+                block = back[:, half * HD : (half + 1) * HD]
+            high = block.astype(BF16)
+            out[:, at * HD : (at + 1) * HD] = high
+            if half == 0:
+                packed += low_code(block, high.astype(F32), 4) * 4.0**place
+        out[:, 8 * HD : 9 * HD] = packed.astype(BF16)
+
+    @pl.when(role[0] == 1)
+    def _():
+        columns = w_rows.shape[1]
+        out[:, :columns] = (front_a[...] + dot(rows[...], w_rows[...], NN)).astype(BF16)
+        out[:, columns:] = (back_a[...] + dot(cots[...], w_cots[...], NT)).astype(BF16)
 
 
 def attention_kernel(whole, out):
     blocks = []
-    for group in range(2):
-        codes = split_codes(whole[:, (8 + group) * HD : (9 + group) * HD].astype(F32))
-        for at in range(4):
-            place = 4 * group + at
-            blocks.append(with_code(whole[:, place * HD : (place + 1) * HD].astype(F32), codes[at]))
-    mixed, q_tan, k_tan, v_tan = attention(*blocks)
+    for pair in range(4):
+        codes = split_codes(whole[:, (8 + pair) * HD : (9 + pair) * HD].astype(F32), 16, 2)
+        for at in range(2):
+            place = 2 * pair + at
+            high = whole[:, place * HD : (place + 1) * HD].astype(F32)
+            blocks.append(with_code(high, codes[at], 16))
+    q, k, v, cot, tq, tk, tv, cot_tan = blocks
+    mixed, q_tan, k_tan, v_tan = attention(q, k, v, tq, tk, tv, cot, cot_tan)
     for at, part in enumerate((q_tan, k_tan, v_tan, mixed)):
         out[:, at * HD : (at + 1) * HD] = part.astype(BF16)
     out[:, 4 * HD :] = jnp.zeros((out.shape[0], out.shape[1] - 4 * HD), BF16)
@@ -146,26 +154,30 @@
 def products_kernel(role, lows, rows, cots, *refs):
     qkv_out, out_out, up_out, down_out, qkv, out, up, down, sems = refs[-9:]
 
-    def write(pairs):
-        copies = [pltpu.make_async_copy(*pair, sems.at[at]) for at, pair in enumerate(pairs)]
-        for copy in copies:
-            copy.start()
-        for copy in copies:
-            copy.wait()
+    def write(at, pair):
+        copy = pltpu.make_async_copy(*pair, sems.at[at])
+        copy.start()
+        return copy
 
     @pl.when(role[0] == 0)
     def _():
         for at in range(3):
             qkv[at] = dot(rows[...], lows[:, at * HD : (at + 1) * HD], TN).astype(BF16)
+        qkv_copy = write(0, (qkv, qkv_out))
         out[...] = dot(lows[:, 3 * HD : 4 * HD], cots[...], TN).astype(BF16)
-        write([(qkv, qkv_out), (out, out_out)])
+        out_copy = write(1, (out, out_out))
+        qkv_copy.wait()
+        out_copy.wait()
 
     @pl.when(role[0] == 1)
     def _():
         hidden = down.shape[0]
         up[...] = dot(rows[...], lows[:, hidden:], TN).astype(BF16)
+        up_copy = write(0, (up, up_out))
         down[...] = dot(lows[:, :hidden], cots[...], TN).astype(BF16)
-        write([(up, up_out), (down, down_out)])
+        down_copy = write(1, (down, down_out))
+        up_copy.wait()
+        down_copy.wait()
 
 
 def hidden_pair(pre, cot_in):
@@ -205,51 +217,51 @@
     kept = (jnp.where(first, attn_front, hid_front), jnp.where(first, attn_back, hid_back))
     lent = (jnp.where(first, hid_front, attn_front), jnp.where(first, hid_back, attn_back))
     taken = tuple(lax.ppermute(a, "mx", swap) for a in lent)
+    anywhere = pl.BlockSpec(memory_space=pl.ANY)
 
     pick = lambda a, at: a[:, at].reshape(count, width)
     rows, cots = pick(gathered, 0), pick(gathered, 1)
-    room = pltpu.CompilerParams(vmem_limit_bytes=48 * 2**20)
-    own_sums = pl.pallas_call(
+    room = pltpu.CompilerParams(vmem_limit_bytes=24 * 2**20)
+    cost = lambda flops, read: pl.CostEstimate(flops=flops, bytes_accessed=read, transcendentals=0)
+    sums_cost = cost(8 * count * width * hidden, 0)
+    own_front, own_back = pl.pallas_call(
         own_sums_kernel,
         out_shape=(jax.ShapeDtypeStruct((count, 2 * hidden), F32),) * 2,
         in_specs=[VMEM] * 4,
         out_specs=(VMEM,) * 2,
         compiler_params=room,
-        cost_estimate=pl.CostEstimate(
-            flops=8 * count * width * hidden,
-            bytes_accessed=8 * width * hidden + 16 * count * hidden,
-            transcendentals=0,
-        ),
+        cost_estimate=sums_cost,
         name="own_sums",
     )(rows, cots, *kept)
-
-    def sums(kernel, columns, name, operands):
-        message = pl.pallas_call(
-            kernel,
-            out_shape=jax.ShapeDtypeStruct((count, columns), BF16),
-            in_specs=[VMEM] * 6,
-            out_specs=VMEM,
-            compiler_params=room,
-            name=name,
-        )(*operands)
-        message = message.reshape(chips, share, columns)
-        return lax.all_to_all(message, "mx", 0, 0, tiled=True, axis_index_groups=ring).astype(F32)
+    role = lambda a: a.reshape(1).astype(jnp.int32)
+    message = pl.pallas_call(
+        sums_kernel,
+        out_shape=jax.ShapeDtypeStruct((count, 4 * hidden), BF16),
+        in_specs=[SMEM] + [VMEM] * 6,
+        out_specs=VMEM,
+        compiler_params=room,
+        cost_estimate=sums_cost,
+        name="sums",
+    )(role(core), own_front, own_back, pick(swapped, 0), pick(swapped, 1), *taken)
+
+    def exchange(part):
+        part = part.reshape(chips, share, -1)
+        return lax.all_to_all(part, "mx", 0, 0, tiled=True, axis_index_groups=ring).astype(F32)
 
     def spread(reply):
         copies = jnp.broadcast_to(reply.astype(BF16), (chips,) + reply.shape)
         whole = lax.all_to_all(copies, "mx", 0, 0, tiled=True, axis_index_groups=ring)
         return whole.reshape(count, -1)
 
-    def attention_part(*operands):
-        parts = sums(attention_sums_kernel, 10 * HD, "attention_sums", operands)
+    def attention_part(message):
+        parts = exchange(message[:, : 9 * HD])
         block = lambda at: parts[..., at * HD : (at + 1) * HD]
-        reply, packed = [], []
-        for group in range(2):
-            codes = split_codes(block(8 + group))
-            whole = [jnp.sum(with_code(block(4 * group + at), codes[at]), axis=0) for at in range(4)]
-            highs = [lax.reduce_precision(a, 8, 7) for a in whole]
-            reply += highs
-            packed.append(sum(low_code(a, high) * 4.0**at for at, (a, high) in enumerate(zip(whole, highs))))
+        codes = split_codes(block(8), 4, 4)
+        refined = [with_code(block(at), codes[at], 4) for at in range(4)]
+        whole = [jnp.sum(a, axis=0) for a in refined + [block(at) for at in range(4, 8)]]
+        highs = [lax.reduce_precision(a, 8, 7) for a in whole]
+        lows = [low_code(a, high, 16) for a, high in zip(whole, highs)]
+        packed = [lows[at] + 16.0 * lows[at + 1] for at in range(0, 8, 2)]
         return pl.pallas_call(
             attention_kernel,
             out_shape=jax.ShapeDtypeStruct((count, 2 * hidden), BF16),
@@ -257,30 +269,20 @@
             out_specs=VMEM,
             compiler_params=room,
             name="attention",
-        )(spread(jnp.concatenate(reply + packed, axis=1)))
-
-    def hidden_part(*operands):
-        parts = sums(hidden_sums_kernel, 4 * hidden, "hidden_sums", operands)
-        whole = jnp.sum(parts, axis=0)
+        )(spread(jnp.concatenate(highs + packed, axis=1)))
+
+    def hidden_part(message):
+        whole = jnp.sum(exchange(message), axis=0)
         pre_hidden, tan_hidden, cot_act, tan_act = jnp.split(whole, 4, axis=1)
         hid_tan = jax.jvp(hidden_pair, (pre_hidden, cot_act), (tan_hidden, tan_act))[1]
         return spread(jnp.concatenate(hid_tan, axis=1))
 
-    lows = lax.cond(
-        first,
-        attention_part,
-        hidden_part,
-        *own_sums,
-        pick(swapped, 0),
-        pick(swapped, 1),
-        *taken,
-    )
+    lows = lax.cond(first, attention_part, hidden_part, message)
     theirs = lax.ppermute(lows, "mx", swap)
 
     shapes = ((3, width, HD), w_out.shape, w_up.shape, w_down.shape)
-    anywhere = pl.BlockSpec(memory_space=pl.ANY)
-
-    def products(role, part, written, name):
+
+    def products(which, part, written, name):
         return pl.pallas_call(
             products_kernel,
             out_shape=tuple(jax.ShapeDtypeStruct(shape, BF16) for shape in shapes),
@@ -290,13 +292,9 @@
             + [pltpu.SemaphoreType.DMA((2,))],
             input_output_aliases={4 + at: at for at in range(len(written))},
             compiler_params=room,
-            cost_estimate=pl.CostEstimate(
-                flops=8 * count * width * hidden,
-                bytes_accessed=8 * width * hidden,
-                transcendentals=0,
-            ),
+            cost_estimate=cost(8 * count * width * hidden, 8 * width * hidden),
             name=name,
-        )(role.reshape(1).astype(jnp.int32), part, rows, cots, *written)
+        )(role(which), part, rows, cots, *written)
 
     written = products(core, lows, (), "own_products")
     hvp_qkv, hvp_out, hvp_up, hvp_down = products(1 - core, theirs, written, "other_products")

time: 98.1 us -> 97.5 us (level)
  no operation moved by 1% of the time
where the time goes in v6:
time: 97.5 us; the launch traced here: 97.1 us
  blocking collectives  53.8 us (55%)
  starting transfers between devices  26.3 us (27%)
  Pallas kernels  6.18 us (6%)
  other arithmetic  4.85 us (5%)
  waiting for transfers between devices  3.69 us (4%)
  local copies, waits for them, and re-layouts  1.35 us (1%)
    all_to_all x1, blocking collectives, exchange(): lax.all_to_all(part, 'mx', 0, 0, tiled=True, axis_index_groups=ring)  36.4 us
    all_to_all x1, blocking collectives, spread(): lax.all_to_all(copies, 'mx', 0, 0, tiled=True, axis_index_groups=ring)  17.4 us
    all_to_all x1, starting transfers between devices, body(): gathered = lax.all_to_all(copies, 'my', 0, 0, tiled=True)  13.7 us
    ppermute x1, starting transfers between devices, body(): swapped = lax.ppermute(gathered, 'mx', swap)  5.73 us
    ppermute x2, starting transfers between devices, body(): taken = tuple((lax.ppermute(a, 'mx', swap) for a in lent))  4.89 us
    pallas_call x1, Pallas kernels, body(): pl.pallas_call(sums_kernel, out_shape=jax.ShapeDtypeStruct((count, 4 * hi...  2.63 us
    pallas_call x2, Pallas kernels, products(): pl.pallas_call(products_kernel, out_shape=tuple((jax.ShapeDtypeStruct(sha...  2.57 us
    all_to_all x1, waiting for transfers between devices, body(): gathered = lax.all_to_all(copies, 'my', 0, 0, tiled=True)  2.57 us
  transfers between devices with their start and end apart: 5, of which 3 were waited for; matrix products, arithmetic and copies ran while one was open for 3% of the time, Pallas kernels for 2%

profile of v6, /device:TPU:1, one launch (start us, length us, event | category | flops | bytes accessed | tf_op | source)
XLA Modules:
  0.0 97.1 jit_solution(11461247808623259928)
XLA Ops:
  0.6 0.0 copy-start.4
  0.6 0.0 copy-start.5
  0.7 0.0 copy-start
  0.7 1.6 %broadcast_select_fusion.2 = bf16[32,2,8,384]{3,2,1,0:T(8,128)(2,1)} fusion(pred[2]{0:T(512)(128)(4,1)S(1)} %iota_compare_fusion.1, bf16[8,384]{1,0:T(8,128)(2,1)} %param.13, bf16[8,384]{1,0:T(8,128)(2,1)} %param.12), kind=kLoop, calls=%fused_computation.134 | loop fusion | flops 196608 | bytes 405506 | tf_op jit(solution)/shard_map/jit(_where)/select_n | solution.py:202
  2.3 13.7 %all-to-all-start.4 = ((bf16[32,2,8,384]{3,2,1,0:T(8,128)(2,1)}), bf16[32,2,8,384]{3,2,1,0:T(8,128)(2,1)S(1)}, u32[]{:S(2)}, u32[]{:S(2)}) async-start(bf16[32,2,8,384]{3,2,1,0:T(8,128)(2,1)} %broadcast_select_fusion.2), calls=%async_computation.4 | async-start | bytes 786432 | tf_op jit(solution)/shard_map/all_to_all | solution.py:207
  16.1 0.0 copy-done.4
  16.1 0.0 copy-start.1
  16.2 0.0 copy-done.5
  16.3 0.0 copy-done
  16.3 0.8 copy-done.1
  17.2 0.0 copy-start.2
  17.2 1.4 %pad_select_fusion = (bf16[384,1536]{1,0:T(8,128)(2,1)}, bf16[384,1536]{1,0:T(8,128)(2,1)S(1)}) fusion(bf16[384,1536]{1,0:T(8,128)(2,1)S(1)} %constant_dynamic-update-slice_fusion.12, bf16[384,768]{1,0:T(8,128)(2,1)S(1)} %bitcast_dynamic-update-slice_fusion, pred[]{:T(512)S(6)} %eq.34), kind=kLoop, calls=%fused_computation.129 | loop fusion | flops 1179648 | bytes 4128769 | tf_op jit(solution)/shard_map/jit(_where)/select_n | solution.py:218
  18.6 0.0 copy-start.3
  18.6 0.0 copy-start.6
  18.6 0.0 copy-start.7
  18.6 3.0 %collective-permute-start.1 = (bf16[384,1536]{1,0:T(8,128)(2,1)}, bf16[384,1536]{1,0:T(8,128)(2,1)}, u32[]{:S(2)}, u32[]{:S(2)}) collective-permute-start(bf16[384,1536]{1,0:T(8,128)(2,1)} %get-tuple-element.39), channel_id=1, source_target_pairs={{0,32},{32,0},{64,96},{96,64},{128,160},{160,128},{192,224},{224,1... | collective-permute-start | bytes 3538952 | tf_op jit(solution)/shard_map/ppermute | solution.py:219
  21.6 0.0 copy-done.2
  21.6 0.1 constant_dynamic-update-slice_fusion.15
  21.7 0.0 copy-done.3
  21.7 0.1 constant_dynamic-update-slice_fusion.14
  21.8 0.0 copy-done.6
  21.8 0.0 copy-done.7
  21.8 1.4 %broadcast_select_fusion = (bf16[1536,384]{1,0:T(8,128)(2,1)}, bf16[1536,384]{1,0:T(8,128)(2,1)S(1)}) fusion(bf16[1536,384]{1,0:T(8,128)(2,1)S(1)} %constant_dynamic-update-slice_fusion.14, pred[]{:T(512)S(6)} %eq.34, bf16[128,384]{1,0:T(8,128)(2,1)S(1)} %copy-done.6, bf16[128,384]{1,0:T(8,128)(2,1)S(1)} %copy-done.7), kind=kLoop, calls=%fused_computation.132 | loop fusion | flops 5308416 | bytes 3735553 | tf_op jit(solution)/shard_map/jit(_where)/select_n | solution.py:218
  23.2 1.9 %collective-permute-start.2 = (bf16[1536,384]{1,0:T(8,128)(2,1)}, bf16[1536,384]{1,0:T(8,128)(2,1)}, u32[]{:S(2)}, u32[]{:S(2)}) collective-permute-start(bf16[1536,384]{1,0:T(8,128)(2,1)} %get-tuple-element.41), channel_id=1, source_target_pairs={{0,32},{32,0},{64,96},{96,64},{128,160},{160,128},{192,224},{224,1... | collective-permute-start | bytes 3538952 | tf_op jit(solution)/shard_map/ppermute | solution.py:219
  25.1 2.6 %all-to-all-done.4 = bf16[32,2,8,384]{3,2,1,0:T(8,128)(2,1)S(1)} async-done(((bf16[32,2,8,384]{3,2,1,0:T(8,128)(2,1)}), bf16[32,2,8,384]{3,2,1,0:T(8,128)(2,1)S(1)}, u32[]{:S(2)}, u32[]{:S(2)}) %all-to-all-start.4) | async-done | bytes 393248 | tf_op jit(solution)/shard_map/all_to_all | solution.py:207
  27.7 5.7 %collective-permute-start = (bf16[32,2,8,384]{3,2,1,0:T(8,128)(2,1)S(1)}, bf16[32,2,8,384]{3,2,1,0:T(8,128)(2,1)S(1)}, u32[]{:S(2)}, u32[]{:S(2)}) collective-permute-start(bf16[32,2,8,384]{3,2,1,0:T(8,128)(2,1)S(1)} %all-to-all-done.4), channel_id=1, source_target_pairs={{0,32},{32,0},{64,96},{96,64},{128,160},{160,128},{192,224},{224,1... | collective-permute-start | bytes 1179656 | tf_op jit(solution)/shard_map/ppermute | solution.py:208
  33.5 1.0 own_sums.1
  34.5 0.3 collective-permute-done
  34.8 0.0 collective-permute-done.1.w_rows
  34.8 0.0 collective-permute-done.2.w_cots
  34.8 2.6 %sums.1 = bf16[256,3072]{1,0:T(8,128)(2,1)S(1)} custom-call(s32[1]{0:T(128)} %bitcast.5.role, f32[256,1536]{1,0:T(8,128)S(1)} %get-tuple-element.19.front_a, f32[256,1536]{1,0:T(8,128)S(1)} %get-tuple-element.20.back_a, bf16[256,384]{1,0:T(8,128)(2,1)S(1)} %get-tuple-element.44.rows, bf16[256,384]{1,0:T(8,128)(2,1)S(1)} %get-tuple-element.43.cots, ...), custom_call_target="tpu_custom_call" | custom-call | flops 603979776 | tf_op jit(solution)/shard_map/sums/pallas_call | solution.py:237
  37.5 54.3 %conditional.1 = (bf16[256,1536]{1,0:T(8,128)(2,1)S(1)}) conditional(s32[]{:T(128)} %convert_element_type.15, bf16[256,3072]{1,0:T(8,128)(2,1)S(1)} %sums.1, bf16[256,3072]{1,0:T(8,128)(2,1)S(1)} %sums.1), branch_computations={%region_0.2_spmd, %region_2.11_spmd} | conditional | flops 2826240 | bytes 8257544 | solution.py:280
  37.5 36.4 %all_to_all.21 = bf16[8,32,3072]{2,1,0:T(8,128)(2,1)S(1)} all-to-all(bf16[8,32,3072]{2,1,0:T(8,128)(2,1)S(1)} %bitcast.28), channel_id=1, replica_groups={{0,64,128,192,256,320,384,448},{32,96,160,224,288,352,416,480},{1,65,12..., dimensions={0} | all-to-all | bytes 3145728 | tf_op jit(solution)/shard_map/cond/branch_0_fun/all_to_all | solution.py:249
  73.9 0.2 convert_reduce_fusion
  74.1 0.2 add_convert_fusion.1
  74.3 0.1 broadcast_in_dim.18
  74.4 17.4 %all_to_all.22 = bf16[8,32,1536]{2,1,0:T(8,128)(2,1)S(1)} all-to-all(bf16[8,32,1536]{2,1,0:T(8,128)(2,1)S(1)} %broadcast_in_dim.18), channel_id=1, replica_groups={{0,64,128,192,256,320,384,448},{32,96,160,224,288,352,416,480},{1,65,12..., dimensions={0} | all-to-all | bytes 1572864 | tf_op jit(solution)/shard_map/cond/branch_0_fun/all_to_all | solution.py:253
  91.8 1.9 %collective-permute-start.3 = (bf16[256,1536]{1,0:T(8,128)(2,1)S(1)}, bf16[256,1536]{1,0:T(8,128)(2,1)S(1)}, u32[]{:S(2)}, u32[]{:S(2)}) collective-permute-start(bf16[256,1536]{1,0:T(8,128)(2,1)S(1)} %get-tuple-element.47.lows), channel_id=1, source_target_pairs={{0,32},{32,0},{64,96},{96,64},{128,160},{160,128},{192,224},{224,1... | collective-permute-start | bytes 2359304 | tf_op jit(solution)/shard_map/ppermute | solution.py:281
  93.7 1.4 %own_products.1 = (bf16[3,384,128]{2,1,0:T(8,128)(2,1)}, bf16[128,384]{1,0:T(8,128)(2,1)}, bf16[384,768]{1,0:T(8,128)(2,1)}, bf16[768,384]{1,0:T(8,128)(2,1)}) custom-call(s32[1]{0:T(128)} %bitcast.5.role, bf16[256,1536]{1,0:T(8,128)(2,1)S(1)} %get-tuple-element.47.lows, bf16[256,384]{1,0:T(8,128)(2,1)S(1)} %get-tuple-element.46.rows, ...), custom_call_target="tpu_custom_call" | custom-call | flops 603979776 | bytes 2359296 | tf_op jit(solution)/shard_map/own_products/pallas_call | solution.py:286
  95.1 0.8 collective-permute-done.3.lows
  95.9 1.1 %other_products.1 = (bf16[3,384,128]{2,1,0:T(8,128)(2,1)}, bf16[128,384]{1,0:T(8,128)(2,1)}, bf16[384,768]{1,0:T(8,128)(2,1)}, bf16[768,384]{1,0:T(8,128)(2,1)}) custom-call(s32[1]{0:T(128)} %bitcast.4.role, bf16[256,1536]{1,0:T(8,128)(2,1)S(1)} %collective-permute-done.3.lows, ...), custom_call_target="tpu_custom_call", output_to_operand_aliasing={{0}: (4, {}), {1}: (5, {}), {2}: (6, {}), {3}: (7, {})} | custom-call | flops 603979776 | bytes 2359296 | tf_op jit(solution)/shard_map/other_products/pallas_call | solution.py:286
  (12 shorter events, 0.3 us)
Async XLA Ops:
  0.6 15.4 %copy-start.4 = (bf16[384,3,128]{2,0,1:T(8,128)(2,1)S(1)}, bf16[384,3,128]{2,0,1:T(8,128)(2,1)}, u32[]{:S(2)}) copy-start(bf16[384,3,128]{2,0,1:T(8,128)(2,1)} %param.14) | copy-start | bytes 884740
  0.6 15.5 %copy-start.5 = (bf16[384,3,128]{2,0,1:T(8,128)(2,1)S(1)}, bf16[384,3,128]{2,0,1:T(8,128)(2,1)}, u32[]{:S(2)}) copy-start(bf16[384,3,128]{2,0,1:T(8,128)(2,1)} %param.18) | copy-start | bytes 884740
  0.7 15.6 %copy-start = (bf16[384,768]{1,0:T(8,128)(2,1)S(1)}, bf16[384,768]{1,0:T(8,128)(2,1)}, u32[]{:S(2)}) copy-start(bf16[384,768]{1,0:T(8,128)(2,1)} %param.16) | copy-start | bytes 1769476
  2.3 25.4 %all-to-all-start.4 = ((bf16[32,2,8,384]{3,2,1,0:T(8,128)(2,1)}), bf16[32,2,8,384]{3,2,1,0:T(8,128)(2,1)S(1)}, u32[]{:S(2)}, u32[]{:S(2)}) async-start(bf16[32,2,8,384]{3,2,1,0:T(8,128)(2,1)} %broadcast_select_fusion.2), calls=%async_computation.4 | async-start | bytes 786432 | tf_op jit(solution)/shard_map/all_to_all | solution.py:207
  16.1 1.1 %copy-start.1 = (bf16[384,768]{1,0:T(8,128)(2,1)S(1)}, bf16[384,768]{1,0:T(8,128)(2,1)}, u32[]{:S(2)}) copy-start(bf16[384,768]{1,0:T(8,128)(2,1)} %param.20) | copy-start | bytes 1769476
  17.2 4.4 %copy-start.2 = (bf16[768,384]{1,0:T(8,128)(2,1)S(1)}, bf16[768,384]{1,0:T(8,128)(2,1)}, u32[]{:S(2)}) copy-start(bf16[768,384]{1,0:T(8,128)(2,1)} %param.17) | copy-start | bytes 1769476
  18.6 3.1 %copy-start.3 = (bf16[768,384]{1,0:T(8,128)(2,1)S(1)}, bf16[768,384]{1,0:T(8,128)(2,1)}, u32[]{:S(2)}) copy-start(bf16[768,384]{1,0:T(8,128)(2,1)} %param.21) | copy-start | bytes 1769476
  18.6 3.2 %copy-start.6 = (bf16[128,384]{1,0:T(8,128)(2,1)S(1)}, bf16[128,384]{1,0:T(8,128)(2,1)}, u32[]{:S(2)}) copy-start(bf16[128,384]{1,0:T(8,128)(2,1)} %param.19) | copy-start | bytes 294916
  18.6 3.2 %copy-start.7 = (bf16[128,384]{1,0:T(8,128)(2,1)S(1)}, bf16[128,384]{1,0:T(8,128)(2,1)}, u32[]{:S(2)}) copy-start(bf16[128,384]{1,0:T(8,128)(2,1)} %param.15) | copy-start | bytes 294916
  18.6 16.2 %collective-permute-start.1 = (bf16[384,1536]{1,0:T(8,128)(2,1)}, bf16[384,1536]{1,0:T(8,128)(2,1)}, u32[]{:S(2)}, u32[]{:S(2)}) collective-permute-start(bf16[384,1536]{1,0:T(8,128)(2,1)} %get-tuple-element.39), channel_id=1, source_target_pairs={{0,32},{32,0},{64,96},{96,64},{128,160},{160,128},{192,224},{224,1... | collective-permute-start | bytes 3538952 | tf_op jit(solution)/shard_map/ppermute | solution.py:219
  23.2 11.6 %collective-permute-start.2 = (bf16[1536,384]{1,0:T(8,128)(2,1)}, bf16[1536,384]{1,0:T(8,128)(2,1)}, u32[]{:S(2)}, u32[]{:S(2)}) collective-permute-start(bf16[1536,384]{1,0:T(8,128)(2,1)} %get-tuple-element.41), channel_id=1, source_target_pairs={{0,32},{32,0},{64,96},{96,64},{128,160},{160,128},{192,224},{224,1... | collective-permute-start | bytes 3538952 | tf_op jit(solution)/shard_map/ppermute | solution.py:219
  27.7 7.1 %collective-permute-start = (bf16[32,2,8,384]{3,2,1,0:T(8,128)(2,1)S(1)}, bf16[32,2,8,384]{3,2,1,0:T(8,128)(2,1)S(1)}, u32[]{:S(2)}, u32[]{:S(2)}) collective-permute-start(bf16[32,2,8,384]{3,2,1,0:T(8,128)(2,1)S(1)} %all-to-all-done.4), channel_id=1, source_target_pairs={{0,32},{32,0},{64,96},{96,64},{128,160},{160,128},{192,224},{224,1... | collective-permute-start | bytes 1179656 | tf_op jit(solution)/shard_map/ppermute | solution.py:208
  91.8 4.2 %collective-permute-start.3 = (bf16[256,1536]{1,0:T(8,128)(2,1)S(1)}, bf16[256,1536]{1,0:T(8,128)(2,1)S(1)}, u32[]{:S(2)}, u32[]{:S(2)}) collective-permute-start(bf16[256,1536]{1,0:T(8,128)(2,1)S(1)} %get-tuple-element.47.lows), channel_id=1, source_target_pairs={{0,32},{32,0},{64,96},{96,64},{128,160},{160,128},{192,224},{224,1... | collective-permute-start | bytes 2359304 | tf_op jit(solution)/shard_map/ppermute | solution.py:281

commit v7 on v6

--- a/solution.py
+++ b/solution.py
@@ -111,11 +111,28 @@
     back[...] = dot(cots[...], w_cots[...], NT)
 
 
-def sums_kernel(role, front_a, back_a, rows, cots, w_rows, w_cots, out):
+def sums_kernel(role, front_a, back_a, rows, cots, far_rows, far_cots, out, w_rows, w_cots, sems):
+    columns = w_rows.shape[1]
+
+    def bring(pairs):
+        copies = [pltpu.make_async_copy(*pair, sems.at[at]) for at, pair in enumerate(pairs)]
+        for copy in copies:
+            copy.start()
+        return copies
+
     @pl.when(role[0] == 0)
     def _():
-        front = front_a[:, : 6 * HD] + dot(rows[...], w_rows[:, : 6 * HD], NN)
-        back = back_a[:, : 2 * HD] + dot(cots[...], w_cots[: 2 * HD, :], NT)
+        heads = slice(0, 6 * HD)
+        outs = slice(0, 2 * HD)
+        for copy in bring(
+            [
+                (far_rows.at[:, heads], w_rows.at[:, heads]),
+                (far_cots.at[outs, :], w_cots.at[outs, :]),
+            ]
+        ):
+            copy.wait()
+        front = front_a[:, heads] + dot(rows[...], w_rows[:, heads], NN)
+        back = back_a[:, outs] + dot(cots[...], w_cots[outs, :], NT)
         packed = 0.0
         for at in range(8):
             half, place = at // 4, at % 4
@@ -131,9 +148,16 @@
 
     @pl.when(role[0] == 1)
     def _():
-        columns = w_rows.shape[1]
+        halves_of = [slice(0, columns // 2), slice(columns // 2, columns)]
+        copies = bring(
+            [(far_cots.at[at, :], w_cots.at[at, :]) for at in halves_of] + [(far_rows, w_rows)]
+        )
+        for copy, at in zip(copies, halves_of):
+            copy.wait()
+            sums = back_a[:, at] + dot(cots[...], w_cots[at, :], NT)
+            out[:, columns + at.start : columns + at.stop] = sums.astype(BF16)
+        copies[2].wait()
         out[:, :columns] = (front_a[...] + dot(rows[...], w_rows[...], NN)).astype(BF16)
-        out[:, columns:] = (back_a[...] + dot(cots[...], w_cots[...], NT)).astype(BF16)
 
 
 def attention_kernel(whole, out):
@@ -237,8 +261,10 @@
     message = pl.pallas_call(
         sums_kernel,
         out_shape=jax.ShapeDtypeStruct((count, 4 * hidden), BF16),
-        in_specs=[SMEM] + [VMEM] * 6,
+        in_specs=[SMEM] + [VMEM] * 4 + [anywhere] * 2,
         out_specs=VMEM,
+        scratch_shapes=[pltpu.VMEM(a.shape, a.dtype) for a in taken]
+        + [pltpu.SemaphoreType.DMA((3,))],
         compiler_params=room,
         cost_estimate=sums_cost,
         name="sums",

time: 97.5 us -> 97.5 us (level)
  no operation moved by 1% of the time
where the time goes in v7:
time: 97.5 us; the launch traced here: 97 us
  blocking collectives  53.7 us (55%)
  starting transfers between devices  26.3 us (27%)
  Pallas kernels  6.17 us (6%)
  other arithmetic  4.85 us (5%)
  waiting for transfers between devices  3.7 us (4%)
  local copies, waits for them, and re-layouts  1.35 us (1%)
    all_to_all x1, blocking collectives, exchange(): lax.all_to_all(part, 'mx', 0, 0, tiled=True, axis_index_groups=ring)  36.4 us
    all_to_all x1, blocking collectives, spread(): lax.all_to_all(copies, 'mx', 0, 0, tiled=True, axis_index_groups=ring)  17.4 us
    all_to_all x1, starting transfers between devices, body(): gathered = lax.all_to_all(copies, 'my', 0, 0, tiled=True)  13.7 us
    ppermute x1, starting transfers between devices, body(): swapped = lax.ppermute(gathered, 'mx', swap)  5.73 us
    ppermute x2, starting transfers between devices, body(): taken = tuple((lax.ppermute(a, 'mx', swap) for a in lent))  4.89 us
    pallas_call x1, Pallas kernels, body(): pl.pallas_call(sums_kernel, out_shape=jax.ShapeDtypeStruct((count, 4 * hi...  2.64 us
    all_to_all x1, waiting for transfers between devices, body(): gathered = lax.all_to_all(copies, 'my', 0, 0, tiled=True)  2.57 us
    pallas_call x2, Pallas kernels, products(): pl.pallas_call(products_kernel, out_shape=tuple((jax.ShapeDtypeStruct(sha...  2.57 us
  transfers between devices with their start and end apart: 5, of which 3 were waited for; matrix products, arithmetic and copies ran while one was open for 3% of the time, Pallas kernels for 2%

profile of v7, /device:TPU:1, one launch (start us, length us, event | category | flops | bytes accessed | tf_op | source)
XLA Modules:
  0.0 97.0 jit_solution(3145159895978534732)
XLA Ops:
  0.6 0.0 copy-start.4
  0.6 0.0 copy-start.5
  0.7 0.0 copy-start
  0.7 1.6 %broadcast_select_fusion.2 = bf16[32,2,8,384]{3,2,1,0:T(8,128)(2,1)} fusion(pred[2]{0:T(512)(128)(4,1)S(1)} %iota_compare_fusion.1, bf16[8,384]{1,0:T(8,128)(2,1)} %param.13, bf16[8,384]{1,0:T(8,128)(2,1)} %param.12), kind=kLoop, calls=%fused_computation.134 | loop fusion | flops 196608 | bytes 405506 | tf_op jit(solution)/shard_map/jit(_where)/select_n | solution.py:226
  2.3 13.7 %all-to-all-start.4 = ((bf16[32,2,8,384]{3,2,1,0:T(8,128)(2,1)}), bf16[32,2,8,384]{3,2,1,0:T(8,128)(2,1)S(1)}, u32[]{:S(2)}, u32[]{:S(2)}) async-start(bf16[32,2,8,384]{3,2,1,0:T(8,128)(2,1)} %broadcast_select_fusion.2), calls=%async_computation.4 | async-start | bytes 786432 | tf_op jit(solution)/shard_map/all_to_all | solution.py:231
  16.1 0.0 copy-done.4
  16.1 0.0 copy-start.1
  16.2 0.0 copy-done.5
  16.3 0.0 copy-done
  16.3 0.8 copy-done.1
  17.2 0.0 copy-start.2
  17.2 1.4 %pad_select_fusion = (bf16[384,1536]{1,0:T(8,128)(2,1)}, bf16[384,1536]{1,0:T(8,128)(2,1)S(1)}) fusion(bf16[384,1536]{1,0:T(8,128)(2,1)S(1)} %constant_dynamic-update-slice_fusion.12, bf16[384,768]{1,0:T(8,128)(2,1)S(1)} %bitcast_dynamic-update-slice_fusion, pred[]{:T(512)S(6)} %eq.34), kind=kLoop, calls=%fused_computation.129 | loop fusion | flops 1179648 | bytes 4128769 | tf_op jit(solution)/shard_map/jit(_where)/select_n | solution.py:242
  18.6 0.0 copy-start.3
  18.6 0.0 copy-start.6
  18.6 0.0 copy-start.7
  18.6 3.0 %collective-permute-start.1 = (bf16[384,1536]{1,0:T(8,128)(2,1)}, bf16[384,1536]{1,0:T(8,128)(2,1)}, u32[]{:S(2)}, u32[]{:S(2)}) collective-permute-start(bf16[384,1536]{1,0:T(8,128)(2,1)} %get-tuple-element.39), channel_id=1, source_target_pairs={{0,32},{32,0},{64,96},{96,64},{128,160},{160,128},{192,224},{224,1... | collective-permute-start | bytes 3538952 | tf_op jit(solution)/shard_map/ppermute | solution.py:243
  21.6 0.0 copy-done.2
  21.6 0.1 constant_dynamic-update-slice_fusion.15
  21.7 0.0 copy-done.3
  21.7 0.1 constant_dynamic-update-slice_fusion.14
  21.8 0.0 copy-done.6
  21.8 0.0 copy-done.7
  21.8 1.4 %broadcast_select_fusion = (bf16[1536,384]{1,0:T(8,128)(2,1)}, bf16[1536,384]{1,0:T(8,128)(2,1)S(1)}) fusion(bf16[1536,384]{1,0:T(8,128)(2,1)S(1)} %constant_dynamic-update-slice_fusion.14, pred[]{:T(512)S(6)} %eq.34, bf16[128,384]{1,0:T(8,128)(2,1)S(1)} %copy-done.6, bf16[128,384]{1,0:T(8,128)(2,1)S(1)} %copy-done.7), kind=kLoop, calls=%fused_computation.132 | loop fusion | flops 5308416 | bytes 3735553 | tf_op jit(solution)/shard_map/jit(_where)/select_n | solution.py:242
  23.2 1.9 %collective-permute-start.2 = (bf16[1536,384]{1,0:T(8,128)(2,1)}, bf16[1536,384]{1,0:T(8,128)(2,1)}, u32[]{:S(2)}, u32[]{:S(2)}) collective-permute-start(bf16[1536,384]{1,0:T(8,128)(2,1)} %get-tuple-element.41), channel_id=1, source_target_pairs={{0,32},{32,0},{64,96},{96,64},{128,160},{160,128},{192,224},{224,1... | collective-permute-start | bytes 3538952 | tf_op jit(solution)/shard_map/ppermute | solution.py:243
  25.1 2.6 %all-to-all-done.4 = bf16[32,2,8,384]{3,2,1,0:T(8,128)(2,1)S(1)} async-done(((bf16[32,2,8,384]{3,2,1,0:T(8,128)(2,1)}), bf16[32,2,8,384]{3,2,1,0:T(8,128)(2,1)S(1)}, u32[]{:S(2)}, u32[]{:S(2)}) %all-to-all-start.4) | async-done | bytes 393248 | tf_op jit(solution)/shard_map/all_to_all | solution.py:231
  27.7 5.7 %collective-permute-start = (bf16[32,2,8,384]{3,2,1,0:T(8,128)(2,1)S(1)}, bf16[32,2,8,384]{3,2,1,0:T(8,128)(2,1)S(1)}, u32[]{:S(2)}, u32[]{:S(2)}) collective-permute-start(bf16[32,2,8,384]{3,2,1,0:T(8,128)(2,1)S(1)} %all-to-all-done.4), channel_id=1, source_target_pairs={{0,32},{32,0},{64,96},{96,64},{128,160},{160,128},{192,224},{224,1... | collective-permute-start | bytes 1179656 | tf_op jit(solution)/shard_map/ppermute | solution.py:232
  33.5 1.0 own_sums.1
  34.5 0.3 collective-permute-done
  34.8 0.0 collective-permute-done.1.far_rows
  34.8 0.0 collective-permute-done.2.far_cots
  34.8 2.6 %sums.1 = bf16[256,3072]{1,0:T(8,128)(2,1)S(1)} custom-call(s32[1]{0:T(128)} %bitcast.5.role, f32[256,1536]{1,0:T(8,128)S(1)} %get-tuple-element.19.front_a, f32[256,1536]{1,0:T(8,128)S(1)} %get-tuple-element.20.back_a, bf16[256,384]{1,0:T(8,128)(2,1)S(1)} %get-tuple-element.44.rows, bf16[256,384]{1,0:T(8,128)(2,1)S(1)} %get-tuple-element.43.cots, ...), custom_call_target="tpu_custom_call" | custom-call | flops 603979776 | tf_op jit(solution)/shard_map/sums/pallas_call | solution.py:261
  37.5 54.2 %conditional.1 = (bf16[256,1536]{1,0:T(8,128)(2,1)S(1)}) conditional(s32[]{:T(128)} %convert_element_type.15, bf16[256,3072]{1,0:T(8,128)(2,1)S(1)} %sums.1, bf16[256,3072]{1,0:T(8,128)(2,1)S(1)} %sums.1), branch_computations={%region_0.2_spmd, %region_2.11_spmd} | conditional | flops 2826240 | bytes 8257544 | solution.py:306
  37.5 36.4 %all_to_all.21 = bf16[8,32,3072]{2,1,0:T(8,128)(2,1)S(1)} all-to-all(bf16[8,32,3072]{2,1,0:T(8,128)(2,1)S(1)} %bitcast.28), channel_id=1, replica_groups={{0,64,128,192,256,320,384,448},{32,96,160,224,288,352,416,480},{1,65,12..., dimensions={0} | all-to-all | bytes 3145728 | tf_op jit(solution)/shard_map/cond/branch_0_fun/all_to_all | solution.py:275
  73.9 0.2 convert_reduce_fusion
  74.1 0.2 add_convert_fusion.1
  74.3 0.1 broadcast_in_dim.18
  74.3 17.4 %all_to_all.22 = bf16[8,32,1536]{2,1,0:T(8,128)(2,1)S(1)} all-to-all(bf16[8,32,1536]{2,1,0:T(8,128)(2,1)S(1)} %broadcast_in_dim.18), channel_id=1, replica_groups={{0,64,128,192,256,320,384,448},{32,96,160,224,288,352,416,480},{1,65,12..., dimensions={0} | all-to-all | bytes 1572864 | tf_op jit(solution)/shard_map/cond/branch_0_fun/all_to_all | solution.py:279
  91.7 1.9 %collective-permute-start.3 = (bf16[256,1536]{1,0:T(8,128)(2,1)S(1)}, bf16[256,1536]{1,0:T(8,128)(2,1)S(1)}, u32[]{:S(2)}, u32[]{:S(2)}) collective-permute-start(bf16[256,1536]{1,0:T(8,128)(2,1)S(1)} %get-tuple-element.47.lows), channel_id=1, source_target_pairs={{0,32},{32,0},{64,96},{96,64},{128,160},{160,128},{192,224},{224,1... | collective-permute-start | bytes 2359304 | tf_op jit(solution)/shard_map/ppermute | solution.py:307
  93.6 1.4 %own_products.1 = (bf16[3,384,128]{2,1,0:T(8,128)(2,1)}, bf16[128,384]{1,0:T(8,128)(2,1)}, bf16[384,768]{1,0:T(8,128)(2,1)}, bf16[768,384]{1,0:T(8,128)(2,1)}) custom-call(s32[1]{0:T(128)} %bitcast.5.role, bf16[256,1536]{1,0:T(8,128)(2,1)S(1)} %get-tuple-element.47.lows, bf16[256,384]{1,0:T(8,128)(2,1)S(1)} %get-tuple-element.46.rows, ...), custom_call_target="tpu_custom_call" | custom-call | flops 603979776 | bytes 2359296 | tf_op jit(solution)/shard_map/own_products/pallas_call | solution.py:312
  95.0 0.8 collective-permute-done.3.lows
  95.9 1.1 %other_products.1 = (bf16[3,384,128]{2,1,0:T(8,128)(2,1)}, bf16[128,384]{1,0:T(8,128)(2,1)}, bf16[384,768]{1,0:T(8,128)(2,1)}, bf16[768,384]{1,0:T(8,128)(2,1)}) custom-call(s32[1]{0:T(128)} %bitcast.4.role, bf16[256,1536]{1,0:T(8,128)(2,1)S(1)} %collective-permute-done.3.lows, ...), custom_call_target="tpu_custom_call", output_to_operand_aliasing={{0}: (4, {}), {1}: (5, {}), {2}: (6, {}), {3}: (7, {})} | custom-call | flops 603979776 | bytes 2359296 | tf_op jit(solution)/shard_map/other_products/pallas_call | solution.py:312
  (12 shorter events, 0.3 us)
Async XLA Ops:
  0.6 15.4 %copy-start.4 = (bf16[384,3,128]{2,0,1:T(8,128)(2,1)S(1)}, bf16[384,3,128]{2,0,1:T(8,128)(2,1)}, u32[]{:S(2)}) copy-start(bf16[384,3,128]{2,0,1:T(8,128)(2,1)} %param.14) | copy-start | bytes 884740
  0.6 15.5 %copy-start.5 = (bf16[384,3,128]{2,0,1:T(8,128)(2,1)S(1)}, bf16[384,3,128]{2,0,1:T(8,128)(2,1)}, u32[]{:S(2)}) copy-start(bf16[384,3,128]{2,0,1:T(8,128)(2,1)} %param.18) | copy-start | bytes 884740
  0.7 15.6 %copy-start = (bf16[384,768]{1,0:T(8,128)(2,1)S(1)}, bf16[384,768]{1,0:T(8,128)(2,1)}, u32[]{:S(2)}) copy-start(bf16[384,768]{1,0:T(8,128)(2,1)} %param.16) | copy-start | bytes 1769476
  2.3 25.4 %all-to-all-start.4 = ((bf16[32,2,8,384]{3,2,1,0:T(8,128)(2,1)}), bf16[32,2,8,384]{3,2,1,0:T(8,128)(2,1)S(1)}, u32[]{:S(2)}, u32[]{:S(2)}) async-start(bf16[32,2,8,384]{3,2,1,0:T(8,128)(2,1)} %broadcast_select_fusion.2), calls=%async_computation.4 | async-start | bytes 786432 | tf_op jit(solution)/shard_map/all_to_all | solution.py:231
  16.1 1.1 %copy-start.1 = (bf16[384,768]{1,0:T(8,128)(2,1)S(1)}, bf16[384,768]{1,0:T(8,128)(2,1)}, u32[]{:S(2)}) copy-start(bf16[384,768]{1,0:T(8,128)(2,1)} %param.20) | copy-start | bytes 1769476
  17.2 4.4 %copy-start.2 = (bf16[768,384]{1,0:T(8,128)(2,1)S(1)}, bf16[768,384]{1,0:T(8,128)(2,1)}, u32[]{:S(2)}) copy-start(bf16[768,384]{1,0:T(8,128)(2,1)} %param.17) | copy-start | bytes 1769476
  18.6 3.1 %copy-start.3 = (bf16[768,384]{1,0:T(8,128)(2,1)S(1)}, bf16[768,384]{1,0:T(8,128)(2,1)}, u32[]{:S(2)}) copy-start(bf16[768,384]{1,0:T(8,128)(2,1)} %param.21) | copy-start | bytes 1769476
  18.6 3.2 %copy-start.6 = (bf16[128,384]{1,0:T(8,128)(2,1)S(1)}, bf16[128,384]{1,0:T(8,128)(2,1)}, u32[]{:S(2)}) copy-start(bf16[128,384]{1,0:T(8,128)(2,1)} %param.19) | copy-start | bytes 294916
  18.6 3.2 %copy-start.7 = (bf16[128,384]{1,0:T(8,128)(2,1)S(1)}, bf16[128,384]{1,0:T(8,128)(2,1)}, u32[]{:S(2)}) copy-start(bf16[128,384]{1,0:T(8,128)(2,1)} %param.15) | copy-start | bytes 294916
  18.6 16.2 %collective-permute-start.1 = (bf16[384,1536]{1,0:T(8,128)(2,1)}, bf16[384,1536]{1,0:T(8,128)(2,1)}, u32[]{:S(2)}, u32[]{:S(2)}) collective-permute-start(bf16[384,1536]{1,0:T(8,128)(2,1)} %get-tuple-element.39), channel_id=1, source_target_pairs={{0,32},{32,0},{64,96},{96,64},{128,160},{160,128},{192,224},{224,1... | collective-permute-start | bytes 3538952 | tf_op jit(solution)/shard_map/ppermute | solution.py:243
  23.2 11.6 %collective-permute-start.2 = (bf16[1536,384]{1,0:T(8,128)(2,1)}, bf16[1536,384]{1,0:T(8,128)(2,1)}, u32[]{:S(2)}, u32[]{:S(2)}) collective-permute-start(bf16[1536,384]{1,0:T(8,128)(2,1)} %get-tuple-element.41), channel_id=1, source_target_pairs={{0,32},{32,0},{64,96},{96,64},{128,160},{160,128},{192,224},{224,1... | collective-permute-start | bytes 3538952 | tf_op jit(solution)/shard_map/ppermute | solution.py:243
  27.7 7.1 %collective-permute-start = (bf16[32,2,8,384]{3,2,1,0:T(8,128)(2,1)S(1)}, bf16[32,2,8,384]{3,2,1,0:T(8,128)(2,1)S(1)}, u32[]{:S(2)}, u32[]{:S(2)}) collective-permute-start(bf16[32,2,8,384]{3,2,1,0:T(8,128)(2,1)S(1)} %all-to-all-done.4), channel_id=1, source_target_pairs={{0,32},{32,0},{64,96},{96,64},{128,160},{160,128},{192,224},{224,1... | collective-permute-start | bytes 1179656 | tf_op jit(solution)/shard_map/ppermute | solution.py:232
  91.7 4.2 %collective-permute-start.3 = (bf16[256,1536]{1,0:T(8,128)(2,1)S(1)}, bf16[256,1536]{1,0:T(8,128)(2,1)S(1)}, u32[]{:S(2)}, u32[]{:S(2)}) collective-permute-start(bf16[256,1536]{1,0:T(8,128)(2,1)S(1)} %get-tuple-element.47.lows), channel_id=1, source_target_pairs={{0,32},{32,0},{64,96},{96,64},{128,160},{160,128},{192,224},{224,1... | collective-permute-start | bytes 2359304 | tf_op jit(solution)/shard_map/ppermute | solution.py:307
